TPU v7x, 32 devices: a whole 2x2x4 slice. The times are simulated.
32 devices in a mesh: dp: 8 (over y, x, core), tensor: 4 (over z).
Axes of the slice: x: 2, y: 2, z: 4, core: 2. Of those that a mesh axis runs over, the one named last changes fastest.
Arguments:
- tokens: bfloat16 [2048, 8, 1024], P('tensor', 'dp'), may hold values from -6 to 6
- qkv_weight: bfloat16 [1024, 3, 1024], P(None, None, 'tensor'), may hold values from -0.1875 to 0.1875
- output_projection_weight: bfloat16 [1024, 1024], P('tensor'), may hold values from -4 to 4
- gate_up_weight: bfloat16 [1024, 2, 4096], P(None, None, 'tensor'), may hold values from -0.1875 to 0.1875
- down_projection_weight: bfloat16 [4096, 1024], P('tensor'), may hold values from -0.09375 to 0.09375
- attention_gain: float32 [1024], replicated, may hold values from 0.1 to 1.9
- feedforward_gain: float32 [1024], replicated, may hold values from 0.1 to 1.9
- window_lengths: int32 [8], P('dp'), may hold values from 512 to 2048, as said below
- key_mask: int32 [2048, 8], P(None, 'dp'), may hold values from 0 to 1, as said below
- cotangent: bfloat16 [2048, 8, 1024], P('tensor', 'dp'), may hold values from -12 to 12
Outputs:
- output: bfloat16 [2048, 8, 1024], P('tensor', 'dp')
- tokens_grad: bfloat16 [2048, 8, 1024], P('tensor', 'dp')
- qkv_grad: float32 [1024, 3, 1024], P(None, None, 'tensor')
- out_grad: float32 [1024, 1024], P('tensor')
- gate_up_grad: float32 [1024, 2, 4096], P(None, None, 'tensor')
- down_projection_gradient: float32 [4096, 1024], P('tensor')
- attention_gain_grad: float32 [1024], replicated
- feedforward_gain_grad: float32 [1024], replicated
Inputs may be any that keep to these rules, and one draw needn't show every extreme that they name: `window_lengths`: among the 1 windows of each index of dp, one drawn from the seed has length 2048. `key_mask`: slot 0 of every window is 1.
All inputs are finite; a program needn't handle non-finite values.
Results may differ from a plain program's by a relative error of at most 0.02.
Values may be sent and summed in bfloat16 or wider, within the bound.
No kernel may reach another device: no remote copies, remote signals or barrier semaphores. Data moves between devices by JAX's collectives and lax.ppermute only.
A program may use at most 384 MiB of HBM per device.

v0:
```python
import jax
import jax.numpy as jnp
from jax import lax
from jax.sharding import PartitionSpec as P

HEAD_DIM = 64
LEN = 2048


EPSILON = 1e-05
MASKED = -1000000000.0
ROPE_BASE = 10000.0


def rope_tables(length, head_size):
    midpoint = head_size // 2
    frequencies = ROPE_BASE ** (-(jnp.arange(midpoint, dtype=jnp.float32) * 2.0 / head_size))
    angles = jnp.arange(length, dtype=jnp.float32)[:, None] * frequencies[None, :]
    angles = jnp.concatenate([angles, angles], axis=1)
    return (jnp.cos(angles)[:, None, None, :], jnp.sin(angles)[:, None, None, :])


def rotate_half(values):
    midpoint = values.shape[-1] // 2
    return jnp.concatenate([-values[..., midpoint:], values[..., :midpoint]], axis=-1)


def rotate_back(values):
    midpoint = values.shape[-1] // 2
    return jnp.concatenate([values[..., midpoint:], -values[..., :midpoint]], axis=-1)


def norm_forward(rows, gains):
    average = jnp.mean(rows, axis=-1, keepdims=True)
    centered = rows - average
    variance = jnp.mean(centered * centered, axis=-1, keepdims=True)
    inverse = lax.rsqrt(variance + EPSILON)
    scaled = centered * inverse
    return (scaled * gains, scaled, inverse)


def norm_backward(upstream, scaled, inverse, gains):
    through = upstream * gains
    first_mean = jnp.mean(through, axis=-1, keepdims=True)
    second_mean = jnp.mean(through * scaled, axis=-1, keepdims=True)
    gradient = inverse * (through - first_mean - scaled * second_mean)
    return (gradient, jnp.sum(upstream * scaled, axis=(0, 1)))


def project_heads(gathered, qkv_weight, cosines, sines):
    projected = jnp.einsum(
        "lsd,dcf->lscf", gathered, qkv_weight, preferred_element_type=jnp.float32
    )
    head_shape = (projected.shape[0], projected.shape[1], -1, HEAD_DIM)
    queries = projected[:, :, 0].reshape(head_shape)
    keys_heads = projected[:, :, 1].reshape(head_shape)
    values_heads = projected[:, :, 2].reshape(head_shape)
    queries = (queries * cosines + rotate_half(queries) * sines).astype(jnp.bfloat16)
    keys_heads = (keys_heads * cosines + rotate_half(keys_heads) * sines).astype(jnp.bfloat16)
    return (queries, keys_heads, values_heads.astype(jnp.bfloat16))


def score_block(query_block, keys_heads, key_valid):
    scores = jnp.einsum(
        "qshe,kshe->shqk", query_block, keys_heads, preferred_element_type=jnp.float32
    ) * HEAD_DIM ** (-0.5)
    return jnp.where(key_valid, scores, MASKED)


def attend(queries, keys_heads, values_heads, key_valid, block_rows):
    outputs = []
    totals = []
    for start in range(0, queries.shape[0], block_rows):
        scores = score_block(queries[start : start + block_rows], keys_heads, key_valid)
        row_max = jnp.max(scores, axis=-1, keepdims=True)
        exp_rows = jnp.exp(scores - row_max)
        row_sum = jnp.sum(exp_rows, axis=-1, keepdims=True)
        prob_low = (exp_rows / row_sum).astype(jnp.bfloat16)
        outputs.append(
            jnp.einsum(
                "shqk,kshe->qshe", prob_low, values_heads, preferred_element_type=jnp.float32
            ).astype(jnp.bfloat16)
        )
        totals.append(row_max + jnp.log(row_sum))
    return (jnp.concatenate(outputs, axis=0), jnp.concatenate(totals, axis=2))


def attend_back(queries, keys_heads, values_heads, key_valid, totals, heads_grad, block_rows):
    scale = HEAD_DIM ** (-0.5)
    heads_parts = []
    query_parts = []
    key_grad = jnp.zeros(keys_heads.shape, jnp.float32)
    value_grad = jnp.zeros(values_heads.shape, jnp.float32)
    for start in range(0, queries.shape[0], block_rows):
        stop = start + block_rows
        query_block = queries[start:stop]
        grad_block = heads_grad[start:stop]
        scores = score_block(query_block, keys_heads, key_valid)
        prob_rows = jnp.exp(scores - totals[:, :, start:stop])
        prob_low = prob_rows.astype(jnp.bfloat16)
        heads_parts.append(
            jnp.einsum(
                "shqk,kshe->qshe", prob_low, values_heads, preferred_element_type=jnp.float32
            ).astype(jnp.bfloat16)
        )
        prob_grad = jnp.einsum(
            "qshe,kshe->shqk", grad_block, values_heads, preferred_element_type=jnp.float32
        )
        centre = jnp.sum(prob_rows * prob_grad, axis=-1, keepdims=True)
        score_grad = (prob_rows * (prob_grad - centre)).astype(jnp.bfloat16)
        query_parts.append(
            jnp.einsum(
                "shqk,kshe->qshe", score_grad, keys_heads, preferred_element_type=jnp.float32
            )
            * scale
        )
        key_grad = (
            key_grad
            + jnp.einsum(
                "shqk,qshe->kshe", score_grad, query_block, preferred_element_type=jnp.float32
            )
            * scale
        )
        value_grad = value_grad + jnp.einsum(
            "shqk,qshe->kshe", prob_low, grad_block, preferred_element_type=jnp.float32
        )
    return (
        jnp.concatenate(heads_parts, axis=0),
        jnp.concatenate(query_parts, axis=0),
        key_grad,
        value_grad,
    )


def swiglu(gathered, gate_up_weight):
    gate_up = jnp.einsum(
        "lsd,dcf->lscf", gathered, gate_up_weight, preferred_element_type=jnp.float32
    )
    gate_part = gate_up[:, :, 0]
    up_part = gate_up[:, :, 1]
    sigmoid_gate = jax.nn.sigmoid(gate_part)
    activated = gate_part * sigmoid_gate
    return ((activated * up_part).astype(jnp.bfloat16), gate_part, up_part, sigmoid_gate, activated)


def on_device(
    tokens,
    qkv_weight,
    output_projection_weight,
    gate_up_weight,
    down_projection_weight,
    attention_gain,
    feedforward_gain,
    window_lengths,
    key_mask,
    cotangent,
):
    windows = tokens.shape[1]
    block_rows = min(512, LEN)
    cosines, sines = rope_tables(LEN, HEAD_DIM)
    positions = jnp.arange(LEN, dtype=jnp.int32)
    key_valid = ((positions[:, None] < window_lengths[None, :]) & (key_mask == 1)).T[
        :, None, None, :
    ]
    residual = tokens.astype(jnp.float32)
    normed_one, scaled_one, inverse_one = norm_forward(residual, attention_gain)
    normed_attn = normed_one.astype(jnp.bfloat16)
    gathered_attn = lax.all_gather(normed_attn, "tensor", axis=0, tiled=True)
    queries, keys_heads, values_heads = project_heads(gathered_attn, qkv_weight, cosines, sines)
    heads_out, totals = attend(queries, keys_heads, values_heads, key_valid, block_rows)
    heads_flat = heads_out.reshape(LEN, windows, -1)
    shard_portion = heads_flat
    attn_branch = lax.psum_scatter(
        jnp.einsum(
            "mtq,qj->mtj",
            shard_portion,
            output_projection_weight,
            preferred_element_type=jnp.float32,
        ).astype(jnp.bfloat16),
        "tensor",
        scatter_dimension=0,
        tiled=True,
    ).astype(jnp.float32)
    middle = residual + attn_branch
    normed_two, scaled_two, inverse_two = norm_forward(middle, feedforward_gain)
    normed_ffn = normed_two.astype(jnp.bfloat16)
    gathered_ffn = lax.all_gather(normed_ffn, "tensor", axis=0, tiled=True)
    hidden_state = swiglu(gathered_ffn, gate_up_weight)[0]
    shard_portion = hidden_state
    output = (
        middle
        + lax.psum_scatter(
            jnp.einsum(
                "mtq,qj->mtj",
                shard_portion,
                down_projection_weight,
                preferred_element_type=jnp.float32,
            ).astype(jnp.bfloat16),
            "tensor",
            scatter_dimension=0,
            tiled=True,
        ).astype(jnp.float32)
    ).astype(jnp.bfloat16)
    gathered_ffn, collected_gradient = (
        lax.all_gather(normed_ffn, "tensor", axis=0, tiled=True),
        lax.all_gather(cotangent, "tensor", axis=0, tiled=True),
    )
    hidden_state, gate_part, up_part, sigmoid_gate, activated = swiglu(gathered_ffn, gate_up_weight)
    down_projection_gradient = jnp.einsum(
        "poh,pov->hv", hidden_state, collected_gradient, preferred_element_type=jnp.float32
    )
    hidden_grad = jnp.einsum(
        "gvi,ki->gvk",
        collected_gradient,
        down_projection_weight,
        preferred_element_type=jnp.float32,
    )
    gate_grad = hidden_grad * up_part * sigmoid_gate * (1.0 + gate_part * (1.0 - sigmoid_gate))
    gate_up_low = jnp.stack([gate_grad, hidden_grad * activated], axis=2).astype(jnp.bfloat16)
    gate_up_grad = jnp.einsum(
        "lsd,lscf->dcf", gathered_ffn, gate_up_low, preferred_element_type=jnp.float32
    )
    shard_portion = gate_up_low
    normed_two_grad = lax.psum_scatter(
        jnp.einsum(
            "lscf,dcf->lsd", shard_portion, gate_up_weight, preferred_element_type=jnp.float32
        ).astype(jnp.bfloat16),
        "tensor",
        scatter_dimension=0,
        tiled=True,
    ).astype(jnp.float32)
    through_two, feedforward_part = norm_backward(
        normed_two_grad, scaled_two, inverse_two, feedforward_gain
    )
    middle_grad = cotangent.astype(jnp.float32) + through_two
    middle_low = middle_grad.astype(jnp.bfloat16)
    gathered_attn, collected_middle = (
        lax.all_gather(normed_attn, "tensor", axis=0, tiled=True),
        lax.all_gather(middle_low, "tensor", axis=0, tiled=True),
    )
    queries, keys_heads, values_heads = project_heads(gathered_attn, qkv_weight, cosines, sines)
    heads_grad = jnp.einsum(
        "gvi,ki->gvk",
        collected_middle,
        output_projection_weight,
        preferred_element_type=jnp.float32,
    ).astype(jnp.bfloat16)
    heads_grad = heads_grad.reshape(LEN, windows, -1, HEAD_DIM)
    heads_again, query_grad, key_grad, value_grad = attend_back(
        queries, keys_heads, values_heads, key_valid, totals, heads_grad, block_rows
    )
    out_grad = jnp.einsum(
        "poh,pov->hv",
        heads_again.reshape(LEN, windows, -1),
        collected_middle,
        preferred_element_type=jnp.float32,
    )
    query_pre = query_grad * cosines + rotate_back(query_grad * sines)
    key_pre = key_grad * cosines + rotate_back(key_grad * sines)
    qkv_low = jnp.stack(
        [
            query_pre.reshape(LEN, windows, -1),
            key_pre.reshape(LEN, windows, -1),
            value_grad.reshape(LEN, windows, -1),
        ],
        axis=2,
    ).astype(jnp.bfloat16)
    qkv_grad = jnp.einsum(
        "lsd,lscf->dcf", gathered_attn, qkv_low, preferred_element_type=jnp.float32
    )
    shard_portion = qkv_low
    normed_one_grad = lax.psum_scatter(
        jnp.einsum(
            "lscf,dcf->lsd", shard_portion, qkv_weight, preferred_element_type=jnp.float32
        ).astype(jnp.bfloat16),
        "tensor",
        scatter_dimension=0,
        tiled=True,
    ).astype(jnp.float32)
    through_one, attention_part = norm_backward(
        normed_one_grad, scaled_one, inverse_one, attention_gain
    )
    tokens_grad = (middle_grad + through_one).astype(jnp.bfloat16)
    qkv_grad, out_grad, gate_up_grad, down_projection_gradient = (
        lax.psum(qkv_grad.astype(jnp.bfloat16), "dp").astype(jnp.float32),
        lax.psum(out_grad.astype(jnp.bfloat16), "dp").astype(jnp.float32),
        lax.psum(gate_up_grad.astype(jnp.bfloat16), "dp").astype(jnp.float32),
        lax.psum(down_projection_gradient.astype(jnp.bfloat16), "dp").astype(jnp.float32),
    )
    attention_part, feedforward_part = lax.psum(
        (attention_part, feedforward_part), ("dp", "tensor")
    )
    return (
        output,
        tokens_grad,
        qkv_grad,
        out_grad,
        gate_up_grad,
        down_projection_gradient,
        attention_part,
        feedforward_part,
    )


def solution(mesh):
    return jax.shard_map(
        on_device,
        mesh=mesh,
        in_specs=(
            P("tensor", "dp", None),
            P(None, None, "tensor"),
            P("tensor", None),
            P(None, None, "tensor"),
            P("tensor", None),
            P(),
            P(),
            P("dp"),
            P(None, "dp"),
            P("tensor", "dp", None),
        ),
        out_specs=(
            P("tensor", "dp", None),
            P("tensor", "dp", None),
            P(None, None, "tensor"),
            P("tensor", None),
            P(None, None, "tensor"),
            P("tensor", None),
            P(),
            P(),
        ),
        check_vma=False,
    )
```

profile of v0, /device:TPU:0, one launch (start us, length us, event | category | flops | bytes accessed | tf_op | source)
XLA Modules:
  0.0 1161.3 jit_solution(2039333268547181301)
XLA Ops:
  11.1 2.6 fusion.72
  15.2 2.7 broadcast_multiply_fusion.2
  17.9 79.4 %all-gather.5.cloned.1.call-done = bf16[2048,1,1024]{2,0,1:T(8,128)(2,1)} async-done(((bf16[512,1,1024]{2,0,1:T(8,128)(2,1)}), bf16[2048,1,1024]{2,0,1:T(8,128)(2,1)}) %all-gather.5.cloned.1.call-update) | async-done | bytes 4194320 | tf_op jit(solution)/shard_map/all_gather | solution.py:168
  97.3 5.8 fusion.46
  105.0 8.1 fusion.123
  113.2 8.1 fusion.122
  121.3 8.1 fusion.121
  129.4 23.9 %fusion.20 = (f32[4,512]{1,0:T(4,128)S(1)}, f32[4,512]{1,0:T(4,128)S(1)}, f32[4,512]{1,0:T(4,128)S(1)}, f32[4,512]{1,0:T(4,128)S(1)}, f32[4,512,2048]{2,1,0:T(8,128)}) fusion(pred[2048]{0:T(1024)(128)(4,1)S(1)} %and_reduce_fusion, f32[4,512,2048]{2,1,0:T(8,128)} %fusion.121, f32[4,512,2048]{2,1,0:T(8,128)} %fusion.122, f32[4,512,2048]{2,1,0:T(8,128)} %fusion.123, ...), kind=kOutput, calls=%fused_computation.54 | convolution fusion | flops 587194368 | bytes 68454400 | tf_op jit(solution)/shard_map/qshe,kshe->shqk/dot_general | solution.py:64
  153.3 23.8 %fusion = (f32[4,512]{1,0:T(4,128)S(1)}, f32[4,512]{1,0:T(4,128)S(1)}, f32[4,512]{1,0:T(4,128)S(1)}, f32[4,512]{1,0:T(4,128)S(1)}) fusion(f32[4,512]{1,0:T(4,128)S(1)} %get-tuple-element.38, f32[4,512,2048]{2,1,0:T(8,128)} %get-tuple-element.74, pred[2048]{0:T(1024)(128)(4,1)S(1)} %and_reduce_fusion, f32[4,512]{1,0:T(4,128)S(1)} %get-tuple-element.41, ...), kind=kLoop, calls=%fused_computation.24 | loop fusion | flops 67100672 | bytes 67176448 | tf_op jit(solution)/shard_map/reduce_sum | solution.py:77
  177.1 8.0 fusion.109
  185.2 8.0 fusion.110
  193.4 4.6 fusion.111
  198.0 8.3 fusion.108
  206.5 3.3 convert_bitcast_fusion.1
  209.9 75.4 %reduce-scatter.5.cloned.1.call-done = bf16[512,1,1024]{2,0,1:T(8,128)(2,1)} async-done(((bf16[2048,1,1024]{2,0,1:T(8,128)(2,1)}), bf16[512,1,1024]{2,0,1:T(8,128)(2,1)}) %reduce-scatter.5.cloned.1.call-update) | async-done | bytes 1048592 | tf_op jit(solution)/shard_map/reduce_scatter | solution.py:173
  288.6 2.7 multiply_convert_fusion.7
  291.9 80.8 %all-gather.7.cloned.1.call-done = bf16[2048,1,1024]{2,0,1:T(8,128)(2,1)} async-done(((bf16[512,1,1024]{2,0,1:T(8,128)(2,1)}), bf16[2048,1,1024]{2,0,1:T(8,128)(2,1)}) %all-gather.7.cloned.1.call-update) | async-done | bytes 4194320 | tf_op jit(solution)/shard_map/all_gather | solution.py:187
  372.7 15.5 %convolution_bitcast_fusion = f32[2048,1,2,1024]{3,0,2,1:T(8,128)} fusion(bf16[2048,1,1024]{2,0,1:T(8,128)(2,1)} %all-gather.7.cloned.1.call-done, bf16[1024,2,1024]{2,1,0:T(2,128)(2,1)} %param.13), kind=kOutput, calls=%fused_computation.58 | convolution fusion | flops 8589934592 | bytes 25165824 | tf_op jit(solution)/shard_map/lsd,dcf->lscf/dot_general | solution.py:136
  388.2 65.4 %all-gather.9.cloned.1.call-done = bf16[2048,1,1024]{2,0,1:T(8,128)(2,1)} async-done(((bf16[512,1,1024]{2,0,1:T(8,128)(2,1)}), bf16[2048,1,1024]{2,0,1:T(8,128)(2,1)}) %all-gather.9.cloned.1.call-update) | async-done | bytes 4194320 | tf_op jit(solution)/shard_map/all_gather | solution.py:206
  453.6 12.8 %fusion.45 = (bf16[2048,1,1024]{2,0,1:T(8,128)(2,1)S(1)}, bf16[2048,1,1024]{2,0,1:T(8,128)(2,1)S(1)}) fusion(f32[2048,1,2,1024]{3,0,2,1:T(8,128)} %convolution_bitcast_fusion, bf16[1024,1024]{1,0:T(8,128)(2,1)S(1)} %copy-done, bf16[2048,1,1024]{2,0,1:T(8,128)(2,1)} %all-gather.9.cloned.1.call-done), kind=kOutput, calls=%fused_computation.81 | convolution fusion | flops 4322230272 | bytes 31457280 | tf_op jit(solution)/shard_map/gvi,ki->gvk/dot_general | solution.py:212
  469.8 11.2 fusion.29
  481.1 2.6 mul.401
  483.7 2.9 copy.39
  486.7 9.6 fusion.113
  496.2 8.4 fusion.114
  504.7 51.8 %reduce-scatter.9.cloned.1.call-done = bf16[512,1,1024]{2,0,1:T(8,128)(2,1)} async-done(((bf16[2048,1,1024]{2,0,1:T(8,128)(2,1)}), bf16[512,1,1024]{2,0,1:T(8,128)(2,1)}) %reduce-scatter.9.cloned.1.call-update) | async-done | bytes 1048592 | tf_op jit(solution)/shard_map/reduce_scatter | solution.py:224
  556.5 3.2 fusion.82
  559.7 3.9 fusion.163
  563.7 9.6 fusion.115
  573.3 8.5 fusion.112
  583.0 12.4 %fusion.92 = bf16[1024,1024]{1,0:T(8,128)(2,1)} fusion(bf16[2048,1,1024]{2,0,1:T(8,128)(2,1)S(1)} %copy-done.46, f32[2048,1,2,1024]{3,0,2,1:T(8,128)} %convolution_bitcast_fusion), kind=kOutput, calls=%fused_computation.145 | convolution fusion | flops 4308598784 | bytes 23068672 | tf_op jit(solution)/shard_map/poh,pov->hv/dot_general | solution.py:209
  595.4 11.1 fusion.55
  606.5 38.5 %all-gather.11.cloned.1.call-done = bf16[2048,1,1024]{2,0,1:T(8,128)(2,1)} async-done(((bf16[512,1,1024]{2,0,1:T(8,128)(2,1)}), bf16[2048,1,1024]{2,0,1:T(8,128)(2,1)}) %all-gather.11.cloned.1.call-update) | async-done | bytes 4194320 | tf_op jit(solution)/shard_map/all_gather | solution.py:239
  645.0 3.6 fusion.65
  648.7 9.0 fusion.131
  657.7 8.1 fusion.170
  665.8 8.2 fusion.172
  674.0 8.1 fusion.171
  682.2 38.3 %multiply_reduce_fusion = (f32[4,512]{1,0:T(4,128)S(1)}, f32[4,512]{1,0:T(4,128)S(1)}, f32[4,512]{1,0:T(4,128)S(1)}, f32[4,512]{1,0:T(4,128)S(1)}, f32[4,512,2048]{2,1,0:T(8,128)}) fusion(f32[4,512]{1,0:T(4,128)S(1)} %log_add_fusion, f32[4,512,2048]{2,1,0:T(8,128)S(1)} %bitcast.257, pred[2048]{0:T(1024)(128)(4,1)S(1)} %and_reduce_fusion, ...), kind=kOutput, calls=%fused_computation.1 | convolution fusion | flops 620748800 | bytes 135596032 | tf_op jit(solution)/shard_map/qshe,kshe->shqk/dot_general | solution.py:106
  720.5 54.9 %multiply_convert_fusion = (bf16[4,512,2048]{2,1,0:T(8,128)(2,1)}, bf16[4,512,2048]{2,1,0:T(8,128)(2,1)}, bf16[4,512,2048]{2,1,0:T(8,128)(2,1)}, bf16[4,512,2048]{2,1,0:T(8,128)(2,1)}) fusion(f32[4,512,2048]{2,1,0:T(8,128)} %get-tuple-element.75, f32[4,512]{1,0:T(4,128)S(1)} %get-tuple-element.30, f32[4,512]{1,0:T(4,128)S(1)} %log_add_fusion, ...), kind=kLoop, calls=%fused_computation | loop fusion | flops 100663296 | bytes 167839744 | tf_op jit(solution)/shard_map/convert_element_type | solution.py:110
  775.5 7.0 convolution_multiply_fusion.3
  782.5 3.9 fusion.119
  786.4 9.4 convolution_add_fusion.2
  795.8 8.8 convolution_add_fusion.1
  804.7 4.7 fusion.64
  809.4 2.6 copy.42
  812.0 6.2 convolution_multiply_fusion
  818.3 6.3 convolution_multiply_fusion.1
  824.6 2.7 convolution_multiply_fusion.2
  834.2 2.3 maximum_multiply_fusion.3
  842.1 3.0 copy.40
  850.4 3.1 fusion.90
  853.5 5.4 fusion.101
  858.9 4.7 fusion.98
  864.8 7.5 fusion.53
  872.6 13.0 %convert_bitcast_fusion = bf16[2048,1,1024]{2,0,1:T(8,128)(2,1)} fusion(bf16[1024,1024]{1,0:T(8,128)(2,1)S(1)} %copy-done, f32[2048,1,2,1024]{3,0,2,1:T(8,128)} %convolution_bitcast_fusion), kind=kOutput, calls=%fused_computation.79 | convolution fusion | flops 4309647360 | bytes 23068672 | tf_op jit(solution)/shard_map/mtq,qj->mtj/dot_general | solution.py:193
  885.7 104.2 %all-reduce.4.cloned.1.call-done = (bf16[1024,2,1024]{2,0,1:T(8,128)(2,1)}, bf16[1024,3,256]{2,0,1:T(8,128)(2,1)}, bf16[256,1024]{1,0:T(8,128)(2,1)}, bf16[1024,1024]{1,0:T(8,128)(2,1)}) async-done(((bf16[1024,2,1024]{2,0,1:T(8,128)(2,1)}, bf16[1024,3,256]{2,0,1:T(8,128)(2,1)}, bf16[256,1024]{1,0:T(8,128)(2,1)}, bf16[1024,1024]{1,0:T(8,128)(2,1)}), (bf16[1024,2,1024]{2,0,1:T(8,128)(2,1)}, ...) | async-done | bytes 8388624 | tf_op jit(solution)/shard_map/psum | solution.py:287
  992.0 3.3 convert_element_type.322
  995.4 10.0 copy.45
  1005.4 4.1 convert_element_type.342
  1009.4 59.8 %reduce-scatter.11.cloned.1.call-done = bf16[512,1,1024]{2,0,1:T(8,128)(2,1)} async-done(((bf16[2048,1,1024]{2,0,1:T(8,128)(2,1)}), bf16[512,1,1024]{2,0,1:T(8,128)(2,1)}) %reduce-scatter.11.cloned.1.call-update) | async-done | bytes 1048592 | tf_op jit(solution)/shard_map/reduce_scatter | solution.py:272
  1071.5 42.9 %all-reduce = (f32[1024]{0:T(1024)}, f32[1024]{0:T(1024)}) all-reduce(f32[1024]{0:T(1024)S(1)} %get-tuple-element.26, f32[1024]{0:T(1024)S(1)} %copy-done.42), channel_id=1, replica_groups=mesh['dp'=8,'tensor'=4] {'dp','tensor'}, use_global_device_ids=true, to_apply=%region_29.30 | all-reduce | flops 2048 | bytes 16384 | tf_op jit(solution)/shard_map/psum | solution.py:290
  1114.4 35.5 %reduce-scatter.7.cloned.1.call-done = bf16[512,1,1024]{2,0,1:T(8,128)(2,1)} async-done(((bf16[2048,1,1024]{2,0,1:T(8,128)(2,1)}), bf16[512,1,1024]{2,0,1:T(8,128)(2,1)}) %reduce-scatter.7.cloned.1.call-update) | async-done | bytes 1048592 | tf_op jit(solution)/shard_map/reduce_scatter | solution.py:192
  1149.9 4.6 fusion.76
  (207 shorter events, 39.2 us)
Async XLA Ops:
  7.2 446.4 %copy-start = (bf16[1024,1024]{1,0:T(8,128)(2,1)S(1)}, bf16[1024,1024]{1,0:T(8,128)(2,1)}, u32[]{:S(2)}) copy-start(bf16[1024,1024]{1,0:T(8,128)(2,1)} %param.14) | copy-start | bytes 6291460
  7.2 90.1 %all-gather.5.cloned.1.call-start = ((), (), s32[]{:S(2)}) async-start(), calls=%async_computation.4 | async-start | bytes 5242880 | tf_op jit(solution)/shard_map/all_gather | solution.py:168
  13.7 271.6 %reduce-scatter.5.cloned.1.call-start = ((), (), s32[]{:S(2)}) async-start(), calls=%async_computation.5 | async-start | bytes 5242880 | tf_op jit(solution)/shard_map/reduce_scatter | solution.py:173
  17.9 86.6 %copy-start.11 = (f32[2048,64]{0,1:T(8,128)}, f32[2048,64]{0,1:T(8,128)S(1)}, u32[]{:S(2)}) copy-start(f32[2048,64]{0,1:T(8,128)S(1)} %get-tuple-element.68) | copy-start | bytes 1572868
  17.9 86.6 %copy-start.13 = (f32[2048,64]{0,1:T(8,128)}, f32[2048,64]{0,1:T(8,128)S(1)}, u32[]{:S(2)}) copy-start(f32[2048,64]{0,1:T(8,128)S(1)} %get-tuple-element.69) | copy-start | bytes 1572868
  103.3 94.7 %copy-start.6 = (bf16[2048,1,1,256]{0,3,2,1:T(8,128)(2,1)}, bf16[2048,1,1,256]{0,3,2,1:T(8,128)(2,1)S(1)}, u32[]{:S(2)}) copy-start(bf16[2048,1,1,256]{0,3,2,1:T(8,128)(2,1)S(1)} %slice.175) | copy-start | bytes 3145732
  104.4 25.0 %copy-start.9 = (bf16[2048,1,4,64]{0,3,2,1:T(8,128)(2,1)}, bf16[2048,1,4,64]{0,3,2,1:T(8,128)(2,1)S(1)}, u32[]{:S(2)}) copy-start(bf16[2048,1,4,64]{0,3,2,1:T(8,128)(2,1)S(1)} %fusion.86) | copy-start | bytes 3145732
  105.0 24.4 %copy-start.3 = (bf16[2048,4,64]{0,2,1:T(8,128)(2,1)}, bf16[2048,4,64]{0,2,1:T(8,128)(2,1)S(1)}, u32[]{:S(2)}) copy-start(bf16[2048,4,64]{0,2,1:T(8,128)(2,1)S(1)} %fusion.88) | copy-start | bytes 3145732
  177.1 16.1 %slice-start = ((s8[16777216]{0:T(1024)(128)(4,1)}), s8[4194304]{0:T(1024)(128)(4,1)S(1)}, s32[]{:S(2)}) async-start(s8[16777216]{0:T(1024)(128)(4,1)} %bitcast.254), calls=%async_computation.13 | async-start | bytes 8388608
  177.1 16.1 %slice-start.1 = ((s8[16777216]{0:T(1024)(128)(4,1)}), s8[4194304]{0:T(1024)(128)(4,1)S(1)}, s32[]{:S(2)}) async-start(s8[16777216]{0:T(1024)(128)(4,1)} %bitcast.254), calls=%async_computation.14 | async-start | bytes 8388608
  185.2 8.1 slice-start.2
  185.2 8.2 slice-start.3
  198.0 8.5 copy-start.47
  206.3 78.9 %copy-start.1 = (bf16[512,1,1024]{2,0,1:T(8,128)(2,1)S(1)}, bf16[512,1,1024]{2,0,1:T(8,128)(2,1)}, u32[]{:S(2)}) copy-start(bf16[512,1,1024]{2,0,1:T(8,128)(2,1)} %param.10) | copy-start | bytes 3145732
  206.3 82.2 %copy-start.29 = (f32[1024]{0:T(1024)S(1)}, f32[1024]{0:T(1024)}, u32[]{:S(2)}) copy-start(f32[1024]{0:T(1024)} %param.16) | copy-start | bytes 12292
  209.8 162.9 %all-gather.7.cloned.1.call-start = ((), (), s32[]{:S(2)}) async-start(), calls=%async_computation.6 | async-start | bytes 5242880 | tf_op jit(solution)/shard_map/all_gather | solution.py:187
  286.9 272.8 %copy-start.27 = (f32[512]{0:T(512)}, f32[512]{0:T(512)S(1)}, u32[]{:S(2)}) copy-start(f32[512]{0:T(512)S(1)} %broadcast_multiply_fusion.7) | copy-start | bytes 6148
  288.6 271.1 %copy-start.31 = (f32[512]{0:T(512)}, f32[512]{0:T(512)S(1)}, u32[]{:S(2)}) copy-start(f32[512]{0:T(512)S(1)} %add_rsqrt_fusion) | copy-start | bytes 6148
  291.3 162.3 %all-gather.9.cloned.1.call-start = ((), (), s32[]{:S(2)}) async-start(), calls=%async_computation.8 | async-start | bytes 5242880 | tf_op jit(solution)/shard_map/all_gather | solution.py:206
  291.9 264.6 %reduce-scatter.9.cloned.1.call-start = ((), (), s32[]{:S(2)}) async-start(), calls=%async_computation.9 | async-start | bytes 5242880 | tf_op jit(solution)/shard_map/reduce_scatter | solution.py:224
  453.6 16.2 %copy-start.43 = (bf16[1024,2,1024]{2,1,0:T(2,128)(2,1)S(1)}, bf16[1024,2,1024]{2,1,0:T(2,128)(2,1)}, u32[]{:S(2)}) copy-start(bf16[1024,2,1024]{2,1,0:T(2,128)(2,1)} %param.13) | copy-start | bytes 12582916
  481.0 164.0 %all-gather.11.cloned.1.call-start = ((), (), s32[]{:S(2)}) async-start(), calls=%async_computation.10 | async-start | bytes 5242880 | tf_op jit(solution)/shard_map/all_gather | solution.py:239
  486.6 9.6 copy-start.7
  563.6 9.7 copy-start.8
  563.6 426.2 %all-reduce.4.cloned.1.call-start = ((), (), s32[]{:S(2)}) async-start(), calls=%async_computation.12 | async-start | bytes 16777216 | tf_op jit(solution)/shard_map/psum | solution.py:287
  573.3 8.6 copy-start.26
  573.3 9.7 copy-start.46
  583.0 12.4 %copy-start.45 = (bf16[2048,1,1024]{2,0,1:T(8,128)(2,1)S(1)}, bf16[2048,1,1024]{2,0,1:T(8,128)(2,1)}, u32[]{:S(2)}) copy-start(bf16[2048,1,1024]{2,0,1:T(8,128)(2,1)} %all-gather.7.cloned.1.call-done) | copy-start | bytes 12582916
  583.0 12.4 %copy-start.50 = (bf16[2048,1,1024]{2,0,1:T(8,128)(2,1)S(1)}, bf16[2048,1,1024]{2,0,1:T(8,128)(2,1)}, u32[]{:S(2)}) copy-start(bf16[2048,1,1024]{2,0,1:T(8,128)(2,1)} %copy-done.49) | copy-start | bytes 12582916
  583.0 12.4 %copy-start.52 = (bf16[2048,1,1024]{2,0,1:T(8,128)(2,1)S(1)}, bf16[2048,1,1024]{2,0,1:T(8,128)(2,1)}, u32[]{:S(2)}) copy-start(bf16[2048,1,1024]{2,0,1:T(8,128)(2,1)} %copy-done.51) | copy-start | bytes 12582916
  665.8 16.3 %slice-start.4 = ((s8[16777216]{0:T(1024)(128)(4,1)}), s8[4194304]{0:T(1024)(128)(4,1)S(1)}, s32[]{:S(2)}) async-start(s8[16777216]{0:T(1024)(128)(4,1)} %bitcast.256), calls=%async_computation.17 | async-start | bytes 8388608
  665.8 16.3 %slice-start.5 = ((s8[16777216]{0:T(1024)(128)(4,1)}), s8[4194304]{0:T(1024)(128)(4,1)S(1)}, s32[]{:S(2)}) async-start(s8[16777216]{0:T(1024)(128)(4,1)} %bitcast.256), calls=%async_computation.18 | async-start | bytes 8388608
  674.0 8.1 slice-start.6
  674.0 8.1 slice-start.7
  720.5 55.0 %copy-start.4 = (bf16[2048,4,64]{0,2,1:T(8,128)(2,1)S(1)}, bf16[2048,4,64]{0,2,1:T(8,128)(2,1)}, u32[]{:S(2)}) copy-start(bf16[2048,4,64]{0,2,1:T(8,128)(2,1)} %copy-done.3) | copy-start | bytes 3145732
  775.4 7.0 copy-start.5
  775.5 10.9 copy-start.48
  786.4 18.2 %slice-start.8 = ((s8[16777216]{0:T(1024)(128)(4,1)}), s8[4194304]{0:T(1024)(128)(4,1)S(1)}, s32[]{:S(2)}) async-start(s8[16777216]{0:T(1024)(128)(4,1)} %bitcast.258), calls=%async_computation.21 | async-start | bytes 8388608
  786.4 18.2 %slice-start.9 = ((s8[16777216]{0:T(1024)(128)(4,1)}), s8[4194304]{0:T(1024)(128)(4,1)S(1)}, s32[]{:S(2)}) async-start(s8[16777216]{0:T(1024)(128)(4,1)} %bitcast.258), calls=%async_computation.22 | async-start | bytes 8388608
  795.8 8.8 slice-start.10
  795.8 8.8 slice-start.11
  812.0 12.5 %slice-start.16 = ((s8[8388608]{0:T(1024)(128)(4,1)}), s8[4194304]{0:T(1024)(128)(4,1)S(1)}, s32[]{:S(2)}) async-start(s8[8388608]{0:T(1024)(128)(4,1)} %bitcast.264), calls=%async_computation.29 | async-start | bytes 8388608
  818.2 16.0 %copy-start.16 = (f32[4,64,512]{2,1,0:T(8,128)}, f32[4,64,512]{2,1,0:T(8,128)S(1)}, u32[]{:S(2)}) copy-start(f32[4,64,512]{2,1,0:T(8,128)S(1)} %convolution_multiply_fusion) | copy-start | bytes 1572868
  818.2 6.3 slice-start.17
  818.2 9.0 copy-start.10
  818.2 9.0 copy-start.14
  824.5 9.7 copy-start.18
  827.2 7.0 copy-start.19
  838.8 10.5 copy-start.17
  850.4 8.5 copy-start.24
  850.4 8.5 copy-start.25
  850.4 8.5 copy-start.44
  863.6 205.6 %reduce-scatter.11.cloned.1.call-start = ((), (), s32[]{:S(2)}) async-start(), calls=%async_computation.11 | async-start | bytes 5242880 | tf_op jit(solution)/shard_map/reduce_scatter | solution.py:272
  872.4 277.5 %reduce-scatter.7.cloned.1.call-start = ((), (), s32[]{:S(2)}) async-start(), calls=%async_computation.7 | async-start | bytes 5242880 | tf_op jit(solution)/shard_map/reduce_scatter | solution.py:192
  995.3 73.9 %copy-start.2 = (bf16[512,1,1024]{2,0,1:T(8,128)(2,1)S(1)}, bf16[512,1,1024]{2,0,1:T(8,128)(2,1)}, u32[]{:S(2)}) copy-start(bf16[512,1,1024]{2,0,1:T(8,128)(2,1)} %param.10) | copy-start | bytes 3145732
  995.3 73.9 %copy-start.34 = (f32[512]{0:T(512)S(1)}, f32[512]{0:T(512)}, u32[]{:S(2)}) copy-start(f32[512]{0:T(512)} %copy-done.33) | copy-start | bytes 6148
  995.3 73.9 %copy-start.35 = (f32[1024]{0:T(1024)S(1)}, f32[1024]{0:T(1024)}, u32[]{:S(2)}) copy-start(f32[1024]{0:T(1024)} %param.15) | copy-start | bytes 12292
  995.3 73.9 %copy-start.37 = (f32[512]{0:T(512)S(1)}, f32[512]{0:T(512)}, u32[]{:S(2)}) copy-start(f32[512]{0:T(512)} %copy-done.36) | copy-start | bytes 6148
  995.3 76.1 %copy-start.42 = (f32[1024]{0:T(1024)S(1)}, f32[1024]{0:T(1024)}, u32[]{:S(2)}) copy-start(f32[1024]{0:T(1024)} %get-tuple-element.24) | copy-start | bytes 12292
  995.3 154.5 %copy-start.28 = (f32[512]{0:T(512)S(1)}, f32[512]{0:T(512)}, u32[]{:S(2)}) copy-start(f32[512]{0:T(512)} %copy-done.27) | copy-start | bytes 6148
  995.3 154.5 %copy-start.30 = (f32[1024]{0:T(1024)S(1)}, f32[1024]{0:T(1024)}, u32[]{:S(2)}) copy-start(f32[1024]{0:T(1024)} %param.16) | copy-start | bytes 12292
  995.4 154.5 %copy-start.32 = (f32[512]{0:T(512)S(1)}, f32[512]{0:T(512)}, u32[]{:S(2)}) copy-start(f32[512]{0:T(512)} %copy-done.31) | copy-start | bytes 6148
  995.4 154.5 %copy-start.39 = (f32[512]{0:T(512)S(1)}, f32[512]{0:T(512)}, u32[]{:S(2)}) copy-start(f32[512]{0:T(512)} %copy-done.38) | copy-start | bytes 6148
  995.4 154.5 %copy-start.41 = (f32[512]{0:T(512)S(1)}, f32[512]{0:T(512)}, u32[]{:S(2)}) copy-start(f32[512]{0:T(512)} %copy-done.40) | copy-start | bytes 6148
  (16 other events, 43.8 us)
Sparse Core Ops, SparseCore 0:
  13.8 83.4 all-gather.4
  210.0 75.2 reduce-scatter.4
  291.4 81.2 all-gather.6
  374.2 79.2 all-gather.8
  481.1 75.2 reduce-scatter.8
  563.7 81.2 all-gather.10
  863.7 126.0 all-reduce.3
  992.2 76.9 reduce-scatter.10
  1071.5 78.2 reduce-scatter.6
where the time goes:
time: 1170 us; the launch traced here: 1160 us
  waiting for transfers between devices  591 us (51%)
  matrix products  345 us (29%)
  other arithmetic  129 us (11%)
  blocking collectives  42.9 us (4%)
  local copies, waits for them, and re-layouts  36.5 us (3%)
  between operations  15.7 us (1%)
    psum x1, waiting for transfers between devices, on_device(): lax.psum(gate_up_grad.astype(jnp.bfloat16), 'dp').astype(jnp.float32)  104 us
    all_gather x1, waiting for transfers between devices, on_device(): gathered_ffn = lax.all_gather(normed_ffn, 'tensor', axis=0, tiled=True)  80.8 us
    all_gather x1, waiting for transfers between devices, on_device(): gathered_attn = lax.all_gather(normed_attn, 'tensor', axis=0, tiled=True)  79.4 us
    reduce_scatter x1, waiting for transfers between devices, on_device(): lax.psum_scatter(jnp.einsum('mtq,qj->mtj', shard_portion, output_projecti...  75.4 us
    all_gather x1, waiting for transfers between devices, on_device(): lax.all_gather(cotangent, 'tensor', axis=0, tiled=True)  65.4 us
    dot_general x4, matrix products, attend_back(): jnp.einsum('qshe,kshe->shqk', grad_block, values_heads, preferred_element...  62.7 us
    reduce_scatter x1, waiting for transfers between devices, on_device(): lax.psum_scatter(jnp.einsum('lscf,dcf->lsd', shard_portion, qkv_weight, p...  59.8 us
    convert_element_type x1, other arithmetic, attend_back(): score_grad = (prob_rows * (prob_grad - centre)).astype(jnp.bfloat16)  54.9 us
  transfers between devices with their start and end apart: 9, of which 9 were waited for; matrix products, arithmetic and copies ran while one was open for 11% of the time, Pallas kernels for 0%

commit v1 on v0

v1 whole, which is shorter than its diff:
```python
import functools
import math

import jax
import jax.numpy as jnp
from jax import lax
from jax.experimental import pallas as pl
from jax.experimental.pallas import tpu as pltpu
from jax.sharding import PartitionSpec as P

HEAD_DIM = 64
EPSILON = 1e-05
MASKED = -1000000000.0
ROPE_BASE = 10000.0
LOG2E = math.log2(math.e)
SCALE = HEAD_DIM ** (-0.5)
BF16 = jnp.bfloat16
F32 = jnp.float32
MIB = 1 << 20


def dot(a, b, ca, cb):
    return lax.dot_general(a, b, (((ca,), (cb,)), ((), ())), preferred_element_type=F32)


def call(body, name, out, vmem=56, flops=0, moved=0, **kw):
    return pl.pallas_call(
        body,
        out_shape=out,
        name=name,
        compiler_params=pltpu.CompilerParams(vmem_limit_bytes=vmem * MIB),
        cost_estimate=pl.CostEstimate(flops=flops, bytes_accessed=moved, transcendentals=0),
        **kw,
    )


def shape(s, d):
    return jax.ShapeDtypeStruct(s, d)


def norm_rows(x, gain):
    centered = x - jnp.mean(x, axis=-1, keepdims=True)
    inverse = lax.rsqrt(jnp.mean(centered * centered, axis=-1, keepdims=True) + EPSILON)
    scaled = centered * inverse
    return scaled * gain, scaled, inverse


def norm_kernel(x_ref, g_ref, o_ref):
    o_ref[...] = norm_rows(x_ref[...].astype(F32), g_ref[...])[0].astype(BF16)


def norm_call(x, gain):
    n, d = x.shape
    b = min(128, n)
    return call(
        norm_kernel,
        "norm_tokens",
        shape((n, d), BF16),
        grid=(n // b,),
        in_specs=[pl.BlockSpec((b, d), lambda i: (i, 0)), pl.BlockSpec((1, d), lambda i: (0, 0))],
        out_specs=pl.BlockSpec((b, d), lambda i: (i, 0)),
        flops=12 * n * d,
        moved=4 * n * d,
    )(x, gain)


def middle_kernel(x_ref, g_ref, *refs):
    parts, (m_ref, o_ref) = refs[:-2], refs[-2:]
    m = x_ref[...].astype(F32)
    for p in parts:
        m = m + p[...].astype(F32)
    m_ref[...] = m
    o_ref[...] = norm_rows(m, g_ref[...])[0].astype(BF16)


def middle_call(x, gain, parts):
    n, d = x.shape
    b = min(128, n)
    row = pl.BlockSpec((b, d), lambda i: (i, 0))
    return call(
        middle_kernel,
        "middle_norm",
        (shape((n, d), F32), shape((n, d), BF16)),
        grid=(n // b,),
        in_specs=[row, pl.BlockSpec((1, d), lambda i: (0, 0))] + [row] * len(parts),
        out_specs=(row, row),
        flops=12 * n * d,
        moved=10 * n * d,
    )(x, gain, *parts)


def back_kernel(n_parts, keep, base_ref, x_ref, g_ref, *refs):
    parts, outs = refs[:n_parts], refs[n_parts:]
    e = parts[0][...].astype(F32)
    for p in parts[1:]:
        e = e + p[...].astype(F32)
    gain = g_ref[...]
    _, scaled, inverse = norm_rows(x_ref[...].astype(F32), gain)
    through = e * gain
    first = jnp.mean(through, axis=-1, keepdims=True)
    second = jnp.mean(through * scaled, axis=-1, keepdims=True)
    total = base_ref[...].astype(F32) + inverse * (through - first - scaled * second)
    if keep:
        outs[0][...] = total
    outs[-2][...] = total.astype(BF16)

    @pl.when(pl.program_id(0) == 0)
    def _():
        outs[-1][...] = jnp.zeros_like(outs[-1])

    outs[-1][...] += jnp.sum(e * scaled, axis=0, keepdims=True)


def back_call(name, base, x, gain, parts, keep):
    n, d = x.shape
    b = min(128, n)
    row = pl.BlockSpec((b, d), lambda i: (i, 0))
    one = pl.BlockSpec((1, d), lambda i: (0, 0))
    out = [shape((n, d), F32)] * keep + [shape((n, d), BF16), shape((1, d), F32)]
    return call(
        functools.partial(back_kernel, len(parts), keep),
        name,
        tuple(out),
        grid=(n // b,),
        in_specs=[row, row, one] + [row] * len(parts),
        out_specs=tuple([row] * (keep + 1) + [one]),
        flops=25 * n * d,
        moved=12 * n * d,
    )(base, x, gain, *parts)


def output_kernel(m_ref, *refs):
    total = m_ref[...]
    for p in refs[:-1]:
        total = total + p[...].astype(F32)
    refs[-1][...] = total.astype(BF16)


def output_call(m, parts):
    n, d = m.shape
    b = min(256, n)
    row = pl.BlockSpec((b, d), lambda i: (i, 0))
    return call(
        output_kernel,
        "output_sum",
        shape((n, d), BF16),
        grid=(n // b,),
        in_specs=[row] * (1 + len(parts)),
        out_specs=row,
        flops=4 * n * d,
        moved=10 * n * d,
    )(m, *parts)


def turn(u, cos, sin):
    half = HEAD_DIM // 2
    first, second = u[:half], u[half:]
    return jnp.concatenate([first * cos - second * sin, second * cos + first * sin], axis=0)


def turn_back(u, cos, sin):
    half = HEAD_DIM // 2
    first, second = u[:half], u[half:]
    return jnp.concatenate([first * cos + second * sin, second * cos - first * sin], axis=0)


def qkv_kernel(n_parts, c_ref, s_ref, w_ref, *refs):
    parts, (q_ref, k_ref, v_ref) = refs[:n_parts], refs[n_parts:]
    n = parts[0].shape[0]
    for i, p in enumerate(parts):
        cols = slice(i * n, (i + 1) * n)
        cos, sin = c_ref[:, cols], s_ref[:, cols]
        for which, out in enumerate((q_ref, k_ref, v_ref)):
            u = dot(w_ref[which], p[...], 0, 1)
            for h in range(u.shape[0] // HEAD_DIM):
                rows = slice(h * HEAD_DIM, (h + 1) * HEAD_DIM)
                head = u[rows]
                if which < 2:
                    head = turn(head, cos, sin)
                out[rows, cols] = head.astype(BF16)


def qkv_call(parts, w, cos, sin):
    n, d = parts[0].shape
    f = w.shape[2]
    total = n * len(parts)
    return call(
        functools.partial(qkv_kernel, len(parts)),
        "project_heads",
        (shape((f, total), BF16),) * 3,
        flops=6 * f * d * total,
        moved=2 * (total * d + 3 * d * f + 3 * f * total),
    )(cos, sin, w, *parts)


def split(x, n):
    out = []
    for _ in range(n):
        h = x.astype(BF16)
        out.append(h)
        x = x - h.astype(F32)
    return out


def attend_kernel(q_ref, k_ref, v_ref, b_ref, o_ref, l_ref, ka, va, *, sub):
    S = k_ref.shape[1]
    bq = q_ref.shape[1]

    @pl.when(pl.program_id(1) == 0)
    def _():
        k = k_ref[...]
        ka[...] = jnp.concatenate([k, k, b_ref[...]], axis=0).T
        va[0:HEAD_DIM] = v_ref[...]
        va[HEAD_DIM:] = jnp.ones((16, S), BF16)

    high, low = split(q_ref[...].astype(F32) * (SCALE * LOG2E), 2)
    row = lax.broadcasted_iota(jnp.int32, (16, bq), 0)
    one = jnp.where(row == 0, 1.0, 0.0).astype(BF16)
    qa = jnp.concatenate([high, low, one], axis=0)
    steps = bq // sub

    def scores(i):
        return dot(ka[...], qa[:, i * sub : (i + 1) * sub], 1, 0)

    s = scores(0)
    for i in range(steps):
        later = scores(i + 1) if i + 1 < steps else None
        cols = slice(i * sub, (i + 1) * sub)
        top = jnp.max(s, axis=0, keepdims=True)
        p = jnp.exp2(s - top).astype(BF16)
        o = dot(va[...], p, 1, 0)
        total = o[HEAD_DIM : HEAD_DIM + 1]
        o_ref[:, cols] = (o[:HEAD_DIM] * (1.0 / total)).astype(BF16)
        l_ref[0, :, cols] = jnp.broadcast_to(top + jnp.log2(total), (8, sub))
        s = later


def attend_call(q, k, v, bias):
    f, S = q.shape
    heads = f // HEAD_DIM
    bq = S
    sub = min(256, S)
    whole = pl.BlockSpec((HEAD_DIM, S), lambda h, i: (h, 0))
    block = pl.BlockSpec((HEAD_DIM, bq), lambda h, i: (h, i))
    return call(
        functools.partial(attend_kernel, sub=sub),
        "attend",
        (shape((f, S), BF16), shape((heads, 8, S), F32)),
        grid=(heads, S // bq),
        in_specs=[block, whole, whole, pl.BlockSpec((16, S), lambda h, i: (0, 0))],
        out_specs=(block, pl.BlockSpec((1, 8, bq), lambda h, i: (h, 0, i))),
        scratch_shapes=[
            pltpu.VMEM((S, 2 * HEAD_DIM + 16), BF16),
            pltpu.VMEM((HEAD_DIM + 16, S), BF16),
        ],
        flops=16 * f * S * S,
        moved=10 * f * S,
    )(q, k, v, bias)


def attend_back_kernel(
    q_ref, k_ref, v_ref, b_ref, o_ref, l_ref, g_ref, c_ref, s_ref, ck_ref, sk_ref,
    dq_ref, dk_ref, dv_ref, ka, va, dka, dva, *, sub
):
    S = k_ref.shape[1]
    bq = q_ref.shape[1]

    @pl.when(pl.program_id(1) == 0)
    def _():
        k = k_ref[...]
        one = jnp.ones((16, S), BF16)
        ka[...] = jnp.concatenate([k, k, b_ref[...], one], axis=0).T
        va[...] = jnp.concatenate([v_ref[...], one], axis=0).T
        dka[...] = jnp.zeros_like(dka)
        dva[...] = jnp.zeros_like(dva)

    q = q_ref[...].astype(F32) * SCALE
    qs = q.astype(BF16)
    high, low = split(q * LOG2E, 2)
    row = lax.broadcasted_iota(jnp.int32, (16, bq), 0)

    def spread(x):
        a, b, c = [y.astype(F32) for y in split(x, 3)]
        rest = jnp.where(row == 2, c, 0.0)
        return jnp.where(row == 0, a, jnp.where(row == 1, b, rest)).astype(BF16)

    one = jnp.where(row == 0, 1.0, 0.0).astype(BF16)
    g = g_ref[...]
    qa = jnp.concatenate([high, low, one, spread(-l_ref[0, 0:1])], axis=0)
    centre = jnp.sum(g.astype(F32) * o_ref[...].astype(F32), axis=0, keepdims=True)
    ga = jnp.concatenate([g, spread(-centre)], axis=0)
    for i in range(bq // sub):
        cols = slice(i * sub, (i + 1) * sub)
        p = jnp.exp2(dot(ka[...], qa[:, cols], 1, 0))
        p_low = p.astype(BF16)
        ds = (p * dot(va[...], ga[:, cols], 1, 0)).astype(BF16)
        dva[...] += dot(g[:, cols], p_low, 1, 1)
        dka[...] += dot(qs[:, cols], ds, 1, 1)
        dq = dot(k_ref[...], ds, 1, 0) * SCALE
        dq_ref[:, cols] = turn_back(dq, c_ref[:, cols], s_ref[:, cols]).astype(BF16)

    @pl.when(pl.program_id(1) == pl.num_programs(1) - 1)
    def _():
        dk_ref[...] = turn_back(dka[...], ck_ref[...], sk_ref[...]).astype(BF16)
        dv_ref[...] = dva[...].astype(BF16)


def attend_back_call(q, k, v, bias, o, lse, g, cos, sin):
    f, S = q.shape
    heads = f // HEAD_DIM
    bq = min(1024, S)
    half = HEAD_DIM // 2
    whole = pl.BlockSpec((HEAD_DIM, S), lambda h, i: (h, 0))
    block = pl.BlockSpec((HEAD_DIM, bq), lambda h, i: (h, i))
    table = pl.BlockSpec((half, S), lambda h, i: (0, 0))
    table_block = pl.BlockSpec((half, bq), lambda h, i: (0, i))
    return call(
        functools.partial(attend_back_kernel, sub=min(256, S)),
        "attend_back",
        (shape((f, S), BF16),) * 3,
        grid=(heads, S // bq),
        in_specs=[
            block, whole, whole,
            pl.BlockSpec((16, S), lambda h, i: (0, 0)),
            block,
            pl.BlockSpec((1, 8, bq), lambda h, i: (h, 0, i)),
            block, table_block, table_block, table, table,
        ],
        out_specs=(block, whole, whole),
        scratch_shapes=[
            pltpu.VMEM((S, 2 * HEAD_DIM + 32), BF16),
            pltpu.VMEM((S, HEAD_DIM + 16), BF16),
            pltpu.VMEM((HEAD_DIM, S), F32),
            pltpu.VMEM((HEAD_DIM, S), F32),
        ],
        flops=40 * f * S * S,
        moved=20 * f * S,
    )(q, k, v, bias, o, lse, g, cos, sin, cos, sin)


def out_kernel(n_parts, o_ref, w_ref, *outs):
    n = outs[0].shape[0]
    for i, out in enumerate(outs):
        out[...] = dot(o_ref[:, i * n : (i + 1) * n], w_ref[...], 0, 0).astype(BF16)


def out_call(o, w, n_parts):
    f, S = o.shape
    d = w.shape[1]
    return call(
        functools.partial(out_kernel, n_parts),
        "output_projection",
        (shape((S // n_parts, d), BF16),) * n_parts,
        flops=2 * f * S * d,
        moved=2 * (f * S + f * d + S * d),
    )(o, w)


def heads_grad_kernel(n_parts, o_ref, w_ref, *refs):
    parts, (g_ref, dw_ref) = refs[:n_parts], refs[n_parts:]
    n = parts[0].shape[0]
    total = None
    for i, p in enumerate(parts):
        cols = slice(i * n, (i + 1) * n)
        g_ref[:, cols] = dot(w_ref[...], p[...], 1, 1).astype(BF16)
        term = dot(o_ref[:, cols], p[...], 1, 0)
        total = term if total is None else total + term
    dw_ref[...] = total.astype(BF16)


def heads_grad_call(o, w, parts):
    f, S = o.shape
    d = w.shape[1]
    return call(
        functools.partial(heads_grad_kernel, len(parts)),
        "heads_grad",
        (shape((f, S), BF16), shape((f, d), BF16)),
        flops=4 * f * S * d,
        moved=2 * (2 * f * S + 2 * f * d + S * d),
    )(o, w, *parts)


def qkv_back_kernel(n_parts, w_ref, q_ref, k_ref, v_ref, *refs):
    parts, outs, dw_ref = refs[:n_parts], refs[n_parts : 2 * n_parts], refs[-1]
    n = parts[0].shape[0]
    grads = (q_ref, k_ref, v_ref)
    for i, out in enumerate(outs):
        cols = slice(i * n, (i + 1) * n)
        total = dot(grads[0][:, cols], w_ref[0], 0, 1)
        for j in (1, 2):
            total = total + dot(grads[j][:, cols], w_ref[j], 0, 1)
        out[...] = total.astype(BF16)
    for j in range(3):
        total = dot(parts[0][...], grads[j][:, 0:n], 0, 1)
        for i in range(1, n_parts):
            total = total + dot(parts[i][...], grads[j][:, i * n : (i + 1) * n], 0, 1)
        dw_ref[j] = total.astype(BF16)


def qkv_back_call(w, dq, dk, dv, parts):
    f, S = dq.shape
    n, d = parts[0].shape
    res = call(
        functools.partial(qkv_back_kernel, len(parts)),
        "qkv_back",
        tuple([shape((n, d), BF16)] * len(parts) + [shape((3, d, f), BF16)]),
        flops=12 * f * S * d,
        moved=2 * (3 * f * S + 6 * f * d + 2 * S * d),
    )(w, dq, dk, dv, *parts)
    return res[:-1], res[-1]


def ffn_kernel(groups, *refs):
    x_ref, c_ref = refs[:2]
    weights = refs[2 : 2 + 3 * groups]
    h_ref, gl_ref, ul_ref, out_ref, dx_ref = refs[2 + 3 * groups :]
    x, c = x_ref[...], c_ref[...]
    out = dx = None
    for m in range(groups):
        wg, wu, wd = [r[...].reshape(-1, r.shape[-1]) for r in weights[3 * m : 3 * m + 3]]
        gate = dot(x, wg, 1, 1)
        up = dot(x, wu, 1, 1)
        hg = dot(c, wd, 1, 1)
        sig = jax.nn.sigmoid(gate)
        act = gate * sig
        hidden = (act * up).astype(BF16)
        gl = (hg * up * (sig * (1.0 + gate * (1.0 - sig)))).astype(BF16)
        ul = (hg * act).astype(BF16)
        cols = slice(m * wg.shape[0], (m + 1) * wg.shape[0])
        h_ref[:, cols] = hidden
        gl_ref[:, cols] = gl
        ul_ref[:, cols] = ul
        o = dot(hidden, wd, 1, 0)
        e = dot(gl, wg, 1, 0) + dot(ul, wu, 1, 0)
        out = o if out is None else out + o
        dx = e if dx is None else dx + e
    out_ref[...] = out.astype(BF16)
    dx_ref[...] = dx.astype(BF16)


def ffn_call(x, c, weights):
    n, d = x.shape
    groups = len(weights)
    T, _, us, _ = weights[0].shape
    units = groups * T * us
    b = min(256, n)
    row = pl.BlockSpec((b, d), lambda i: (i, 0))
    urow = pl.BlockSpec((b, units), lambda i: (i, 0))
    specs, args = [], []
    for w in weights:
        for j in range(3):
            specs.append(
                pl.BlockSpec((T, None, us, d), functools.partial(lambda j, i: (0, j, 0, 0), j))
            )
            args.append(w)
    return call(
        functools.partial(ffn_kernel, groups),
        "feed_forward",
        (shape((n, units), BF16),) * 3 + (shape((n, d), BF16),) * 2,
        grid=(n // b,),
        in_specs=[row, row] + specs,
        out_specs=(urow,) * 3 + (row, row),
        flops=12 * n * d * units,
        moved=2 * (4 * n * d + 3 * n * units + 3 * d * units),
    )(x, c, *args)


def ffn_weight_kernel(n_parts, T, us, *refs):
    x, c, h, gl, ul = [refs[i * n_parts : (i + 1) * n_parts] for i in range(5)]
    dn_ref, gu_ref = refs[5 * n_parts :]

    def product(a, b):
        total = dot(a[0][...], b[0][...], 0, 0)
        for i in range(1, n_parts):
            total = total + dot(a[i][...], b[i][...], 0, 0)
        return total.astype(BF16)

    dn_ref[...] = product(h, c).reshape(dn_ref.shape)
    for j, g in enumerate((gl, ul)):
        dw = product(x, g)
        for t in range(dn_ref.shape[0]):
            gu_ref[t, j] = dw[:, t * us : (t + 1) * us]


def ffn_weight_call(x, c, h, gl, ul, m, T, us):
    n_parts = len(x)
    n, d = x[0].shape
    tb = max(1, min(T, 256 // us))
    row = pl.BlockSpec((n, d), lambda i: (0, 0))
    urow = pl.BlockSpec((n, tb * us), lambda i: (0, m * (T // tb) + i))
    return call(
        functools.partial(ffn_weight_kernel, n_parts, T, us),
        "feed_forward_weights",
        (shape((T, us, d), BF16), shape((T, 2, d, us), BF16)),
        grid=(T // tb,),
        in_specs=[row] * (2 * n_parts) + [urow] * (3 * n_parts),
        out_specs=(
            pl.BlockSpec((tb, us, d), lambda i: (i, 0, 0)),
            pl.BlockSpec((tb, 2, d, us), lambda i: (i, 0, 0, 0)),
        ),
        flops=6 * n * n_parts * d * T * us,
        moved=2 * (2 * n * n_parts * d + 3 * n * n_parts * T * us + 3 * d * T * us),
    )(*x, *c, *h, *gl, *ul)


def build(DP, T):
    M = DP // 4
    R = T // 2

    def parts_of(d):
        return d // (DP // 2), (d // 2) % M, d % 2

    def over_dp(x, f):
        return lax.ppermute(x, "dp", [(i, f(i)) for i in range(DP)])

    def core_flip(x):
        return over_dp(x, lambda i: i ^ 1)

    def top_flip(x):
        return over_dp(x, lambda i: (i + DP // 2) % DP)

    def mid_from(x, k):
        def dest(i):
            a, m, c = parts_of(i)
            return a * (DP // 2) + ((m - k) % M) * 2 + c

        return over_dp(x, dest)

    def row_from(x, k):
        return lax.ppermute(
            x, "tensor", [((t // R) * R + (t % R + k) % R, t) for t in range(T)]
        )

    def half_swap(x):
        return lax.ppermute(x, "tensor", [(t, (t + R) % T) for t in range(T)])

    def reshard(x):
        pairs = []
        for d in range(DP):
            for t in range(T):
                j, c, h, r = d // 2, d % 2, t // R, t % R
                pairs.append((d * T + t, (2 * j + h) * T + c * R + r))
        return lax.ppermute(x, ("dp", "tensor"), pairs)

    def gather_heads(x):
        out = []
        for k in range(R):
            y = x if k == 0 else row_from(x, k)
            out += [y, core_flip(y)]
        return out

    def scatter_heads(pieces):
        out = []
        for k in range(R):
            mine, theirs = pieces[2 * k], core_flip(pieces[2 * k + 1])
            if k == 0:
                out += [mine, theirs]
            else:
                both = (mine.astype(F32) + theirs.astype(F32)).astype(BF16)
                out.append(row_from(both, R - k))
        return out

    def on_device(
        tokens, qkv_weight, output_projection_weight, gate_up_weight, down_projection_weight,
        attention_gain, feedforward_gain, window_lengths, key_mask, cotangent,
    ):
        n, _, d = tokens.shape
        length = key_mask.shape[0]
        me_d, me_t = lax.axis_index("dp"), lax.axis_index("tensor")
        core, h, r = me_d % 2, me_t // R, me_t % R
        us = down_projection_weight.shape[0] // DP
        gain_one, gain_two = attention_gain[None], feedforward_gain[None]

        x = reshard(tokens[:, 0])
        wq_own = qkv_weight.transpose(1, 0, 2)
        f = wq_own.shape[2]
        flat = wq_own.reshape(3 * d, f)
        wq_far = lax.all_gather(
            half_swap(lax.dynamic_slice_in_dim(flat, me_d * (3 * d // DP), 3 * d // DP, 0)),
            "dp", axis=0, tiled=True,
        ).reshape(3, d, f)
        fo = output_projection_weight.shape[0]
        wo_far = lax.all_gather(
            half_swap(
                lax.dynamic_slice_in_dim(output_projection_weight, me_d * (fo // DP), fo // DP, 0)
            ),
            "dp", axis=0, tiled=True,
        )
        wq = jnp.where(core == 0, wq_own, wq_far)
        wo = jnp.where(core == 0, output_projection_weight, wo_far)

        positions = jnp.arange(length, dtype=jnp.int32)
        valid = (positions < window_lengths[0]) & (key_mask[:, 0] == 1)
        bias_own = jnp.where(valid, 0.0, MASKED).astype(F32)
        bias = jnp.where(core == h, bias_own, core_flip(bias_own))
        order = jnp.stack(
            [((core + dc) % 2) * R + (r + dr) % R for dr in range(R) for dc in (0, 1)]
        )
        bias = jnp.take(bias.reshape(T, n), order, axis=0).reshape(length)
        bias = jnp.concatenate(
            [bias[None].astype(BF16), jnp.zeros((15, length), BF16)], axis=0
        )
        places = (order[:, None] * n + jnp.arange(n, dtype=jnp.int32)[None]).reshape(length)
        half = HEAD_DIM // 2
        frequencies = ROPE_BASE ** (-(jnp.arange(half, dtype=F32) * 2.0 / HEAD_DIM))
        angles = frequencies[:, None] * places.astype(F32)[None]
        cos, sin = jnp.cos(angles), jnp.sin(angles)

        normed_one = gather_heads(norm_call(x, gain_one))

        def unit_slices():
            gu = lax.dynamic_slice_in_dim(gate_up_weight, me_d * us, us, 2)
            dn = lax.dynamic_slice_in_dim(down_projection_weight, me_d * us, us, 0)
            return jnp.concatenate([gu.transpose(1, 2, 0), dn[None]], axis=0)

        slices, _ = lax.optimization_barrier((unit_slices(), normed_one[-1]))
        units = lax.all_gather(slices, "tensor", axis=0)
        weights = [units] + [mid_from(units, k) for k in range(1, M)]

        q, k, v = qkv_call(normed_one, wq, cos, sin)
        o, lse = attend_call(q, k, v, bias)
        arrived = scatter_heads(out_call(o, wo, 2 * R))
        middle, normed = middle_call(x, gain_two, arrived)

        cot = reshard(cotangent[:, 0])

        def gather_units(y):
            z = top_flip(y)
            return [y, core_flip(y), z, core_flip(z)]

        cots = gather_units(cot)
        xs = gather_units(normed)
        near = ffn_call(jnp.concatenate(xs[:2]), jnp.concatenate(cots[:2]), weights)
        far = ffn_call(jnp.concatenate(xs[2:]), jnp.concatenate(cots[2:]), weights)

        def scatter_units(i):
            def both(y):
                return y[:n], core_flip(y[n:])

            mine, theirs = both(far[i])
            crossed = top_flip((mine.astype(F32) + theirs.astype(F32)).astype(BF16))
            return [*both(near[i]), crossed]

        dx_parts = scatter_units(4)
        middle_grad, middle_low, gain_two_part = back_call(
            "middle_grad", cot, middle, gain_two, dx_parts, 1
        )

        def weight_grads(m):
            cat = [jnp.concatenate(z) for z in (xs[:2], xs[2:], cots[:2], cots[2:])]
            return ffn_weight_call(
                cat[:2], cat[2:], *[[near[i], far[i]] for i in range(3)], m, T, us
            )

        grads = None
        for m in range(M - 1, -1, -1):
            got = weight_grads(m)
            if m:
                got = [mid_from(g, M - m) for g in got]
            got = [g.astype(F32) for g in got]
            grads = got if grads is None else [a + b for a, b in zip(grads, got)]
        dn_grad, gu_grad = [
            lax.all_gather(
                lax.psum_scatter(g.astype(BF16), "tensor", scatter_dimension=0, tiled=False),
                "dp", axis=0,
            )
            for g in grads
        ]
        down_grad = dn_grad.reshape(DP * us, d).astype(F32)
        gate_up_grad = gu_grad.transpose(2, 1, 0, 3).reshape(d, 2, DP * us).astype(F32)

        output = reshard(output_call(middle, scatter_units(3)))[:, None]

        lows = gather_heads(middle_low)
        g, wo_grad = heads_grad_call(o, wo, lows)
        dq, dk, dv = attend_back_call(q, k, v, bias, o, lse, g, cos, sin)
        dx_pieces, wq_grad = qkv_back_call(wq, dq, dk, dv, normed_one)
        arrived = scatter_heads(dx_pieces)
        tokens_low, gain_one_part = back_call(
            "tokens_grad", middle_grad, x, gain_one, arrived, 0
        )
        tokens_grad = reshard(tokens_low)[:, None]

        same_core = [[i for i in range(DP) if i % 2 == c] for c in (0, 1)]

        def reduce_heads(g):
            part = lax.psum_scatter(
                g, "dp", scatter_dimension=0, tiled=True, axis_index_groups=same_core
            )
            pairs = [
                ((2 * j + 1) * T + t, 2 * j * T + (t + R) % T)
                for j in range(DP // 2)
                for t in range(T)
            ]
            part = part.astype(F32) + lax.ppermute(part, ("dp", "tensor"), pairs).astype(F32)
            part = part.astype(BF16)
            part = jnp.where(core == 0, part, core_flip(part))
            return lax.all_gather(
                part, "dp", axis=0, tiled=True, axis_index_groups=same_core
            ).astype(F32)

        qkv_grad = reduce_heads(wq_grad.reshape(3 * d, f)).reshape(3, d, f).transpose(1, 0, 2)
        out_grad = reduce_heads(wo_grad)
        gains = lax.psum(
            jnp.concatenate([gain_one_part, gain_two_part], axis=0), ("dp", "tensor")
        )
        return (
            output, tokens_grad, qkv_grad, out_grad, gate_up_grad, down_grad, gains[0], gains[1]
        )

    return on_device


def solution(mesh):
    return jax.shard_map(
        build(mesh.shape["dp"], mesh.shape["tensor"]),
        mesh=mesh,
        in_specs=(
            P("tensor", "dp", None),
            P(None, None, "tensor"),
            P("tensor", None),
            P(None, None, "tensor"),
            P("tensor", None),
            P(),
            P(),
            P("dp"),
            P(None, "dp"),
            P("tensor", "dp", None),
        ),
        out_specs=(
            P("tensor", "dp", None),
            P("tensor", "dp", None),
            P(None, None, "tensor"),
            P("tensor", None),
            P(None, None, "tensor"),
            P("tensor", None),
            P(),
            P(),
        ),
        check_vma=False,
    )
```

time: 1170 us -> 700 us (0.60)
  matrix products: 345 us -> 0 us
  waiting for transfers between devices: 591 us -> 287 us
  Pallas kernels: 0 us -> 191 us
  other arithmetic: 129 us -> 32 us
  starting transfers between devices: 0.58 us -> 67 us
  blocking collectives: 42.9 us -> 59.9 us
    dot_general x40 -> x0, matrix products: 345 us -> none  [the longest x4 62.7 us: attend_back(): jnp.einsum('qshe,kshe->shqk', grad_block, values_heads, preferred_element...]
    ppermute x0 -> x38, waiting for transfers between devices: none -> 271 us  [the longest x26 138 us: over_dp(): return lax.ppermute(x, 'dp', [(i, f(i)) for i in range(DP)])]
    all_gather x4 -> x5, waiting for transfers between devices: 264 us -> 4.11 us  [the longest x1 4.1 us: on_device(): units = lax.all_gather(slices, 'tensor', axis=0)]
    reduce_scatter x4, waiting for transfers between devices: 222 us -> 9.8 us  [the longest x2 9.76 us: on_device(): lax.psum_scatter(g.astype(BF16), 'tensor', scatter_dimension=0, tiled=False)]
    pallas_call x0 -> x15, Pallas kernels: none -> 191 us  [the longest x1 47.1 us: attend_back_call(): call(functools.partial(attend_back_kernel, sub=min(256, S)), 'attend_back...]
    psum x1 -> x0, waiting for transfers between devices: 104 us -> none  [on_device(): lax.psum(gate_up_grad.astype(jnp.bfloat16), 'dp').astype(jnp.float32)]
    ppermute x0 -> x38, starting transfers between devices: none -> 66.4 us  [the longest x26 45.4 us: over_dp(): return lax.ppermute(x, 'dp', [(i, f(i)) for i in range(DP)])]
    convert_element_type x10 -> x11, other arithmetic: 79.3 us -> 22.2 us  [the longest x1 6.6 us: on_device(): gu_grad.transpose(2, 1, 0, 3).reshape(d, 2, DP * us).astype(F32)]
  transfers between devices with their start and end apart: 9 -> 47, of which waited for: 9 -> 19; matrix products, arithmetic and copies ran while one was open for 11% -> 5% of each run, Pallas kernels for 0% -> 24%
where the time goes in v1:
time: 700 us; the launch traced here: 696 us
  waiting for transfers between devices  287 us (41%)
  Pallas kernels  191 us (27%)
  starting transfers between devices  67 us (10%)
  blocking collectives  59.9 us (9%)
  local copies, waits for them, and re-layouts  44.5 us (6%)
  other arithmetic  32 us (5%)
  between operations  15.2 us (2%)
    ppermute x26, waiting for transfers between devices, over_dp(): return lax.ppermute(x, 'dp', [(i, f(i)) for i in range(DP)])  138 us
    ppermute x4, waiting for transfers between devices, row_from(): lax.ppermute(x, 'tensor', [(t // R * R + (t % R + k) % R, t) for t in ran...  59.2 us
    pallas_call x1, Pallas kernels, attend_back_call(): call(functools.partial(attend_back_kernel, sub=min(256, S)), 'attend_back...  47.1 us
    ppermute x26, starting transfers between devices, over_dp(): return lax.ppermute(x, 'dp', [(i, f(i)) for i in range(DP)])  45.4 us
    ppermute x2, waiting for transfers between devices, reduce_heads(): lax.ppermute(part, ('dp', 'tensor'), pairs).astype(F32)  42.2 us
    pallas_call x2, Pallas kernels, ffn_call(): call(functools.partial(ffn_kernel, groups), 'feed_forward', (shape((n, un...  38.9 us
    psum x1, blocking collectives, on_device(): lax.psum(jnp.concatenate([gain_one_part, gain_two_part], axis=0), ('dp',...  38.5 us
    ppermute x2, waiting for transfers between devices, half_swap(): return lax.ppermute(x, 'tensor', [(t, (t + R) % T) for t in range(T)])  31.6 us
  transfers between devices with their start and end apart: 47, of which 19 were waited for; matrix products, arithmetic and copies ran while one was open for 5% of the time, Pallas kernels for 24%

profile of v1, /device:TPU:0, one launch (start us, length us, event | category | flops | bytes accessed | tf_op | source)
XLA Modules:
  0.0 696.0 jit_solution(2376838721380947114)
XLA Ops:
  7.2 2.0 collective-permute-start
  10.2 4.2 collective-permute-start.1
  14.4 31.6 %collective-permute-done.1 = bf16[384,256]{1,0:T(8,128)(2,1)S(1)} collective-permute-done((bf16[384,256]{1,0:T(8,128)(2,1)S(1)}, bf16[384,256]{1,0:T(8,128)(2,1)S(1)}, u32[]{:S(2)}, u32[]{:S(2)}) %collective-permute-start.1) | collective-permute-done | bytes 196640 | tf_op jit(solution)/shard_map/ppermute | solution.py:535
  47.7 3.8 norm_tokens.1.refs_0_
  53.4 3.1 collective-permute-start.6
  56.7 20.4 %collective-permute-done.3.refs_2_ = bf16[512,1024]{1,0:T(8,128)(2,1)} collective-permute-done((bf16[512,1024]{1,0:T(8,128)(2,1)}, bf16[512,1024]{1,0:T(8,128)(2,1)}, u32[]{:S(2)}, u32[]{:S(2)}) %collective-permute-start.3) | collective-permute-done | bytes 1048608 | tf_op jit(solution)/shard_map/ppermute | solution.py:530
  77.1 1.4 constant_dynamic-slice_fusion
  80.0 1.8 multiply_sine_fusion
  83.8 10.1 %all_gather.25 = bf16[256,1024]{1,0:T(8,128)(2,1)S(1)} all-gather(bf16[32,1024]{1,0:T(8,128)(2,1)S(1)} %collective-permute-done.6), channel_id=1, replica_groups=mesh['dp'=8,'tensor'=4] {'dp'}, dimensions={0}, use_global_device_ids=true | all-gather | bytes 589824 | tf_op jit(solution)/shard_map/all_gather | solution.py:583
  94.8 1.3 bitcast_select_fusion.w_ref
  96.1 7.5 %project_heads.1 = (bf16[256,2048]{1,0:T(8,128)(2,1)}, bf16[256,2048]{1,0:T(8,128)(2,1)}, bf16[256,2048]{1,0:T(8,128)(2,1)}) custom-call(f32[32,2048]{1,0:T(8,128)} %get-tuple-element.113.c_ref.ck_ref, f32[32,2048]{1,0:T(8,128)} %get-tuple-element.112.s_ref.sk_ref, bf16[3,1024,256]{2,1,0:T(8,128)(2,1)} %bitcast_select_fusion.w_ref, ...), custom_call_target="tpu_custom_call" | custom-call | flops 3221225472 | bytes 8912896 | tf_op jit(solution)/shard_map/project_heads/pallas_call | solution.py:187
  103.7 27.0 %attend.1 = (bf16[256,2048]{1,0:T(8,128)(2,1)}, f32[4,8,2048]{2,1,0:T(8,128)}) custom-call(bf16[256,2048]{1,0:T(8,128)(2,1)} %get-tuple-element.49.q_ref, bf16[256,2048]{1,0:T(8,128)(2,1)} %get-tuple-element.50.k_ref, bf16[256,2048]{1,0:T(8,128)(2,1)} %get-tuple-element.51.v_ref, bf16[16,2048]{1,0:T(8,128)(2,1)} %concatenate.54.b_ref), custom_call_target="tpu_custom_call" | custom-call | flops 17179869184 | bytes 5242880 | tf_op jit(solution)/shard_map/attend/pallas_call | solution.py:245
  130.7 3.9 output_projection.1
  134.6 1.8 collective-permute-start.8
  136.3 2.4 collective-permute-start.11
  139.3 2.7 add_convert_fusion.5
  142.0 2.1 collective-permute-start.9
  144.1 4.1 all-gather.15.cloned.1.call-done
  148.2 1.5 collective-permute-start.13
  149.7 1.7 collective-permute-start.17
  151.4 28.3 %collective-permute-done.9.refs_2_ = bf16[512,1024]{1,0:T(8,128)(2,1)S(1)} collective-permute-done((bf16[512,1024]{1,0:T(8,128)(2,1)}, bf16[512,1024]{1,0:T(8,128)(2,1)S(1)}, u32[]{:S(2)}, u32[]{:S(2)}) %collective-permute-start.9) | collective-permute-done | bytes 1048608 | tf_op jit(solution)/shard_map/ppermute | solution.py:530
  180.7 4.5 middle_norm.1
  185.2 1.5 collective-permute-start.15
  187.2 23.3 %collective-permute-done.15 = bf16[512,1024]{1,0:T(8,128)(2,1)S(1)} collective-permute-done((bf16[512,1024]{1,0:T(8,128)(2,1)}, bf16[512,1024]{1,0:T(8,128)(2,1)S(1)}, u32[]{:S(2)}, u32[]{:S(2)}) %collective-permute-start.15) | collective-permute-done | bytes 1048608 | tf_op jit(solution)/shard_map/ppermute | solution.py:514
  210.8 1.5 copy-done.14
  215.1 2.6 collective-permute-done.13.refs_5_.refs_6_.refs_7_
  217.8 19.5 %feed_forward.3 = (bf16[1024,1024]{1,0:T(8,128)(2,1)}, bf16[1024,1024]{1,0:T(8,128)(2,1)}, bf16[1024,1024]{1,0:T(8,128)(2,1)}, bf16[1024,1024]{1,0:T(8,128)(2,1)}, bf16[1024,1024]{1,0:T(8,128)(2,1)}) custom-call(bf16[1024,1024]{1,0:T(8,128)(2,1)} %copy-done.21, bf16[1024,1024]{1,0:T(8,128)(2,1)} %copy-done.22, bf16[4,3,128,1024]{3,2,1,0:T(8,128)(2,1)} %bitcast.65, ...), custom_call_target="tpu_custom_call" | custom-call | flops 12884901888 | bytes 20971520 | tf_op jit(solution)/shard_map/feed_forward/pallas_call | solution.py:456
  237.2 1.3 slice.37
  238.6 19.5 %feed_forward.2 = (bf16[1024,1024]{1,0:T(8,128)(2,1)}, bf16[1024,1024]{1,0:T(8,128)(2,1)}, bf16[1024,1024]{1,0:T(8,128)(2,1)}, bf16[1024,1024]{1,0:T(8,128)(2,1)}, bf16[1024,1024]{1,0:T(8,128)(2,1)}) custom-call(bf16[1024,1024]{1,0:T(8,128)(2,1)} %copy-done.23, bf16[1024,1024]{1,0:T(8,128)(2,1)} %copy-done.24, bf16[4,3,128,1024]{3,2,1,0:T(8,128)(2,1)} %bitcast.68, ...), custom_call_target="tpu_custom_call" | custom-call | flops 12884901888 | bytes 20971520 | tf_op jit(solution)/shard_map/feed_forward/pallas_call | solution.py:456
  258.1 2.8 fusion.4
  261.8 1.6 collective-permute-start.24
  263.7 23.3 %collective-permute-done.24.refs_2_ = bf16[512,1024]{1,0:T(8,128)(2,1)S(1)} collective-permute-done((bf16[512,1024]{1,0:T(8,128)(2,1)S(1)}, bf16[512,1024]{1,0:T(8,128)(2,1)S(1)}, u32[]{:S(2)}, u32[]{:S(2)}) %collective-permute-start.24) | collective-permute-done | bytes 1048608 | tf_op jit(solution)/shard_map/ppermute | solution.py:514
  287.9 5.8 middle_grad.1
  294.5 12.9 %feed_forward_weights.2 = (bf16[4,128,1024]{2,1,0:T(8,128)(2,1)}, bf16[4,2,1024,128]{3,2,1,0:T(8,128)(2,1)}) custom-call(bf16[1024,1024]{1,0:T(8,128)(2,1)} %copy-done.23, bf16[1024,1024]{1,0:T(8,128)(2,1)} %copy-done.21, bf16[1024,1024]{1,0:T(8,128)(2,1)} %copy-done.24, bf16[1024,1024]{1,0:T(8,128)(2,1)} %copy-done.22, ...), custom_call_target="tpu_custom_call" | custom-call | flops 6442450944 | bytes 17825792 | tf_op jit(solution)/shard_map/feed_forward_weights/pallas_call | solution.py:491
  307.5 1.6 collective-permute-start.37
  309.1 9.2 %collective-permute-done.26.refs_2_ = bf16[512,1024]{1,0:T(8,128)(2,1)S(1)} collective-permute-done((bf16[512,1024]{1,0:T(8,128)(2,1)}, bf16[512,1024]{1,0:T(8,128)(2,1)S(1)}, u32[]{:S(2)}, u32[]{:S(2)}) %collective-permute-start.26) | collective-permute-done | bytes 1048608 | tf_op jit(solution)/shard_map/ppermute | solution.py:530
  318.3 13.1 %feed_forward_weights.3 = (bf16[4,128,1024]{2,1,0:T(8,128)(2,1)}, bf16[4,2,1024,128]{3,2,1,0:T(8,128)(2,1)}) custom-call(bf16[1024,1024]{1,0:T(8,128)(2,1)} %copy-done.23, bf16[1024,1024]{1,0:T(8,128)(2,1)} %copy-done.21, bf16[1024,1024]{1,0:T(8,128)(2,1)} %copy-done.24, bf16[1024,1024]{1,0:T(8,128)(2,1)} %copy-done.22, ...), custom_call_target="tpu_custom_call" | custom-call | flops 6442450944 | bytes 17825792 | tf_op jit(solution)/shard_map/feed_forward_weights/pallas_call | solution.py:491
  331.6 2.6 add_convert_fusion.1
  334.4 5.9 heads_grad.1
  340.3 47.1 %attend_back.1 = (bf16[256,2048]{1,0:T(8,128)(2,1)}, bf16[256,2048]{1,0:T(8,128)(2,1)}, bf16[256,2048]{1,0:T(8,128)(2,1)}) custom-call(bf16[256,2048]{1,0:T(8,128)(2,1)} %get-tuple-element.49.q_ref, bf16[256,2048]{1,0:T(8,128)(2,1)} %get-tuple-element.50.k_ref, bf16[256,2048]{1,0:T(8,128)(2,1)} %get-tuple-element.51.v_ref, ...), custom_call_target="tpu_custom_call" | custom-call | flops 42949672960 | bytes 10485760 | tf_op jit(solution)/shard_map/attend_back/pallas_call | solution.py:317
  387.4 11.5 %qkv_back.1 = (bf16[512,1024]{1,0:T(8,128)(2,1)}, bf16[512,1024]{1,0:T(8,128)(2,1)}, bf16[512,1024]{1,0:T(8,128)(2,1)}, bf16[512,1024]{1,0:T(8,128)(2,1)}, bf16[3,1024,256]{2,1,0:T(8,128)(2,1)}) custom-call(bf16[3,1024,256]{2,1,0:T(8,128)(2,1)} %bitcast_select_fusion.w_ref, bf16[256,2048]{1,0:T(8,128)(2,1)} %get-tuple-element.68.q_ref, ...), custom_call_target="tpu_custom_call" | custom-call | flops 6442450944 | bytes 14680064 | tf_op jit(solution)/shard_map/qkv_back/pallas_call | solution.py:403
  399.0 1.5 collective-permute-start.36
  400.5 58.6 %collective-permute-done.36 = bf16[4,2,1024,128]{3,2,1,0:T(8,128)(2,1)S(1)} collective-permute-done((bf16[4,2,1024,128]{3,2,1,0:T(8,128)(2,1)}, bf16[4,2,1024,128]{3,2,1,0:T(8,128)(2,1)S(1)}, u32[]{:S(2)}, u32[]{:S(2)}) %collective-permute-start.36) | collective-permute-done | bytes 2097184 | tf_op jit(solution)/shard_map/ppermute | solution.py:514
  459.1 1.9 add_convert_fusion
  463.7 31.8 %collective-permute-done.32 = bf16[768,256]{1,0:T(8,128)(2,1)S(1)} collective-permute-done((bf16[768,256]{1,0:T(8,128)(2,1)}, bf16[768,256]{1,0:T(8,128)(2,1)S(1)}, u32[]{:S(2)}, u32[]{:S(2)}) %collective-permute-start.32) | collective-permute-done | bytes 393248 | tf_op jit(solution)/shard_map/ppermute | solution.py:695
  496.7 1.7 collective-permute-done.33
  499.5 9.7 %reduce-scatter.9.cloned.1.call-done = bf16[1,2,1024,128]{3,2,1,0:T(8,128)(2,1)} async-done(((bf16[4,2,1024,128]{3,2,1,0:T(8,128)(2,1)}), bf16[1,2,1024,128]{3,2,1,0:T(8,128)(2,1)}) %reduce-scatter.9.cloned.1.call-update) | async-done | bytes 524304 | tf_op jit(solution)/shard_map/reduce_scatter | solution.py:664
  509.5 1.4 copy-done.7
  512.5 1.5 collective-permute-start.20
  514.7 27.6 %collective-permute-done.20.refs_2_ = bf16[512,1024]{1,0:T(8,128)(2,1)S(1)} collective-permute-done((bf16[512,1024]{1,0:T(8,128)(2,1)S(1)}, bf16[512,1024]{1,0:T(8,128)(2,1)S(1)}, u32[]{:S(2)}, u32[]{:S(2)}) %collective-permute-start.20) | collective-permute-done | bytes 1048608 | tf_op jit(solution)/shard_map/ppermute | solution.py:514
  543.3 3.6 output_sum.1
  546.9 1.9 collective-permute-start.21
  548.7 6.2 collective-permute-start.28
  556.7 10.4 %collective-permute-done.34 = bf16[64,1024]{1,0:T(8,128)(2,1)S(1)} collective-permute-done((bf16[64,1024]{1,0:T(8,128)(2,1)}, bf16[64,1024]{1,0:T(8,128)(2,1)S(1)}, u32[]{:S(2)}, u32[]{:S(2)}) %collective-permute-start.34) | collective-permute-done | bytes 131104 | tf_op jit(solution)/shard_map/ppermute | solution.py:695
  568.1 23.7 %collective-permute-start.35 = (bf16[64,1024]{1,0:T(8,128)(2,1)S(1)}, bf16[64,1024]{1,0:T(8,128)(2,1)S(1)}, u32[]{:S(2)}, u32[]{:S(2)}) collective-permute-start(bf16[64,1024]{1,0:T(8,128)(2,1)S(1)} %add_convert_fusion.7), channel_id=1, source_target_pairs={{0,4},{4,0},{8,12},{12,8},{16,20},{20,16},{24,28},{28,24},{1,5},{5... | collective-permute-start | bytes 393224 | tf_op jit(solution)/shard_map/ppermute | solution.py:514
  594.0 5.2 tokens_grad.1
  599.2 2.0 collective-permute-start.31
  601.2 11.3 %all_gather.29 = bf16[256,1024]{1,0:T(8,128)(2,1)S(1)} all-gather(bf16[64,1024]{1,0:T(8,128)(2,1)S(1)} %broadcast_select_fusion.2), channel_id=1, replica_groups={{0,8,16,24},{4,12,20,28},{1,9,17,25},{5,13,21,29},{2,10,18,26},{6,14,22..., dimensions={0}, use_global_device_ids=true | all-gather | bytes 655360 | tf_op jit(solution)/shard_map/all_gather | solution.py:698
  613.6 38.5 %psum.7 = f32[2,1024]{1,0:T(2,128)S(1)} all-reduce(f32[2,1024]{1,0:T(2,128)S(1)} %pad_maximum_fusion.1), channel_id=1, replica_groups=mesh['dp'=8,'tensor'=4] {'dp','tensor'}, use_global_device_ids=true, to_apply=%region_4.5 | all-reduce | flops 2048 | bytes 16384 | tf_op jit(solution)/shard_map/psum | solution.py:704
  652.8 4.1 bitcast_convert_fusion
  656.8 3.7 convert_bitcast_fusion
  660.6 6.2 copy.24
  666.7 6.6 convert_element_type.151
  673.3 13.3 %copy.25 = f32[1024,2,1024]{2,1,0:T(2,128)} copy(f32[1024,2,1024]{0,2,1:T(8,128)} %bitcast.48) | data formatting | bytes 16777216
  (177 shorter events, 34.5 us)
Async XLA Ops:
  7.2 71.9 %copy-start = (bf16[1024,1024]{1,0:T(8,128)(2,1)S(1)}, bf16[1024,1024]{1,0:T(8,128)(2,1)}, u32[]{:S(2)}) copy-start(bf16[1024,1024]{1,0:T(8,128)(2,1)} %param.14) | copy-start | bytes 6291460
  7.2 45.0 %copy-start.26 = (s32[2048,1]{0,1:T(1,128)S(1)}, s32[2048,1]{0,1:T(1,128)}, u32[]{:S(2)}) copy-start(s32[2048,1]{0,1:T(1,128)} %param.18) | copy-start | bytes 24580
  7.2 87.6 %all-gather.7.cloned.1.call-start = ((), (), s32[]{:S(2)}) async-start(), calls=%async_computation.4 | async-start | bytes 1769472 | tf_op jit(solution)/shard_map/all_gather | solution.py:578
  7.2 39.5 %collective-permute-start = (bf16[512,1024]{1,0:T(8,128)(2,1)}, bf16[512,1024]{1,0:T(8,128)(2,1)S(1)}, u32[]{:S(2)}, u32[]{:S(2)}) collective-permute-start(bf16[512,1024]{1,0:T(8,128)(2,1)} %bitcast.71), channel_id=1, source_target_pairs={{0,0},{1,1},{2,4},{3,5},{4,2},{5,3},{6,6},{7,7},{8,8},{9,9},{10,12... | collective-permute-start | bytes 3145736 | tf_op jit(solution)/shard_map/ppermute | solution.py:543
  10.2 35.8 %collective-permute-start.1 = (bf16[384,256]{1,0:T(8,128)(2,1)S(1)}, bf16[384,256]{1,0:T(8,128)(2,1)S(1)}, u32[]{:S(2)}, u32[]{:S(2)}) collective-permute-start(bf16[384,256]{1,0:T(8,128)(2,1)S(1)} %constant_dynamic-slice_fusion.2), channel_id=1, source_target_pairs={{0,2},{1,3},{2,0},{3,1},{4,6},{5,7},{6,4},{7,5},{8,10},{9,11},{10,... | collective-permute-start | bytes 589832 | tf_op jit(solution)/shard_map/ppermute | solution.py:535
  46.7 101.5 %all-gather.15.cloned.1.call-start = ((), (), s32[]{:S(2)}) async-start(), calls=%async_computation.12 | async-start | bytes 3932160 | tf_op jit(solution)/shard_map/all_gather | solution.py:617
  51.5 25.6 %collective-permute-start.3 = (bf16[512,1024]{1,0:T(8,128)(2,1)}, bf16[512,1024]{1,0:T(8,128)(2,1)}, u32[]{:S(2)}, u32[]{:S(2)}) collective-permute-start(bf16[512,1024]{1,0:T(8,128)(2,1)} %norm_tokens.1.refs_0_), channel_id=1, source_target_pairs={{1,0},{0,1},{3,2},{2,3},{5,4},{4,5},{7,6},{6,7},{9,8},{8,9},{11,10... | collective-permute-start | bytes 3145736 | tf_op jit(solution)/shard_map/ppermute | solution.py:530
  52.2 30.2 %collective-permute-start.5 = (bf16[2048]{0:T(1024)(128)(2,1)S(1)}, bf16[2048]{0:T(1024)(128)(2,1)S(1)}, u32[]{:S(2)}, u32[]{:S(2)}) collective-permute-start(bf16[2048]{0:T(1024)(128)(2,1)S(1)} %fusion.1), channel_id=1, source_target_pairs={{0,4},{4,0},{8,12},{12,8},{16,20},{20,16},{24,28},{28,24},{1,5},{5... | collective-permute-start | bytes 12296 | tf_op jit(solution)/shard_map/ppermute | solution.py:514
  53.4 30.4 %collective-permute-start.6 = (bf16[32,1024]{1,0:T(8,128)(2,1)S(1)}, bf16[32,1024]{1,0:T(8,128)(2,1)S(1)}, u32[]{:S(2)}, u32[]{:S(2)}) collective-permute-start(bf16[32,1024]{1,0:T(8,128)(2,1)S(1)} %constant_dynamic-slice_fusion.1), channel_id=1, source_target_pairs={{0,2},{1,3},{2,0},{3,1},{4,6},{5,7},{6,4},{7,5},{8,10},{9,11},{10,... | collective-permute-start | bytes 196616 | tf_op jit(solution)/shard_map/ppermute | solution.py:535
  77.1 4.7 collective-permute-start.4
  79.0 14.9 %copy-start.20 = (bf16[256,1024]{1,0:T(8,128)(2,1)S(1)}, bf16[256,1024]{1,0:T(8,128)(2,1)}, u32[]{:S(2)}) copy-start(bf16[256,1024]{1,0:T(8,128)(2,1)} %param.12) | copy-start | bytes 1572868
  80.0 14.8 %copy-start.8 = (bf16[1024,3,256]{2,0,1:T(8,128)(2,1)S(1)}, bf16[1024,3,256]{2,0,1:T(8,128)(2,1)}, u32[]{:S(2)}) copy-start(bf16[1024,3,256]{2,0,1:T(8,128)(2,1)} %param.11) | copy-start | bytes 4718596
  81.8 379.8 %reduce-scatter.11.cloned.1.call-start = ((), (), s32[]{:S(2)}) async-start(), calls=%async_computation.10 | async-start | bytes 1310720 | tf_op jit(solution)/shard_map/reduce_scatter | solution.py:664
  81.9 14.2 %collective-permute-start.2 = (bf16[512,1024]{1,0:T(8,128)(2,1)}, bf16[512,1024]{1,0:T(8,128)(2,1)}, u32[]{:S(2)}, u32[]{:S(2)}) collective-permute-start(bf16[512,1024]{1,0:T(8,128)(2,1)} %norm_tokens.1.refs_0_), channel_id=1, source_target_pairs={{0,4},{4,0},{8,12},{12,8},{16,20},{20,16},{24,28},{28,24},{1,5},{5... | collective-permute-start | bytes 3145736 | tf_op jit(solution)/shard_map/ppermute | solution.py:514
  134.6 4.7 collective-permute-start.8
  136.3 13.4 %collective-permute-start.11 = (bf16[512,1024]{1,0:T(8,128)(2,1)}, bf16[512,1024]{1,0:T(8,128)(2,1)S(1)}, u32[]{:S(2)}, u32[]{:S(2)}) collective-permute-start(bf16[512,1024]{1,0:T(8,128)(2,1)} %bitcast.16), channel_id=1, source_target_pairs={{0,0},{1,1},{2,4},{3,5},{4,2},{5,3},{6,6},{7,7},{8,8},{9,9},{10,12... | collective-permute-start | bytes 3145736 | tf_op jit(solution)/shard_map/ppermute | solution.py:543
  138.7 12.7 %collective-permute-start.7 = (bf16[512,1024]{1,0:T(8,128)(2,1)}, bf16[512,1024]{1,0:T(8,128)(2,1)S(1)}, u32[]{:S(2)}, u32[]{:S(2)}) collective-permute-start(bf16[512,1024]{1,0:T(8,128)(2,1)} %get-tuple-element.54), channel_id=1, source_target_pairs={{0,4},{4,0},{8,12},{12,8},{16,20},{20,16},{24,28},{28,24},{1,5},{5... | collective-permute-start | bytes 3145736 | tf_op jit(solution)/shard_map/ppermute | solution.py:514
  142.0 37.7 %collective-permute-start.9 = (bf16[512,1024]{1,0:T(8,128)(2,1)}, bf16[512,1024]{1,0:T(8,128)(2,1)S(1)}, u32[]{:S(2)}, u32[]{:S(2)}) collective-permute-start(bf16[512,1024]{1,0:T(8,128)(2,1)} %add_convert_fusion.5), channel_id=1, source_target_pairs={{1,0},{0,1},{3,2},{2,3},{5,4},{4,5},{7,6},{6,7},{9,8},{8,9},{11,10... | collective-permute-start | bytes 3145736 | tf_op jit(solution)/shard_map/ppermute | solution.py:530
  148.2 69.6 %collective-permute-start.13 = (bf16[4,3,128,1024]{3,2,1,0:T(8,128)(2,1)}, bf16[4,3,128,1024]{3,2,1,0:T(8,128)(2,1)}, u32[]{:S(2)}, u32[]{:S(2)}) collective-permute-start(bf16[4,3,128,1024]{3,2,1,0:T(8,128)(2,1)} %bitcast.64), channel_id=1, source_target_pairs={{0,8},{4,12},{8,0},{12,4},{16,24},{20,28},{24,16},{28,20},{1,9},{5... | collective-permute-start | bytes 9437192 | tf_op jit(solution)/shard_map/ppermute | solution.py:514
  149.7 60.8 %copy-start.3 = (bf16[512,1024]{1,0:T(8,128)(2,1)}, bf16[512,1024]{1,0:T(8,128)(2,1)S(1)}, u32[]{:S(2)}) copy-start(bf16[512,1024]{1,0:T(8,128)(2,1)S(1)} %collective-permute-done.11.base_ref) | copy-start | bytes 3145732
  149.7 37.0 %collective-permute-start.17 = (bf16[512,1024]{1,0:T(8,128)(2,1)S(1)}, bf16[512,1024]{1,0:T(8,128)(2,1)S(1)}, u32[]{:S(2)}, u32[]{:S(2)}) collective-permute-start(bf16[512,1024]{1,0:T(8,128)(2,1)S(1)} %collective-permute-done.11.base_ref), channel_id=1, source_target_pairs={{0,16},{4,20},{8,24},{12,28},{16,0},{20,4},{24,8},{28,12},{1,17},{... | collective-permute-start | bytes 3145736 | tf_op jit(solution)/shard_map/ppermute | solution.py:514
  151.4 28.3 %copy-start.10 = (bf16[512,1024]{1,0:T(8,128)(2,1)}, bf16[512,1024]{1,0:T(8,128)(2,1)S(1)}, u32[]{:S(2)}) copy-start(bf16[512,1024]{1,0:T(8,128)(2,1)S(1)} %collective-permute-done.7.refs_1_) | copy-start | bytes 3145732
  185.2 25.3 %collective-permute-start.15 = (bf16[512,1024]{1,0:T(8,128)(2,1)}, bf16[512,1024]{1,0:T(8,128)(2,1)S(1)}, u32[]{:S(2)}, u32[]{:S(2)}) collective-permute-start(bf16[512,1024]{1,0:T(8,128)(2,1)} %get-tuple-element.58), channel_id=1, source_target_pairs={{0,16},{4,20},{8,24},{12,28},{16,0},{20,4},{24,8},{28,12},{1,17},{... | collective-permute-start | bytes 3145736 | tf_op jit(solution)/shard_map/ppermute | solution.py:514
  186.7 24.0 %collective-permute-start.12 = (bf16[512,1024]{1,0:T(8,128)(2,1)S(1)}, bf16[512,1024]{1,0:T(8,128)(2,1)S(1)}, u32[]{:S(2)}, u32[]{:S(2)}) collective-permute-start(bf16[512,1024]{1,0:T(8,128)(2,1)S(1)} %collective-permute-done.11.base_ref), channel_id=1, source_target_pairs={{0,4},{4,0},{8,12},{12,8},{16,20},{20,16},{24,28},{28,24},{1,5},{5... | collective-permute-start | bytes 3145736 | tf_op jit(solution)/shard_map/ppermute | solution.py:514
  186.7 24.1 %collective-permute-start.18 = (bf16[512,1024]{1,0:T(8,128)(2,1)S(1)}, bf16[512,1024]{1,0:T(8,128)(2,1)S(1)}, u32[]{:S(2)}, u32[]{:S(2)}) collective-permute-start(bf16[512,1024]{1,0:T(8,128)(2,1)S(1)} %collective-permute-done.17), channel_id=1, source_target_pairs={{0,4},{4,0},{8,12},{12,8},{16,20},{20,16},{24,28},{28,24},{1,5},{5... | collective-permute-start | bytes 3145736 | tf_op jit(solution)/shard_map/ppermute | solution.py:514
  187.2 26.6 %collective-permute-start.10 = (bf16[512,1024]{1,0:T(8,128)(2,1)}, bf16[512,1024]{1,0:T(8,128)(2,1)S(1)}, u32[]{:S(2)}, u32[]{:S(2)}) collective-permute-start(bf16[512,1024]{1,0:T(8,128)(2,1)} %get-tuple-element.58), channel_id=1, source_target_pairs={{0,4},{4,0},{8,12},{12,8},{16,20},{20,16},{24,28},{28,24},{1,5},{5... | collective-permute-start | bytes 3145736 | tf_op jit(solution)/shard_map/ppermute | solution.py:514
  210.5 3.4 collective-permute-start.16
  238.5 22.9 %collective-permute-start.23 = (bf16[512,1024]{1,0:T(8,128)(2,1)S(1)}, bf16[512,1024]{1,0:T(8,128)(2,1)S(1)}, u32[]{:S(2)}, u32[]{:S(2)}) collective-permute-start(bf16[512,1024]{1,0:T(8,128)(2,1)S(1)} %slice.37), channel_id=1, source_target_pairs={{0,4},{4,0},{8,12},{12,8},{16,20},{20,16},{24,28},{28,24},{1,5},{5... | collective-permute-start | bytes 3145736 | tf_op jit(solution)/shard_map/ppermute | solution.py:514
  258.1 3.3 copy-start.6
  260.9 2.8 collective-permute-start.22
  261.8 25.2 %collective-permute-start.24 = (bf16[512,1024]{1,0:T(8,128)(2,1)S(1)}, bf16[512,1024]{1,0:T(8,128)(2,1)S(1)}, u32[]{:S(2)}, u32[]{:S(2)}) collective-permute-start(bf16[512,1024]{1,0:T(8,128)(2,1)S(1)} %add_convert_fusion.3), channel_id=1, source_target_pairs={{0,16},{4,20},{8,24},{12,28},{16,0},{20,4},{24,8},{28,12},{1,17},{... | collective-permute-start | bytes 3145736 | tf_op jit(solution)/shard_map/ppermute | solution.py:514
  263.7 23.3 %copy-start.16 = (bf16[512,1024]{1,0:T(8,128)(2,1)}, bf16[512,1024]{1,0:T(8,128)(2,1)S(1)}, u32[]{:S(2)}) copy-start(bf16[512,1024]{1,0:T(8,128)(2,1)S(1)} %collective-permute-done.22.refs_1_) | copy-start | bytes 3145732
  293.8 24.5 %collective-permute-start.26 = (bf16[512,1024]{1,0:T(8,128)(2,1)}, bf16[512,1024]{1,0:T(8,128)(2,1)S(1)}, u32[]{:S(2)}, u32[]{:S(2)}) collective-permute-start(bf16[512,1024]{1,0:T(8,128)(2,1)} %get-tuple-element.66.refs_0_), channel_id=1, source_target_pairs={{1,0},{0,1},{3,2},{2,3},{5,4},{4,5},{7,6},{6,7},{9,8},{8,9},{11,10... | collective-permute-start | bytes 3145736 | tf_op jit(solution)/shard_map/ppermute | solution.py:530
  294.5 14.6 %copy-start.30 = (bf16[512,1024]{1,0:T(8,128)(2,1)S(1)}, bf16[512,1024]{1,0:T(8,128)(2,1)}, u32[]{:S(2)}) copy-start(bf16[512,1024]{1,0:T(8,128)(2,1)} %get-tuple-element.66.refs_0_) | copy-start | bytes 3145732
  307.5 24.2 %collective-permute-start.37 = (bf16[4,128,1024]{2,1,0:T(8,128)(2,1)}, bf16[4,128,1024]{2,1,0:T(8,128)(2,1)S(1)}, u32[]{:S(2)}, u32[]{:S(2)}) collective-permute-start(bf16[4,128,1024]{2,1,0:T(8,128)(2,1)} %get-tuple-element.86), channel_id=1, source_target_pairs={{0,8},{4,12},{8,0},{12,4},{16,24},{20,28},{24,16},{28,20},{1,9},{5... | collective-permute-start | bytes 3145736 | tf_op jit(solution)/shard_map/ppermute | solution.py:514
  309.1 25.3 %collective-permute-start.25 = (bf16[512,1024]{1,0:T(8,128)(2,1)S(1)}, bf16[512,1024]{1,0:T(8,128)(2,1)}, u32[]{:S(2)}, u32[]{:S(2)}) collective-permute-start(bf16[512,1024]{1,0:T(8,128)(2,1)S(1)} %copy-done.30), channel_id=1, source_target_pairs={{0,4},{4,0},{8,12},{12,8},{16,20},{20,16},{24,28},{28,24},{1,5},{5... | collective-permute-start | bytes 3145736 | tf_op jit(solution)/shard_map/ppermute | solution.py:514
  318.3 13.1 %copy-start.31 = (bf16[512,1024]{1,0:T(8,128)(2,1)}, bf16[512,1024]{1,0:T(8,128)(2,1)S(1)}, u32[]{:S(2)}) copy-start(bf16[512,1024]{1,0:T(8,128)(2,1)S(1)} %collective-permute-done.26.refs_2_) | copy-start | bytes 3145732
  318.3 16.1 %collective-permute-start.27 = (bf16[512,1024]{1,0:T(8,128)(2,1)S(1)}, bf16[512,1024]{1,0:T(8,128)(2,1)}, u32[]{:S(2)}, u32[]{:S(2)}) collective-permute-start(bf16[512,1024]{1,0:T(8,128)(2,1)S(1)} %collective-permute-done.26.refs_2_), channel_id=1, source_target_pairs={{0,4},{4,0},{8,12},{12,8},{16,20},{20,16},{24,28},{28,24},{1,5},{5... | collective-permute-start | bytes 3145736 | tf_op jit(solution)/shard_map/ppermute | solution.py:514
  334.3 128.1 %reduce-scatter.5.cloned.1.call-start = ((), (), s32[]{:S(2)}) async-start(), calls=%async_computation.5 | async-start | bytes 1966080 | tf_op jit(solution)/shard_map/reduce_scatter | solution.py:687
  387.4 71.7 %copy-start.4 = (bf16[4,2,1024,128]{3,2,1,0:T(8,128)(2,1)S(1)}, bf16[4,2,1024,128]{3,2,1,0:T(8,128)(2,1)}, u32[]{:S(2)}) copy-start(bf16[4,2,1024,128]{3,2,1,0:T(8,128)(2,1)} %get-tuple-element.85) | copy-start | bytes 6291460
  399.0 110.3 %reduce-scatter.9.cloned.1.call-start = ((), (), s32[]{:S(2)}) async-start(), calls=%async_computation.8 | async-start | bytes 2621440 | tf_op jit(solution)/shard_map/reduce_scatter | solution.py:664
  399.0 60.1 %collective-permute-start.36 = (bf16[4,2,1024,128]{3,2,1,0:T(8,128)(2,1)}, bf16[4,2,1024,128]{3,2,1,0:T(8,128)(2,1)S(1)}, u32[]{:S(2)}, u32[]{:S(2)}) collective-permute-start(bf16[4,2,1024,128]{3,2,1,0:T(8,128)(2,1)} %get-tuple-element.84), channel_id=1, source_target_pairs={{0,8},{4,12},{8,0},{12,4},{16,24},{20,28},{24,16},{28,20},{1,9},{5... | collective-permute-start | bytes 6291464 | tf_op jit(solution)/shard_map/ppermute | solution.py:514
  461.0 48.3 %copy-start.5 = (bf16[1024,1024]{1,0:T(8,128)(2,1)S(1)}, bf16[1024,1024]{1,0:T(8,128)(2,1)}, u32[]{:S(2)}) copy-start(bf16[1024,1024]{1,0:T(8,128)(2,1)} %get-tuple-element.61) | copy-start | bytes 6291460
  461.0 94.4 %reduce-scatter.7.cloned.1.call-start = ((), (), s32[]{:S(2)}) async-start(), calls=%async_computation.7 | async-start | bytes 655360 | tf_op jit(solution)/shard_map/reduce_scatter | solution.py:687
  461.6 191.1 %all-gather.13.cloned.1.call-start = ((), (), s32[]{:S(2)}) async-start(), calls=%async_computation.11 | async-start | bytes 2359296 | tf_op jit(solution)/shard_map/all_gather | solution.py:663
  462.4 194.5 %all-gather.9.cloned.1.call-start = ((), (), s32[]{:S(2)}) async-start(), calls=%async_computation.6 | async-start | bytes 1966080 | tf_op jit(solution)/shard_map/all_gather | solution.py:698
  462.4 33.1 %collective-permute-start.32 = (bf16[768,256]{1,0:T(8,128)(2,1)}, bf16[768,256]{1,0:T(8,128)(2,1)S(1)}, u32[]{:S(2)}, u32[]{:S(2)}) collective-permute-start(bf16[768,256]{1,0:T(8,128)(2,1)} %reduce-scatter.5.cloned.1.call-done), channel_id=1, source_target_pairs={{4,2},{5,3},{6,0},{7,1},{12,10},{13,11},{14,8},{15,9},{20,18},{21,... | collective-permute-start | bytes 1179656 | tf_op jit(solution)/shard_map/ppermute | solution.py:695
  496.6 1.8 collective-permute-start.33
  499.2 161.3 %all-gather.11.cloned.1.call-start = ((), (), s32[]{:S(2)}) async-start(), calls=%async_computation.9 | async-start | bytes 4718592 | tf_op jit(solution)/shard_map/all_gather | solution.py:663
  509.4 2.7 collective-permute-start.19
  512.0 2.7 collective-permute-start.14
  512.5 29.8 %collective-permute-start.20 = (bf16[512,1024]{1,0:T(8,128)(2,1)S(1)}, bf16[512,1024]{1,0:T(8,128)(2,1)S(1)}, u32[]{:S(2)}, u32[]{:S(2)}) collective-permute-start(bf16[512,1024]{1,0:T(8,128)(2,1)S(1)} %add_convert_fusion.4), channel_id=1, source_target_pairs={{0,16},{4,20},{8,24},{12,28},{16,0},{20,4},{24,8},{28,12},{1,17},{... | collective-permute-start | bytes 3145736 | tf_op jit(solution)/shard_map/ppermute | solution.py:514
  514.1 40.9 %collective-permute-start.29 = (bf16[512,1024]{1,0:T(8,128)(2,1)S(1)}, bf16[512,1024]{1,0:T(8,128)(2,1)S(1)}, u32[]{:S(2)}, u32[]{:S(2)}) collective-permute-start(bf16[512,1024]{1,0:T(8,128)(2,1)S(1)} %copy-done.29), channel_id=1, source_target_pairs={{0,4},{4,0},{8,12},{12,8},{16,20},{20,16},{24,28},{28,24},{1,5},{5... | collective-permute-start | bytes 3145736 | tf_op jit(solution)/shard_map/ppermute | solution.py:514
  514.7 27.6 %copy-start.17 = (bf16[512,1024]{1,0:T(8,128)(2,1)}, bf16[512,1024]{1,0:T(8,128)(2,1)S(1)}, u32[]{:S(2)}) copy-start(bf16[512,1024]{1,0:T(8,128)(2,1)S(1)} %collective-permute-done.14.refs_1_) | copy-start | bytes 3145732
  543.3 11.6 %copy-start.9 = (bf16[512,1024]{1,0:T(8,128)(2,1)S(1)}, bf16[512,1024]{1,0:T(8,128)(2,1)}, u32[]{:S(2)}) copy-start(bf16[512,1024]{1,0:T(8,128)(2,1)} %get-tuple-element.73) | copy-start | bytes 3145732
  546.9 44.9 %collective-permute-start.21 = (bf16[512,1024]{1,0:T(8,128)(2,1)}, bf16[512,1024]{1,0:T(8,128)(2,1)S(1)}, u32[]{:S(2)}, u32[]{:S(2)}) collective-permute-start(bf16[512,1024]{1,0:T(8,128)(2,1)} %output_sum.1), channel_id=1, source_target_pairs={{0,0},{1,1},{2,4},{3,5},{4,2},{5,3},{6,6},{7,7},{8,8},{9,9},{10,12... | collective-permute-start | bytes 3145736 | tf_op jit(solution)/shard_map/ppermute | solution.py:543
  548.7 43.1 %collective-permute-start.28 = (bf16[512,1024]{1,0:T(8,128)(2,1)}, bf16[512,1024]{1,0:T(8,128)(2,1)}, u32[]{:S(2)}, u32[]{:S(2)}) collective-permute-start(bf16[512,1024]{1,0:T(8,128)(2,1)} %get-tuple-element.72), channel_id=1, source_target_pairs={{0,4},{4,0},{8,12},{12,8},{16,20},{20,16},{24,28},{28,24},{1,5},{5... | collective-permute-start | bytes 3145736 | tf_op jit(solution)/shard_map/ppermute | solution.py:514
  555.3 37.7 %collective-permute-start.30 = (bf16[512,1024]{1,0:T(8,128)(2,1)S(1)}, bf16[512,1024]{1,0:T(8,128)(2,1)S(1)}, u32[]{:S(2)}, u32[]{:S(2)}) collective-permute-start(bf16[512,1024]{1,0:T(8,128)(2,1)S(1)} %add_convert_fusion.2), channel_id=1, source_target_pairs={{1,0},{0,1},{3,2},{2,3},{5,4},{4,5},{7,6},{6,7},{9,8},{8,9},{11,10... | collective-permute-start | bytes 3145736 | tf_op jit(solution)/shard_map/ppermute | solution.py:530
  555.4 11.7 %collective-permute-start.34 = (bf16[64,1024]{1,0:T(8,128)(2,1)}, bf16[64,1024]{1,0:T(8,128)(2,1)S(1)}, u32[]{:S(2)}, u32[]{:S(2)}) collective-permute-start(bf16[64,1024]{1,0:T(8,128)(2,1)} %reduce-scatter.7.cloned.1.call-done), channel_id=1, source_target_pairs={{4,2},{5,3},{6,0},{7,1},{12,10},{13,11},{14,8},{15,9},{20,18},{21,... | collective-permute-start | bytes 393224 | tf_op jit(solution)/shard_map/ppermute | solution.py:695
  568.1 33.1 %collective-permute-start.35 = (bf16[64,1024]{1,0:T(8,128)(2,1)S(1)}, bf16[64,1024]{1,0:T(8,128)(2,1)S(1)}, u32[]{:S(2)}, u32[]{:S(2)}) collective-permute-start(bf16[64,1024]{1,0:T(8,128)(2,1)S(1)} %add_convert_fusion.7), channel_id=1, source_target_pairs={{0,4},{4,0},{8,12},{12,8},{16,20},{20,16},{24,28},{28,24},{1,5},{5... | collective-permute-start | bytes 393224 | tf_op jit(solution)/shard_map/ppermute | solution.py:514
  599.2 14.4 %copy-start.27 = (f32[1,1024]{1,0:T(1,128)S(1)}, f32[1,1024]{1,0:T(1,128)}, u32[]{:S(2)}) copy-start(f32[1,1024]{1,0:T(1,128)} %get-tuple-element.89) | copy-start | bytes 12292
  599.2 14.4 %copy-start.28 = (f32[1,1024]{1,0:T(1,128)S(1)}, f32[1,1024]{1,0:T(1,128)}, u32[]{:S(2)}) copy-start(f32[1,1024]{1,0:T(1,128)} %get-tuple-element.88) | copy-start | bytes 12292
  599.2 57.6 %collective-permute-start.31 = (bf16[512,1024]{1,0:T(8,128)(2,1)}, bf16[512,1024]{1,0:T(8,128)(2,1)S(1)}, u32[]{:S(2)}, u32[]{:S(2)}) collective-permute-start(bf16[512,1024]{1,0:T(8,128)(2,1)} %get-tuple-element.75), channel_id=1, source_target_pairs={{0,0},{1,1},{2,4},{3,5},{4,2},{5,3},{6,6},{7,7},{8,8},{9,9},{10,12... | collective-permute-start | bytes 3145736 | tf_op jit(solution)/shard_map/ppermute | solution.py:543
  656.8 3.7 copy-start.12
  (15 other events, 22.1 us)
Sparse Core Ops, SparseCore 0:
  46.8 26.0 all-gather.6
  82.0 66.1 all-gather.14
  334.4 28.3 reduce-scatter.10
  399.1 44.7 reduce-scatter.4
  461.1 48.0 reduce-scatter.8
  512.0 30.2 reduce-scatter.6
  544.3 27.8 all-gather.12
  574.2 30.9 all-gather.8
  607.3 39.1 all-gather.10

commit v2 on v1

v2 whole, which is shorter than its diff:
```python
import functools
import math

import jax
import jax.numpy as jnp
from jax import lax
from jax.experimental import pallas as pl
from jax.experimental.pallas import tpu as pltpu
from jax.sharding import PartitionSpec as P

HEAD_DIM = 64
EPSILON = 1e-05
MASKED = -1000000000.0
ROPE_BASE = 10000.0
LOG2E = math.log2(math.e)
SCALE = HEAD_DIM ** (-0.5)
BF16 = jnp.bfloat16
F32 = jnp.float32
MIB = 1 << 20
PER_US = 1.15e9 * 0.25


def dot(a, b, ca, cb):
    return lax.dot_general(a, b, (((ca,), (cb,)), ((), ())), preferred_element_type=F32)


def call(body, name, out, us, vmem=56, **kw):
    return pl.pallas_call(
        body,
        out_shape=out,
        name=name,
        compiler_params=pltpu.CompilerParams(vmem_limit_bytes=vmem * MIB),
        cost_estimate=pl.CostEstimate(
            flops=int(us * PER_US), bytes_accessed=0, transcendentals=0
        ),
        **kw,
    )


def shape(s, d):
    return jax.ShapeDtypeStruct(s, d)


def norm_rows(x, gain):
    centered = x - jnp.mean(x, axis=-1, keepdims=True)
    inverse = lax.rsqrt(jnp.mean(centered * centered, axis=-1, keepdims=True) + EPSILON)
    scaled = centered * inverse
    return scaled * gain, scaled, inverse


def norm_kernel(x_ref, g_ref, o_ref):
    o_ref[...] = norm_rows(x_ref[...].astype(F32), g_ref[...])[0].astype(BF16)


def norm_call(x, gain):
    n, d = x.shape
    b = min(128, n)
    return call(
        norm_kernel,
        "norm_tokens",
        shape((n, d), BF16),
        grid=(n // b,),
        in_specs=[pl.BlockSpec((b, d), lambda i: (i, 0)), pl.BlockSpec((1, d), lambda i: (0, 0))],
        out_specs=pl.BlockSpec((b, d), lambda i: (i, 0)),
        us=2.2,
    )(x, gain)


def middle_kernel(x_ref, g_ref, *refs):
    parts, (m_ref, o_ref) = refs[:-2], refs[-2:]
    m = x_ref[...].astype(F32)
    for p in parts:
        m = m + p[...].astype(F32)
    m_ref[...] = m
    o_ref[...] = norm_rows(m, g_ref[...])[0].astype(BF16)


def middle_call(x, gain, parts):
    n, d = x.shape
    b = min(128, n)
    row = pl.BlockSpec((b, d), lambda i: (i, 0))
    return call(
        middle_kernel,
        "middle_norm",
        (shape((n, d), F32), shape((n, d), BF16)),
        grid=(n // b,),
        in_specs=[row, pl.BlockSpec((1, d), lambda i: (0, 0))] + [row] * len(parts),
        out_specs=(row, row),
        us=4.5,
    )(x, gain, *parts)


def back_kernel(n_parts, keep, base_ref, x_ref, g_ref, *refs):
    parts, outs = refs[:n_parts], refs[n_parts:]
    e = parts[0][...].astype(F32)
    for p in parts[1:]:
        e = e + p[...].astype(F32)
    gain = g_ref[...]
    _, scaled, inverse = norm_rows(x_ref[...].astype(F32), gain)
    through = e * gain
    first = jnp.mean(through, axis=-1, keepdims=True)
    second = jnp.mean(through * scaled, axis=-1, keepdims=True)
    total = base_ref[...].astype(F32) + inverse * (through - first - scaled * second)
    if keep:
        outs[0][...] = total
    outs[-2][...] = total.astype(BF16)

    @pl.when(pl.program_id(0) == 0)
    def _():
        outs[-1][...] = jnp.zeros_like(outs[-1])

    outs[-1][...] += jnp.sum(e * scaled, axis=0, keepdims=True)


def back_call(name, base, x, gain, parts, keep):
    n, d = x.shape
    b = min(128, n)
    row = pl.BlockSpec((b, d), lambda i: (i, 0))
    one = pl.BlockSpec((1, d), lambda i: (0, 0))
    out = [shape((n, d), F32)] * keep + [shape((n, d), BF16), shape((1, d), F32)]
    return call(
        functools.partial(back_kernel, len(parts), keep),
        name,
        tuple(out),
        grid=(n // b,),
        in_specs=[row, row, one] + [row] * len(parts),
        out_specs=tuple([row] * (keep + 1) + [one]),
        us=5.5,
    )(base, x, gain, *parts)


def output_kernel(m_ref, *refs):
    total = m_ref[...]
    for p in refs[:-1]:
        total = total + p[...].astype(F32)
    refs[-1][...] = total.astype(BF16)


def output_call(m, parts):
    n, d = m.shape
    b = min(256, n)
    row = pl.BlockSpec((b, d), lambda i: (i, 0))
    return call(
        output_kernel,
        "output_sum",
        shape((n, d), BF16),
        grid=(n // b,),
        in_specs=[row] * (1 + len(parts)),
        out_specs=row,
        us=3.6,
    )(m, *parts)


def turn(u, cos, sin):
    half = HEAD_DIM // 2
    first, second = u[:half], u[half:]
    return jnp.concatenate([first * cos - second * sin, second * cos + first * sin], axis=0)


def turn_back(u, cos, sin):
    half = HEAD_DIM // 2
    first, second = u[:half], u[half:]
    return jnp.concatenate([first * cos + second * sin, second * cos - first * sin], axis=0)


def part_cols(i, n_parts, n):
    at = (i % (n_parts // 2)) * 2 + i // (n_parts // 2)
    return slice(at * n, (at + 1) * n)


def qkv_kernel(n_parts, c_ref, s_ref, w_ref, *refs):
    parts, (q_ref, k_ref, v_ref) = refs[:n_parts], refs[n_parts:]
    n, d = parts[0].shape
    f = w_ref.shape[-1]
    for which, out in enumerate((q_ref, k_ref, v_ref)):
        w = w_ref[:, which].reshape(d, f)
        for i, p in enumerate(parts):
            cols = part_cols(i, n_parts, n)
            cos, sin = c_ref[:, cols], s_ref[:, cols]
            u = dot(w, p[...], 0, 1)
            for h in range(f // HEAD_DIM):
                rows = slice(h * HEAD_DIM, (h + 1) * HEAD_DIM)
                head = u[rows]
                if which < 2:
                    head = turn(head, cos, sin)
                out[rows, cols] = head.astype(BF16)


def qkv_call(parts, pack, cos, sin):
    n, d = parts[0].shape
    f = pack.shape[-1]
    total = n * len(parts)
    return call(
        functools.partial(qkv_kernel, len(parts)),
        "project_heads",
        (shape((f, total), BF16),) * 3,
        us=7.6,
    )(cos, sin, pack, *parts)


def split(x, n):
    out = []
    for _ in range(n):
        h = x.astype(BF16)
        out.append(h)
        x = x - h.astype(F32)
    return out


def attend_kernel(q_ref, k_ref, v_ref, b_ref, o_ref, l_ref, ka, va, *, sub):
    S = k_ref.shape[1]
    bq = q_ref.shape[1]

    @pl.when(pl.program_id(1) == 0)
    def _():
        k = k_ref[...]
        ka[...] = jnp.concatenate([k, k, b_ref[...]], axis=0).T
        va[0:HEAD_DIM] = v_ref[...]
        va[HEAD_DIM:] = jnp.ones((16, S), BF16)

    high, low = split(q_ref[...].astype(F32) * (SCALE * LOG2E), 2)
    row = lax.broadcasted_iota(jnp.int32, (16, bq), 0)
    one = jnp.where(row == 0, 1.0, 0.0).astype(BF16)
    qa = jnp.concatenate([high, low, one], axis=0)
    steps = bq // sub

    def scores(i):
        return dot(ka[...], qa[:, i * sub : (i + 1) * sub], 1, 0)

    s = scores(0)
    for i in range(steps):
        later = scores(i + 1) if i + 1 < steps else None
        cols = slice(i * sub, (i + 1) * sub)
        top = jnp.max(s, axis=0, keepdims=True)
        p = jnp.exp2(s - top).astype(BF16)
        o = dot(va[...], p, 1, 0)
        total = o[HEAD_DIM : HEAD_DIM + 1]
        o_ref[:, cols] = (o[:HEAD_DIM] * (1.0 / total)).astype(BF16)
        l_ref[0, :, cols] = jnp.broadcast_to(top + jnp.log2(total), (8, sub))
        s = later


def attend_call(q, k, v, bias, first, count):
    S = q.shape[1]
    bq = S
    sub = min(256, S)
    whole = pl.BlockSpec((HEAD_DIM, S), lambda h, i: (h + first, 0))
    block = pl.BlockSpec((HEAD_DIM, bq), lambda h, i: (h + first, i))
    return call(
        functools.partial(attend_kernel, sub=sub),
        "attend",
        (shape((count * HEAD_DIM, S), BF16), shape((count, 8, S), F32)),
        grid=(count, S // bq),
        in_specs=[block, whole, whole, pl.BlockSpec((16, S), lambda h, i: (0, 0))],
        out_specs=(
            pl.BlockSpec((HEAD_DIM, bq), lambda h, i: (h, i)),
            pl.BlockSpec((1, 8, bq), lambda h, i: (h, 0, i)),
        ),
        scratch_shapes=[
            pltpu.VMEM((S, 2 * HEAD_DIM + 16), BF16),
            pltpu.VMEM((HEAD_DIM + 16, S), BF16),
        ],
        us=7.4 * count,
    )(q, k, v, bias)


def attend_back_kernel(
    q_ref, k_ref, v_ref, b_ref, o_ref, l_ref, g_ref, c_ref, s_ref, ck_ref, sk_ref,
    dq_ref, dk_ref, dv_ref, ka, va, dka, dva, *, sub
):
    S = k_ref.shape[1]
    bq = q_ref.shape[1]

    @pl.when(pl.program_id(1) == 0)
    def _():
        k = k_ref[...]
        one = jnp.ones((16, S), BF16)
        ka[...] = jnp.concatenate([k, k, b_ref[...], one], axis=0).T
        va[...] = jnp.concatenate([v_ref[...], one], axis=0).T
        dka[...] = jnp.zeros_like(dka)
        dva[...] = jnp.zeros_like(dva)

    q = q_ref[...].astype(F32) * SCALE
    qs = q.astype(BF16)
    high, low = split(q * LOG2E, 2)
    row = lax.broadcasted_iota(jnp.int32, (16, bq), 0)

    def spread(x):
        a, b, c = [y.astype(F32) for y in split(x, 3)]
        rest = jnp.where(row == 2, c, 0.0)
        return jnp.where(row == 0, a, jnp.where(row == 1, b, rest)).astype(BF16)

    one = jnp.where(row == 0, 1.0, 0.0).astype(BF16)
    g = g_ref[...]
    qa = jnp.concatenate([high, low, one, spread(-l_ref[0, 0:1])], axis=0)
    centre = jnp.sum(g.astype(F32) * o_ref[...].astype(F32), axis=0, keepdims=True)
    ga = jnp.concatenate([g, spread(-centre)], axis=0)
    for i in range(bq // sub):
        cols = slice(i * sub, (i + 1) * sub)
        p = jnp.exp2(dot(ka[...], qa[:, cols], 1, 0))
        p_low = p.astype(BF16)
        ds = (p * dot(va[...], ga[:, cols], 1, 0)).astype(BF16)
        dva[...] += dot(g[:, cols], p_low, 1, 1)
        dka[...] += dot(qs[:, cols], ds, 1, 1)
        dq = dot(k_ref[...], ds, 1, 0) * SCALE
        dq_ref[:, cols] = turn_back(dq, c_ref[:, cols], s_ref[:, cols]).astype(BF16)

    @pl.when(pl.program_id(1) == pl.num_programs(1) - 1)
    def _():
        dk_ref[...] = turn_back(dka[...], ck_ref[...], sk_ref[...]).astype(BF16)
        dv_ref[...] = dva[...].astype(BF16)


def attend_back_call(q, k, v, bias, o, lse, g, cos, sin, head, place):
    S = q.shape[1]
    bq = min(1024, S)
    half = HEAD_DIM // 2
    whole = pl.BlockSpec((HEAD_DIM, S), lambda h, i: (head, 0))
    block = pl.BlockSpec((HEAD_DIM, bq), lambda h, i: (head, i))
    table = pl.BlockSpec((half, S), lambda h, i: (0, 0))
    table_block = pl.BlockSpec((half, bq), lambda h, i: (0, i))
    return call(
        functools.partial(attend_back_kernel, sub=min(256, S)),
        "attend_back",
        (shape((HEAD_DIM, S), BF16),) * 3,
        us=12.3,
        grid=(1, S // bq),
        in_specs=[
            block, whole, whole,
            pl.BlockSpec((16, S), lambda h, i: (0, 0)),
            pl.BlockSpec((HEAD_DIM, bq), lambda h, i: (place, i)),
            pl.BlockSpec((1, 8, bq), lambda h, i: (place, 0, i)),
            block, table_block, table_block, table, table,
        ],
        out_specs=(
            pl.BlockSpec((HEAD_DIM, bq), lambda h, i: (0, i)),
            pl.BlockSpec((HEAD_DIM, S), lambda h, i: (0, 0)),
            pl.BlockSpec((HEAD_DIM, S), lambda h, i: (0, 0)),
        ),
        scratch_shapes=[
            pltpu.VMEM((S, 2 * HEAD_DIM + 32), BF16),
            pltpu.VMEM((S, HEAD_DIM + 16), BF16),
            pltpu.VMEM((HEAD_DIM, S), F32),
            pltpu.VMEM((HEAD_DIM, S), F32),
        ],
    )(q, k, v, bias, o, lse, g, cos, sin, cos, sin)


def stack_rows(refs, cols):
    return jnp.concatenate([r[:, cols] for r in refs], axis=0)


def out_kernel(n_heads, w_ref, *refs):
    heads, outs = refs[:n_heads], refs[n_heads:]
    n, d = outs[0].shape
    J, b = w_ref.shape[0], w_ref.shape[-1]
    for i, out in enumerate(outs):
        o = stack_rows(heads, slice(i * n, (i + 1) * n))
        for j in range(J):
            out[:, j * b : (j + 1) * b] = dot(o, w_ref[j], 0, 0).astype(BF16)


def pack_spec(pack, which):
    J, _, a, b = pack.shape
    return pl.BlockSpec((J, None, a, b), lambda i: (0, which, 0, 0))


def full(s):
    return pl.BlockSpec(s, lambda i: (0,) * len(s))


def out_call(heads, pack, n_parts, d):
    S = heads[0].shape[1]
    f = sum(o.shape[0] for o in heads)
    return call(
        functools.partial(out_kernel, len(heads)),
        "output_projection",
        (shape((S // n_parts, d), BF16),) * n_parts,
        grid=(1,),
        in_specs=[pack_spec(pack, 3)] + [full(o.shape) for o in heads],
        out_specs=(full((S // n_parts, d)),) * n_parts,
        us=4.2,
    )(pack, *heads)


def heads_grad_kernel(n_heads, n_parts, w_ref, *refs):
    heads, parts, (g_ref, dw_ref) = (
        refs[:n_heads], refs[n_heads : n_heads + n_parts], refs[n_heads + n_parts :]
    )
    n = parts[0].shape[0]
    J, b = w_ref.shape[0], w_ref.shape[-1]
    w = jnp.concatenate([w_ref[j] for j in range(J)], axis=1)
    total = None
    for i, p in enumerate(parts):
        cols = slice(i * n, (i + 1) * n)
        g_ref[:, cols] = dot(w, p[...], 1, 1).astype(BF16)
        term = dot(stack_rows(heads, cols), p[...], 1, 0)
        total = term if total is None else total + term
    for j in range(J):
        dw_ref[j] = total[:, j * b : (j + 1) * b].astype(BF16)


def heads_grad_call(heads, pack, parts):
    S = heads[0].shape[1]
    f = sum(o.shape[0] for o in heads)
    n, d = parts[0].shape
    J, _, a, b = pack.shape
    return call(
        functools.partial(heads_grad_kernel, len(heads), len(parts)),
        "heads_grad",
        (shape((f, S), BF16), shape((J, a, b), BF16)),
        grid=(1,),
        in_specs=[pack_spec(pack, 3)] + [full(o.shape) for o in heads] + [full((n, d))] * len(parts),
        out_specs=(full((f, S)), full((J, a, b))),
        us=6,
    )(pack, *heads, *parts)


def qkv_back_kernel(n_parts, n_groups, w_ref, *refs):
    grads, outs = refs[: 3 * n_groups], refs[3 * n_groups :]
    n, d = outs[0].shape
    f = w_ref.shape[-1]
    for i, out in enumerate(outs):
        cols = slice(i * n, (i + 1) * n)
        total = None
        for j in range(3):
            g = stack_rows(grads[j::3], cols)
            term = dot(g, w_ref[:, j].reshape(d, f), 0, 1)
            total = term if total is None else total + term
        out[...] = total.astype(BF16)


def qkv_back_call(pack, grads, n_parts, d):
    f = pack.shape[-1]
    S = grads[0][0].shape[1]
    flat = [g for group in grads for g in group]
    return call(
        functools.partial(qkv_back_kernel, n_parts, len(grads)),
        "qkv_back",
        (shape((S // n_parts, d), BF16),) * n_parts,
        us=7,
    )(pack, *flat)


def qkv_weight_kernel(n_parts, n_groups, wo_ref, *refs):
    grads, parts, dw_ref = refs[: 3 * n_groups], refs[3 * n_groups : -1], refs[-1]
    n = parts[0].shape[0]
    J, _, a, b = dw_ref.shape
    for j in range(3):
        total = None
        for i, p in enumerate(parts):
            g = stack_rows(grads[j::3], part_cols(i, n_parts, n))
            term = dot(p[...], g, 0, 1)
            total = term if total is None else total + term
        dw_ref[:, j] = total.astype(BF16).reshape(J, a, b)
    dw_ref[:, 3] = wo_ref[...]


def qkv_weight_call(wo_grad, grads, parts, pack_shape):
    n, d = parts[0].shape
    f = pack_shape[-1]
    S = n * len(parts)
    flat = [g for group in grads for g in group]
    return call(
        functools.partial(qkv_weight_kernel, len(parts), len(grads)),
        "qkv_weights",
        shape(pack_shape, BF16),
        us=8,
    )(wo_grad, *flat, *parts)


def pack_kernel(n_parts, index_ref, q_ref, o_ref, *refs):
    parts, out = refs[:-1], refs[-1]
    J, _, a, b = out.shape

    @pl.when(index_ref[n_parts] == 0)
    def _():
        for j in range(J):
            for which in range(3):
                out[j, which] = q_ref[which, j * a : (j + 1) * a]
            out[j, 3] = o_ref[:, j * b : (j + 1) * b]

    @pl.when(index_ref[n_parts] == 1)
    def _():
        for i, p in enumerate(parts):
            out[index_ref[i]] = p[...]


def pack_call(index, wq, wo, parts):
    _, a, b = parts[0].shape
    J = len(parts)
    vmem = pl.BlockSpec(memory_space=pltpu.VMEM)
    return call(
        functools.partial(pack_kernel, J),
        "pack_heads",
        shape((J, 4, a, b), BF16),
        in_specs=[pl.BlockSpec(memory_space=pltpu.SMEM)] + [vmem] * (J + 2),
        out_specs=vmem,
        us=3.7,
    )(index, wq, wo, *parts)


def unpack_kernel(n_parts, index_ref, *refs):
    parts, (q_ref, o_ref) = refs[:n_parts], refs[n_parts:]
    a, b = parts[0].shape[1:]
    for i, p in enumerate(parts):
        j = index_ref[i]
        for which in range(3):
            q_ref[which, pl.ds(pl.multiple_of(j * a, a), a), :] = p[which].astype(F32)
        o_ref[:, pl.ds(pl.multiple_of(j * b, b), b)] = p[3].astype(F32)


def unpack_call(index, parts):
    _, a, b = parts[0].shape
    J = len(parts)
    vmem = pl.BlockSpec(memory_space=pltpu.VMEM)
    return call(
        functools.partial(unpack_kernel, J),
        "unpack_heads",
        (shape((3, J * a, b), F32), shape((a, J * b), F32)),
        in_specs=[pl.BlockSpec(memory_space=pltpu.SMEM)] + [vmem] * J,
        out_specs=(vmem, vmem),
        us=3.8,
    )(index, *parts)


def ffn_kernel(groups, steps, *refs):
    x0, x1, c0, c1 = refs[:4]
    weights = refs[4 : 4 + 3 * groups]
    h_ref, gl_ref, ul_ref, out0, out1, dx0, dx1 = refs[4 + 3 * groups :]
    early = pl.program_id(0) < steps
    x = jnp.where(early, x0[...], x1[...])
    c = jnp.where(early, c0[...], c1[...])
    out = dx = None
    for m in range(groups):
        wg, wu, wd = [r[...].reshape(-1, r.shape[-1]) for r in weights[3 * m : 3 * m + 3]]
        gate = dot(x, wg, 1, 1)
        up = dot(x, wu, 1, 1)
        hg = dot(c, wd, 1, 1)
        sig = jax.nn.sigmoid(gate)
        act = gate * sig
        hidden = (act * up).astype(BF16)
        gl = (hg * up * (sig * (1.0 + gate * (1.0 - sig)))).astype(BF16)
        ul = (hg * act).astype(BF16)
        cols = slice(m * wg.shape[0], (m + 1) * wg.shape[0])
        h_ref[:, cols] = hidden
        gl_ref[:, cols] = gl
        ul_ref[:, cols] = ul
        o = dot(hidden, wd, 1, 0)
        e = dot(gl, wg, 1, 0) + dot(ul, wu, 1, 0)
        out = o if out is None else out + o
        dx = e if dx is None else dx + e

    @pl.when(early)
    def _():
        out0[...] = out.astype(BF16)
        dx0[...] = dx.astype(BF16)

    @pl.when(jnp.logical_not(early))
    def _():
        out1[...] = out.astype(BF16)
        dx1[...] = dx.astype(BF16)


def ffn_call(xs, cs, weights):
    n, d = xs[0].shape
    groups = len(weights)
    T, us, _ = weights[0][0].shape
    units = groups * T * us
    b = min(256, n)
    steps = n // b
    first = pl.BlockSpec((b, d), lambda i: (jnp.minimum(i, steps - 1), 0))
    second = pl.BlockSpec((b, d), lambda i: (jnp.maximum(i - steps, 0), 0))
    urow = pl.BlockSpec((b, units), lambda i: (i, 0))
    specs, args = [], []
    for group in weights:
        specs += [pl.BlockSpec((T, us, d), lambda i: (0, 0, 0))] * 3
        args += group
    return call(
        functools.partial(ffn_kernel, groups, steps),
        "feed_forward",
        (shape((2 * n, units), BF16),) * 3 + (shape((n, d), BF16),) * 4,
        grid=(2 * steps,),
        in_specs=[first, second, first, second] + specs,
        out_specs=(urow,) * 3 + (first, second, first, second),
        us=21,
    )(*xs, *cs, *args)


def ffn_weight_kernel(T, us, *refs):
    x, c = refs[:4], refs[4:8]
    h, gl, ul = refs[8:10], refs[10:12], refs[12:14]
    outs = refs[14:]
    n = x[0].shape[0]

    def product(a, b):
        total = None
        for i in range(4):
            rows = slice((i % 2) * n, (i % 2 + 1) * n)
            term = dot(a[i][...], b(i, rows), 0, 0)
            total = term if total is None else total + term
        return total.astype(BF16)

    dw = product(c, lambda i, rows: h[i // 2][rows])
    for t in range(T):
        outs[1][t, 1] = dw[:, t * us : (t + 1) * us]
    dw = product(x, lambda i, rows: jnp.concatenate([gl[i // 2][rows], ul[i // 2][rows]], axis=1))
    for t in range(T):
        outs[0][t] = dw[:, t * us : (t + 1) * us]
        outs[1][t, 0] = dw[:, (T + t) * us : (T + t + 1) * us]


def ffn_weight_call(x, c, h, gl, ul, m, T, us):
    n, d = x[0].shape
    db = min(256, d)
    spec = [pl.BlockSpec((n, db), lambda i: (0, i))] * 8
    spec += [pl.BlockSpec((2 * n, T * us), lambda i: (0, m))] * 6
    return call(
        functools.partial(ffn_weight_kernel, T, us),
        "feed_forward_weights",
        (shape((T, d, us), BF16), shape((T, 2, d, us), BF16)),
        grid=(d // db,),
        in_specs=spec,
        out_specs=(
            pl.BlockSpec((T, db, us), lambda i: (0, i, 0)),
            pl.BlockSpec((T, 2, db, us), lambda i: (0, 0, i, 0)),
        ),
        us=12.4,
    )(*x, *c, *h, *gl, *ul)


def assemble_kernel(w_ref, gu_ref, dn_ref):
    DP, _, _, us = w_ref.shape
    for j in range(2):
        rows = jnp.concatenate([w_ref[p, j] for p in range(DP)], axis=1)
        gu_ref[:, j, :] = rows.astype(F32)
    rows = jnp.concatenate([w_ref[p, 2] for p in range(DP)], axis=1)
    dn_ref[...] = rows.T.astype(F32)


def assemble_call(w):
    DP, _, d, us = w.shape
    b = min(256, d)
    return call(
        assemble_kernel,
        "feed_forward_gradients",
        (shape((d, 2, DP * us), F32), shape((DP * us, d), F32)),
        grid=(d // b,),
        in_specs=[pl.BlockSpec((DP, 3, b, us), lambda i: (0, 0, i, 0))],
        out_specs=(
            pl.BlockSpec((b, 2, DP * us), lambda i: (i, 0, 0)),
            pl.BlockSpec((DP * us, b), lambda i: (0, i)),
        ),
        us=8,
    )(w)


def after(x, *deps):
    return lax.optimization_barrier((x, *deps))[0]


def tie(*xs):
    return lax.optimization_barrier(xs)


def build(DP, T):
    M = DP // 4
    R = T // 2
    J = DP // 2

    def over_dp(x, f):
        return lax.ppermute(x, "dp", [(i, f(i)) for i in range(DP)])

    def core_flip(x):
        return over_dp(x, lambda i: i ^ 1)

    def top_flip(x):
        return over_dp(x, lambda i: (i + DP // 2) % DP)

    def mid_from(x, k):
        def dest(i):
            a, m, c = i // (DP // 2), (i // 2) % M, i % 2
            return a * (DP // 2) + ((m - k) % M) * 2 + c

        return over_dp(x, dest)

    def pair_from(x, k):
        return over_dp(x, lambda i: ((i // 2) ^ k) * 2 + i % 2)

    def row_from(x, k):
        return lax.ppermute(
            x, "tensor", [((t // R) * R + (t % R + k) % R, t) for t in range(T)]
        )

    def reshard(x):
        pairs = []
        for d in range(DP):
            for t in range(T):
                j, c, h, r = d // 2, d % 2, t // R, t % R
                pairs.append((d * T + t, (2 * j + h) * T + c * R + r))
        return lax.ppermute(x, ("dp", "tensor"), pairs)

    def send_rows(x):
        return [row_from(x, k) for k in range(1, R)]

    def gather_heads(x, flipped, rows, hold):
        out = [x, flipped]
        for y in rows:
            y = after(y, hold)
            out += [y, core_flip(y)]
        return out

    def scatter_heads(pieces):
        out = []
        for k in range(R):
            mine, theirs = pieces[2 * k], core_flip(pieces[2 * k + 1])
            if k == 0:
                out += [mine, theirs]
            else:
                both = (mine.astype(F32) + theirs.astype(F32)).astype(BF16)
                out.append(row_from(both, R - k))
        return out

    def gather_units(y):
        z = top_flip(y)
        return [y, core_flip(y), z, core_flip(z)]

    def sum_all(x):
        for bit in range(DP.bit_length() - 1):
            x = x + over_dp(x, lambda i, bit=bit: i ^ (1 << bit))
        for bit in range(T.bit_length() - 1):
            x = x + lax.ppermute(x, "tensor", [(t, t ^ (1 << bit)) for t in range(T)])
        return x

    def on_device(
        tokens, qkv_weight, output_projection_weight, gate_up_weight, down_projection_weight,
        attention_gain, feedforward_gain, window_lengths, key_mask, cotangent,
    ):
        n, _, d = tokens.shape
        length = key_mask.shape[0]
        me_d, me_t = lax.axis_index("dp"), lax.axis_index("tensor")
        core, h, r, pair = me_d % 2, me_t // R, me_t % R, me_d // 2
        us = down_projection_weight.shape[0] // DP
        gain_one, gain_two = attention_gain[None], feedforward_gain[None]
        a = d // J

        xs = [reshard(tokens[i * n // 2 : (i + 1) * n // 2, 0]) for i in (0, 1)]

        wq_own = qkv_weight.transpose(1, 0, 2)
        f = wq_own.shape[2]
        share = jnp.concatenate(
            [
                lax.dynamic_slice_in_dim(wq_own, pair * a, a, 1),
                lax.dynamic_slice_in_dim(output_projection_weight, pair * a, a, 1)[None],
            ],
            axis=0,
        )
        far_pairs = [
            ((2 * j + 1) * T + t, (2 * j + 1) * T + (t + R) % T)
            for j in range(J)
            for t in range(T)
        ]
        share = lax.ppermute(after(share, xs[0]), ("dp", "tensor"), far_pairs)
        shares = [share] + [
            lax.ppermute(
                share, "dp", [(2 * j + 1, 2 * (j ^ k) + 1) for j in range(J)]
            )
            for k in range(1, J)
        ]
        index = jnp.stack([pair ^ k for k in range(J)] + [core]).astype(jnp.int32)
        pack = pack_call(index, wq_own, output_projection_weight, shares)

        positions = jnp.arange(length, dtype=jnp.int32)
        valid = (positions < window_lengths[0]) & (key_mask[:, 0] == 1)
        bias_own = jnp.where(valid, 0.0, MASKED).astype(F32)
        bias = jnp.where(core == h, bias_own, core_flip(bias_own))
        order = jnp.stack(
            [((core + dc) % 2) * R + (r + dr) % R for dr in range(R) for dc in (0, 1)]
        )
        bias = jnp.take(bias.reshape(T, n), order, axis=0).reshape(length)
        bias = jnp.concatenate(
            [bias[None].astype(BF16), jnp.zeros((15, length), BF16)], axis=0
        )
        places = (order[:, None] * n + jnp.arange(n, dtype=jnp.int32)[None]).reshape(length)
        half = HEAD_DIM // 2
        frequencies = ROPE_BASE ** (-(jnp.arange(half, dtype=F32) * 2.0 / HEAD_DIM))
        angles = frequencies[:, None] * places.astype(F32)[None]
        cos, sin = jnp.cos(angles), jnp.sin(angles)

        gate, up = lax.dynamic_slice_in_dim(gate_up_weight, me_d * us, us, 2).transpose(1, 2, 0)
        dn = lax.dynamic_slice_in_dim(down_projection_weight, me_d * us, us, 0)

        xs[0], _ = lax.optimization_barrier((xs[0], (bias, cos, sin, gate, up, index)))
        first = norm_call(xs[0], gain_one)
        rows_one = send_rows(first)
        second = norm_call(after(xs[1], first), gain_one)
        rows_two = send_rows(second)
        flips = [core_flip(first), core_flip(second)]
        normed_one = gather_heads(first, flips[0], rows_one, second)
        normed_one += gather_heads(second, flips[1], rows_two, pack)
        x = jnp.concatenate(xs)
        cot = reshard(after(cotangent[:, 0], xs[1]))

        gate, up, dn = [
            lax.all_gather(z, "tensor", axis=0) for z in tie(gate, up, dn, second)[:3]
        ]
        own_units = (gate, up, dn)
        weights = [own_units] + [[mid_from(z, k) for z in own_units] for k in range(1, M)]
        q, k, v = qkv_call(normed_one, pack, cos, sin)
        heads = f // HEAD_DIM
        count = max(1, heads // 2)
        o, lse = [], []
        for first in range(0, heads, count):
            if first:
                q, o[0] = tie(q, o[0])
            got = attend_call(q, k, v, bias, first, count)
            o.append(got[0])
            lse.append(got[1])
        o[-1], cot = tie(o[-1], cot)
        pieces = out_call(o, pack, T, d)
        cots = gather_units(after(cot, pieces[0]))
        arrived = scatter_heads(pieces)
        middle, normed = middle_call(x, gain_two, arrived)

        xs = gather_units(normed)
        near = ffn_call(xs[:2], cots[:2], weights)
        near_dx = core_flip(near[6])
        far_x, near_dx = tie(xs[2], near_dx)
        far = ffn_call([far_x, xs[3]], cots[2:], weights)

        def cross(mine, theirs):
            both = mine.astype(F32) + core_flip(theirs).astype(F32)
            return top_flip(both.astype(BF16))

        crossed = cross(far[5], far[6])

        def weight_grads(m, hold):
            return ffn_weight_call(
                [after(xs[0], hold), *xs[1:]], cots, *[[near[i], far[i]] for i in range(3)], m, T, us
            )

        sent, hold = [], far[0]
        for m in range(M - 1, 0, -1):
            got = weight_grads(m, hold)
            hold = got[0]
            sent.append([mid_from(g, M - m) for g in got])
        crossed, _ = tie(crossed, hold)
        middle_grad, middle_low, gain_two_part = back_call(
            "middle_grad", cot, middle, gain_two, [near[5], near_dx, crossed], 1
        )
        low_rows = send_rows(middle_low)
        flipped = core_flip(middle_low)
        own_grads = weight_grads(0, flipped)
        out_crossed = cross(after(far[3], flipped), far[4])

        def total(i, hold):
            t = after(own_grads[i], hold).astype(F32)
            for z in sent:
                t = t + z[i].astype(F32)
            return t.astype(BF16)

        def reduce_rows(g):
            return lax.psum_scatter(g, "tensor", scatter_dimension=0)

        first_sum = total(0, own_grads[0])
        first_part = reduce_rows(first_sum)
        lows = gather_heads(middle_low, flipped, low_rows, first_sum)
        g, wo_grad = heads_grad_call(o, pack, lows)

        back = []
        for i in range(heads):
            if i == 1:
                near_out = core_flip(after(near[4], g))
                output = output_call(after(middle, back[0][0]), [near[3], near_out, out_crossed])
                moved_output = reshard(output)
                second_sum = total(1, output)
                g, second_sum = tie(g, second_sum)
                second_part = reduce_rows(second_sum)
            elif i:
                g = after(g, back[-1][0])
            if i == heads - 1:
                g, first_part = tie(g, first_part)
            j = i // count
            back.append(
                attend_back_call(q, k, v, bias, o[j], lse[j], g, cos, sin, i, i - j * count)
            )
        wo_grad, _ = tie(wo_grad, back[-1][0])
        dw = qkv_weight_call(wo_grad, back, normed_one, pack.shape)
        pieces = qkv_back_call(after(pack, dw), back, T, d)
        second_part, *pieces = tie(second_part, *pieces)
        slices = jnp.concatenate([first_part[None], second_part])
        slices = lax.all_gather(slices, "dp", axis=0)

        def share_of(k):
            return lax.dynamic_index_in_dim(dw, pair ^ k, 0, keepdims=False)

        travelled = [pair_from(share_of(k), k) for k in range(1, J)]
        arrived = scatter_heads(pieces)
        part = share_of(0).astype(F32)
        for p in travelled:
            part = part + p.astype(F32)
        part = part.astype(BF16)
        home_pairs = [
            ((2 * j + 1) * T + t, 2 * j * T + (t + R) % T) for j in range(J) for t in range(T)
        ]
        moved = lax.ppermute(part, ("dp", "tensor"), home_pairs)
        part = (part.astype(F32) + moved.astype(F32)).astype(BF16)
        part = jnp.where(core == 0, part, core_flip(part))
        shares = [part] + [pair_from(part, k) for k in range(1, J)]

        tokens_low, gain_one_part = back_call(
            "tokens_grad", middle_grad, x, gain_one, arrived, 0
        )
        tokens_grad = reshard(tokens_low)[:, None]
        gains = jnp.concatenate([gain_one_part, gain_two_part], axis=0)
        gains = sum_all(after(gains, part))
        gate_up_grad, down_grad = assemble_call(after(slices, gains))
        qkv_grad, out_grad = unpack_call(after(index, down_grad), shares)
        qkv_grad = qkv_grad.transpose(1, 0, 2)
        return (
            moved_output[:, None], tokens_grad, qkv_grad, out_grad, gate_up_grad, down_grad, gains[0], gains[1]
        )

    return on_device


def solution(mesh):
    return jax.shard_map(
        build(mesh.shape["dp"], mesh.shape["tensor"]),
        mesh=mesh,
        in_specs=(
            P("tensor", "dp", None),
            P(None, None, "tensor"),
            P("tensor", None),
            P(None, None, "tensor"),
            P("tensor", None),
            P(),
            P(),
            P("dp"),
            P(None, "dp"),
            P("tensor", "dp", None),
        ),
        out_specs=(
            P("tensor", "dp", None),
            P("tensor", "dp", None),
            P(None, None, "tensor"),
            P("tensor", None),
            P(None, None, "tensor"),
            P("tensor", None),
            P(),
            P(),
        ),
        check_vma=False,
    )
```

time: 700 us -> 576 us (0.82)
  waiting for transfers between devices: 287 us -> 204 us
  blocking collectives: 59.9 us -> 0 us
  Pallas kernels: 191 us -> 223 us
  local copies, waits for them, and re-layouts: 44.5 us -> 25.5 us
  starting transfers between devices: 67 us -> 77.1 us
  other arithmetic: 32 us -> 22.3 us
    psum x1 -> x0, blocking collectives: 38.5 us -> none  [on_device(): lax.psum(jnp.concatenate([gain_one_part, gain_two_part], axis=0), ('dp',...]
    ppermute x4 -> x5, waiting for transfers between devices: 59.2 us -> 22.1 us  [row_from(): lax.ppermute(x, 'tensor', [(t // R * R + (t % R + k) % R, t) for t in ran...]
    ppermute x4 -> x7, waiting for transfers between devices: 73.8 us -> 41.4 us  [the longest x1 29.9 us: on_device(): moved = lax.ppermute(part, ('dp', 'tensor'), home_pairs)]
    ppermute x26 -> x38, waiting for transfers between devices: 138 us -> 107 us  [over_dp(): return lax.ppermute(x, 'dp', [(i, f(i)) for i in range(DP)])]
    all_gather x5 -> x4, waiting for transfers between devices: 4.11 us -> 33.1 us  [the longest x3 33 us: on_device(): lax.all_gather(z, 'tensor', axis=0)]
    pallas_call x8 -> x13, Pallas kernels: 113 us -> 137 us  [the longest x2 42.3 us: ffn_call(): call(functools.partial(ffn_kernel, groups, steps), 'feed_forward', (shape...]
    all_gather x2 -> x0, blocking collectives: 21.4 us -> none  [the longest x1 11.3 us: reduce_heads(): lax.all_gather(part, 'dp', axis=0, tiled=True, axis_index_groups=same_core)]
    unnamed x74 -> x90, local copies, waits for them, and re-layouts: 27.6 us -> 12.8 us
  transfers between devices with their start and end apart: 47 -> 61, of which waited for: 19 -> 26; matrix products, arithmetic and copies ran while one was open for 5% -> 5% of each run, Pallas kernels for 24% -> 34%
where the time goes in v2:
time: 576 us; the launch traced here: 568 us
  Pallas kernels  223 us (39%)
  waiting for transfers between devices  204 us (35%)
  starting transfers between devices  77.1 us (13%)
  local copies, waits for them, and re-layouts  25.5 us (4%)
  other arithmetic  22.3 us (4%)
  between operations  15.9 us (3%)
    ppermute x38, waiting for transfers between devices, over_dp(): return lax.ppermute(x, 'dp', [(i, f(i)) for i in range(DP)])  107 us
    pallas_call x4, Pallas kernels, attend_back_call(): call(functools.partial(attend_back_kernel, sub=min(256, S)), 'attend_back...  54.4 us
    ppermute x38, starting transfers between devices, over_dp(): return lax.ppermute(x, 'dp', [(i, f(i)) for i in range(DP)])  50.6 us
    pallas_call x2, Pallas kernels, ffn_call(): call(functools.partial(ffn_kernel, groups, steps), 'feed_forward', (shape...  42.3 us
    all_gather x3, waiting for transfers between devices, on_device(): lax.all_gather(z, 'tensor', axis=0)  33 us
    ppermute x1, waiting for transfers between devices, on_device(): moved = lax.ppermute(part, ('dp', 'tensor'), home_pairs)  29.9 us
    pallas_call x2, Pallas kernels, attend_call(): call(functools.partial(attend_kernel, sub=sub), 'attend', (shape((count *...  29 us
    pallas_call x2, Pallas kernels, ffn_weight_call(): call(functools.partial(ffn_weight_kernel, T, us), 'feed_forward_weights',...  24.8 us
  transfers between devices with their start and end apart: 61, of which 26 were waited for; matrix products, arithmetic and copies ran while one was open for 5% of the time, Pallas kernels for 34%

profile of v2, /device:TPU:0, one launch (start us, length us, event | category | flops | bytes accessed | tf_op | source)
XLA Modules:
  0.0 568.0 jit_solution(8418718125696099308)
XLA Ops:
  7.2 2.4 slice_bitcast_fusion
  9.6 5.3 collective-permute-start
  16.4 5.3 collective-permute-start.2
  30.0 1.8 multiply_sine_fusion
  34.5 2.2 norm_tokens.2.refs_0_.refs_12_
  36.7 2.3 norm_tokens.3.refs_4_.refs_16_
  39.1 2.4 collective-permute-start.8
  43.7 18.1 %collective-permute-done.8.refs_2_.refs_14_ = bf16[256,1024]{1,0:T(8,128)(2,1)S(1)} collective-permute-done((bf16[256,1024]{1,0:T(8,128)(2,1)S(1)}, bf16[256,1024]{1,0:T(8,128)(2,1)S(1)}, u32[]{:S(2)}, u32[]{:S(2)}) %collective-permute-start.8) | collective-permute-done | bytes 524320 | tf_op jit(solution)/shard_map/ppermute | solution.py:691
  61.7 15.9 %collective-permute-start.10 = (bf16[256,1024]{1,0:T(8,128)(2,1)}, bf16[256,1024]{1,0:T(8,128)(2,1)S(1)}, u32[]{:S(2)}, u32[]{:S(2)}) collective-permute-start(bf16[256,1024]{1,0:T(8,128)(2,1)} %norm_tokens.3.refs_4_.refs_16_), channel_id=1, source_target_pairs={{0,4},{4,0},{8,12},{12,8},{16,20},{20,16},{24,28},{28,24},{1,5},{5... | collective-permute-start | bytes 1572872 | tf_op jit(solution)/shard_map/ppermute | solution.py:672
  78.9 3.6 pack_heads.1.w_ref
  83.9 2.7 collective-permute-start.12
  86.7 1.9 collective-permute-start.13
  89.4 7.6 %project_heads.1 = (bf16[256,2048]{1,0:T(8,128)(2,1)}, bf16[256,2048]{1,0:T(8,128)(2,1)}, bf16[256,2048]{1,0:T(8,128)(2,1)}) custom-call(f32[32,2048]{1,0:T(8,128)} %get-tuple-element.214.c_ref.ck_ref, f32[32,2048]{1,0:T(8,128)} %get-tuple-element.213.s_ref.sk_ref, bf16[4,4,256,256]{3,2,1,0:T(8,128)(2,1)} %pack_heads.1.w_ref, ...), custom_call_target="tpu_custom_call" | custom-call | flops 2184999936 | tf_op jit(solution)/shard_map/project_heads/pallas_call | solution.py:193
  97.0 14.7 %attend.2 = (bf16[128,2048]{1,0:T(8,128)(2,1)}, f32[2,8,2048]{2,1,0:T(8,128)}) custom-call(bf16[256,2048]{1,0:T(8,128)(2,1)} %get-tuple-element.116.q_ref, bf16[256,2048]{1,0:T(8,128)(2,1)} %get-tuple-element.112.k_ref, bf16[256,2048]{1,0:T(8,128)(2,1)} %get-tuple-element.113.v_ref, bf16[16,2048]{1,0:T(8,128)(2,1)} %concatenate.40.b_ref), custom_call_target="tpu_custom_call" | custom-call | flops 4255000064 | tf_op jit(solution)/shard_map/attend/pallas_call | solution.py:249
  111.7 14.4 %attend.3 = (bf16[128,2048]{1,0:T(8,128)(2,1)}, f32[2,8,2048]{2,1,0:T(8,128)}) custom-call(bf16[256,2048]{1,0:T(8,128)(2,1)} %get-tuple-element.116.q_ref, bf16[256,2048]{1,0:T(8,128)(2,1)} %get-tuple-element.112.k_ref, bf16[256,2048]{1,0:T(8,128)(2,1)} %get-tuple-element.113.v_ref, bf16[16,2048]{1,0:T(8,128)(2,1)} %concatenate.40.b_ref), custom_call_target="tpu_custom_call" | custom-call | flops 4255000064 | tf_op jit(solution)/shard_map/attend/pallas_call | solution.py:249
  126.0 4.2 output_projection.1
  130.3 6.9 %collective-permute-start.15 = (bf16[512,1024]{1,0:T(8,128)(2,1)}, bf16[512,1024]{1,0:T(8,128)(2,1)S(1)}, u32[]{:S(2)}, u32[]{:S(2)}) collective-permute-start(bf16[512,1024]{1,0:T(8,128)(2,1)} %get-tuple-element.123), channel_id=1, source_target_pairs={{0,4},{4,0},{8,12},{12,8},{16,20},{20,16},{24,28},{28,24},{1,5},{5... | collective-permute-start | bytes 3145736 | tf_op jit(solution)/shard_map/ppermute | solution.py:672
  137.3 2.4 collective-permute-done.15
  139.7 2.6 add_convert_fusion.5
  147.5 33.0 %all-gather.13.cloned.1.call-done = bf16[512,1024]{1,0:T(8,128)(2,1)} async-done(((bf16[128,1024]{1,0:T(8,128)(2,1)}), bf16[512,1024]{1,0:T(8,128)(2,1)}) %all-gather.13.cloned.1.call-update) | async-done | bytes 1048592 | tf_op jit(solution)/shard_map/all_gather | solution.py:805
  180.6 1.7 collective-permute-start.21
  182.3 2.6 collective-permute-done.16.refs_2_
  184.9 4.9 middle_norm.1
  192.0 21.9 %collective-permute-done.21.refs_9_ = bf16[4,128,1024]{2,1,0:T(8,128)(2,1)S(1)} collective-permute-done((bf16[4,128,1024]{2,1,0:T(8,128)(2,1)}, bf16[4,128,1024]{2,1,0:T(8,128)(2,1)S(1)}, u32[]{:S(2)}, u32[]{:S(2)}) %collective-permute-start.21) | collective-permute-done | bytes 1048608 | tf_op jit(solution)/shard_map/ppermute | solution.py:672
  215.9 21.1 %feed_forward.2 = (bf16[1024,1024]{1,0:T(8,128)(2,1)}, bf16[1024,1024]{1,0:T(8,128)(2,1)}, bf16[1024,1024]{1,0:T(8,128)(2,1)}, bf16[512,1024]{1,0:T(8,128)(2,1)}...) custom-call(bf16[512,1024]{1,0:T(8,128)(2,1)} %get-tuple-element.148.refs_0_, ...), custom_call_target="tpu_custom_call" | custom-call | flops 6037499904 | tf_op jit(solution)/shard_map/feed_forward/pallas_call | solution.py:579
  238.0 2.6 collective-permute-done.23.refs_1_
  243.8 21.1 %feed_forward.3 = (bf16[1024,1024]{1,0:T(8,128)(2,1)}, bf16[1024,1024]{1,0:T(8,128)(2,1)}, bf16[1024,1024]{1,0:T(8,128)(2,1)}, bf16[512,1024]{1,0:T(8,128)(2,1)}...) custom-call(bf16[512,1024]{1,0:T(8,128)(2,1)} %copy-done.7, ...), custom_call_target="tpu_custom_call" | custom-call | flops 6037499904 | tf_op jit(solution)/shard_map/feed_forward/pallas_call | solution.py:579
  265.1 2.7 collective-permute-done.27
  267.9 1.6 add_convert_fusion.4
  271.1 12.2 %feed_forward_weights.2 = (bf16[4,1024,128]{2,1,0:T(8,128)(2,1)}, bf16[4,2,1024,128]{3,2,1,0:T(8,128)(2,1)}) custom-call(bf16[512,1024]{1,0:T(8,128)(2,1)} %get-tuple-element.148.refs_0_, bf16[512,1024]{1,0:T(8,128)(2,1)} %copy-done.5, bf16[512,1024]{1,0:T(8,128)(2,1)} %copy-done.7, bf16[512,1024]{1,0:T(8,128)(2,1)} %copy-done.9, ...), custom_call_target="tpu_custom_call" | custom-call | flops 3564999936 | tf_op jit(solution)/shard_map/feed_forward_weights/pallas_call | solution.py:618
  283.2 11.5 %collective-permute-done.28.refs_2_ = bf16[512,1024]{1,0:T(8,128)(2,1)S(1)} collective-permute-done((bf16[512,1024]{1,0:T(8,128)(2,1)S(1)}, bf16[512,1024]{1,0:T(8,128)(2,1)S(1)}, u32[]{:S(2)}, u32[]{:S(2)}) %collective-permute-start.28) | collective-permute-done | bytes 1048608 | tf_op jit(solution)/shard_map/ppermute | solution.py:672
  295.8 5.9 %middle_grad.1 = (f32[512,1024]{1,0:T(8,128)}, bf16[512,1024]{1,0:T(8,128)(2,1)}, f32[1,1024]{1,0:T(1,128)}) custom-call(bf16[512,1024]{1,0:T(8,128)(2,1)} %copy-done.2, f32[512,1024]{1,0:T(8,128)} %get-tuple-element.153.x_ref.m_ref, f32[1,1024]{1,0:T(1,128)} %bitcast.73, bf16[512,1024]{1,0:T(8,128)(2,1)} %get-tuple-element.132.refs_0_, ...), custom_call_target="tpu_custom_call" | custom-call | flops 1581250048 | tf_op jit(solution)/shard_map/middle_grad/pallas_call | solution.py:121
  304.6 12.6 %feed_forward_weights.3 = (bf16[4,1024,128]{2,1,0:T(8,128)(2,1)}, bf16[4,2,1024,128]{3,2,1,0:T(8,128)(2,1)}) custom-call(bf16[512,1024]{1,0:T(8,128)(2,1)} %get-tuple-element.148.refs_0_, bf16[512,1024]{1,0:T(8,128)(2,1)} %copy-done.5, bf16[512,1024]{1,0:T(8,128)(2,1)} %copy-done.7, bf16[512,1024]{1,0:T(8,128)(2,1)} %copy-done.9, ...), custom_call_target="tpu_custom_call" | custom-call | flops 3564999936 | tf_op jit(solution)/shard_map/feed_forward_weights/pallas_call | solution.py:618
  317.3 10.1 %collective-permute-done.31 = bf16[4,1024,128]{2,1,0:T(8,128)(2,1)S(1)} collective-permute-done((bf16[4,1024,128]{2,1,0:T(8,128)(2,1)S(1)}, bf16[4,1024,128]{2,1,0:T(8,128)(2,1)S(1)}, u32[]{:S(2)}, u32[]{:S(2)}) %collective-permute-start.31) | collective-permute-done | bytes 1048608 | tf_op jit(solution)/shard_map/ppermute | solution.py:672
  327.3 2.5 add_convert_fusion.3
  331.5 1.6 add_convert_fusion.2
  335.7 6.1 %heads_grad.1 = (bf16[256,2048]{1,0:T(8,128)(2,1)}, bf16[4,256,256]{2,1,0:T(8,128)(2,1)}) custom-call(bf16[4,4,256,256]{3,2,1,0:T(8,128)(2,1)} %pack_heads.1.w_ref, bf16[128,2048]{1,0:T(8,128)(2,1)} %get-tuple-element.115.refs_0_.o_ref, bf16[128,2048]{1,0:T(8,128)(2,1)} %get-tuple-element.119.refs_1_.o_ref, bf16[512,1024]{1,0:T(8,128)(2,1)} %get-tuple-element.147.refs_2_, ...), custom_call_target="tpu_custom_call" | custom-call | flops 1724999936 | tf_op jit(solution)/shard_map/heads_grad/pallas_call | solution.py:408
  341.8 13.5 %attend_back.4 = (bf16[64,2048]{1,0:T(8,128)(2,1)}, bf16[64,2048]{1,0:T(8,128)(2,1)}, bf16[64,2048]{1,0:T(8,128)(2,1)}) custom-call(bf16[256,2048]{1,0:T(8,128)(2,1)} %get-tuple-element.116.q_ref, bf16[256,2048]{1,0:T(8,128)(2,1)} %get-tuple-element.112.k_ref, bf16[256,2048]{1,0:T(8,128)(2,1)} %get-tuple-element.113.v_ref, ...), custom_call_target="tpu_custom_call" | custom-call | flops 3536250112 | tf_op jit(solution)/shard_map/attend_back/pallas_call | solution.py:322
  355.2 3.2 collective-permute-done.35.refs_2_
  359.7 3.6 output_sum.1
  363.4 14.8 %collective-permute-done.37 = bf16[4,2,1024,128]{3,2,1,0:T(8,128)(2,1)} collective-permute-done((bf16[4,2,1024,128]{3,2,1,0:T(8,128)(2,1)}, bf16[4,2,1024,128]{3,2,1,0:T(8,128)(2,1)}, u32[]{:S(2)}, u32[]{:S(2)}) %collective-permute-start.37) | collective-permute-done | bytes 2097184 | tf_op jit(solution)/shard_map/ppermute | solution.py:672
  378.2 3.5 add_convert_fusion
  381.7 13.7 %attend_back.5 = (bf16[64,2048]{1,0:T(8,128)(2,1)}, bf16[64,2048]{1,0:T(8,128)(2,1)}, bf16[64,2048]{1,0:T(8,128)(2,1)}) custom-call(bf16[256,2048]{1,0:T(8,128)(2,1)} %get-tuple-element.116.q_ref, bf16[256,2048]{1,0:T(8,128)(2,1)} %get-tuple-element.112.k_ref, bf16[256,2048]{1,0:T(8,128)(2,1)} %get-tuple-element.113.v_ref, ...), custom_call_target="tpu_custom_call" | custom-call | flops 3536250112 | tf_op jit(solution)/shard_map/attend_back/pallas_call | solution.py:322
  395.4 13.5 %attend_back.6 = (bf16[64,2048]{1,0:T(8,128)(2,1)}, bf16[64,2048]{1,0:T(8,128)(2,1)}, bf16[64,2048]{1,0:T(8,128)(2,1)}) custom-call(bf16[256,2048]{1,0:T(8,128)(2,1)} %get-tuple-element.116.q_ref, bf16[256,2048]{1,0:T(8,128)(2,1)} %get-tuple-element.112.k_ref, bf16[256,2048]{1,0:T(8,128)(2,1)} %get-tuple-element.113.v_ref, ...), custom_call_target="tpu_custom_call" | custom-call | flops 3536250112 | tf_op jit(solution)/shard_map/attend_back/pallas_call | solution.py:322
  408.9 13.7 %attend_back.7 = (bf16[64,2048]{1,0:T(8,128)(2,1)}, bf16[64,2048]{1,0:T(8,128)(2,1)}, bf16[64,2048]{1,0:T(8,128)(2,1)}) custom-call(bf16[256,2048]{1,0:T(8,128)(2,1)} %get-tuple-element.116.q_ref, bf16[256,2048]{1,0:T(8,128)(2,1)} %get-tuple-element.112.k_ref, bf16[256,2048]{1,0:T(8,128)(2,1)} %get-tuple-element.113.v_ref, ...), custom_call_target="tpu_custom_call" | custom-call | flops 3536250112 | tf_op jit(solution)/shard_map/attend_back/pallas_call | solution.py:322
  422.7 8.1 %qkv_weights.1 = bf16[4,4,256,256]{3,2,1,0:T(8,128)(2,1)} custom-call(bf16[4,256,256]{2,1,0:T(8,128)(2,1)} %get-tuple-element.174.wo_ref, bf16[64,2048]{1,0:T(8,128)(2,1)} %get-tuple-element.152.refs_0_, bf16[64,2048]{1,0:T(8,128)(2,1)} %get-tuple-element.175.refs_1_, bf16[64,2048]{1,0:T(8,128)(2,1)} %get-tuple-element.176.refs_2_, ...), custom_call_target="tpu_custom_call" | custom-call | flops 2300000000 | tf_op jit(solution)/shard_map/qkv_weights/pallas_call | solution.py:464
  430.8 7.0 %qkv_back.1 = (bf16[512,1024]{1,0:T(8,128)(2,1)}, bf16[512,1024]{1,0:T(8,128)(2,1)}, bf16[512,1024]{1,0:T(8,128)(2,1)}, bf16[512,1024]{1,0:T(8,128)(2,1)}) custom-call(bf16[4,4,256,256]{3,2,1,0:T(8,128)(2,1)} %pack_heads.1.w_ref, bf16[64,2048]{1,0:T(8,128)(2,1)} %get-tuple-element.152.refs_0_, bf16[64,2048]{1,0:T(8,128)(2,1)} %get-tuple-element.175.refs_1_, ...), custom_call_target="tpu_custom_call" | custom-call | flops 2012499968 | tf_op jit(solution)/shard_map/qkv_back/pallas_call | solution.py:437
  437.8 2.1 pad_maximum_fusion
  444.8 1.6 add_convert_fusion.1
  447.6 13.4 %collective-permute-done.42 = bf16[4,256,256]{2,1,0:T(8,128)(2,1)} collective-permute-done((bf16[4,256,256]{2,1,0:T(8,128)(2,1)}, bf16[4,256,256]{2,1,0:T(8,128)(2,1)}, u32[]{:S(2)}, u32[]{:S(2)}) %collective-permute-start.42) | collective-permute-done | bytes 524320 | tf_op jit(solution)/shard_map/ppermute | solution.py:672
  461.0 5.1 collective-permute-done.43
  466.1 10.4 %collective-permute-done.44 = bf16[4,256,256]{2,1,0:T(8,128)(2,1)} collective-permute-done((bf16[4,256,256]{2,1,0:T(8,128)(2,1)}, bf16[4,256,256]{2,1,0:T(8,128)(2,1)}, u32[]{:S(2)}, u32[]{:S(2)}) %collective-permute-start.44) | collective-permute-done | bytes 524320 | tf_op jit(solution)/shard_map/ppermute | solution.py:672
  476.5 1.6 fusion.2
  479.5 1.9 collective-permute-start.36
  481.3 29.9 %collective-permute-done.45 = bf16[4,256,256]{2,1,0:T(8,128)(2,1)S(1)} collective-permute-done((bf16[4,256,256]{2,1,0:T(8,128)(2,1)S(1)}, bf16[4,256,256]{2,1,0:T(8,128)(2,1)S(1)}, u32[]{:S(2)}, u32[]{:S(2)}) %collective-permute-start.45) | collective-permute-done | bytes 524320 | tf_op jit(solution)/shard_map/ppermute | solution.py:906
  512.8 5.1 tokens_grad.1
  517.9 1.9 collective-permute-start.41
  520.6 1.7 collective-permute-start.47
  524.5 2.2 collective-permute-done.48
  527.3 3.2 collective-permute-done.49
  532.4 6.9 %collective-permute-done.50 = f32[2,1024]{1,0:T(2,128)S(1)} collective-permute-done((f32[2,1024]{1,0:T(2,128)S(1)}, f32[2,1024]{1,0:T(2,128)S(1)}, u32[]{:S(2)}, u32[]{:S(2)}) %collective-permute-start.50) | collective-permute-done | bytes 8224 | tf_op jit(solution)/shard_map/ppermute | solution.py:732
  541.1 4.5 collective-permute-done.51
  546.2 8.2 %feed_forward_gradients.1 = (f32[1024,2,1024]{2,1,0:T(2,128)}, f32[1024,1024]{1,0:T(8,128)}) custom-call(bf16[8,3,1024,128]{3,2,1,0:T(8,128)(2,1)} %bitcast.77), custom_call_target="tpu_custom_call" | custom-call | flops 2300000000 | tf_op jit(solution)/shard_map/feed_forward_gradients/pallas_call | solution.py:644
  554.9 3.8 unpack_heads.1
  (219 shorter events, 61.4 us)
Async XLA Ops:
  7.2 136.0 %all-gather.9.cloned.1.call-start = ((), (), s32[]{:S(2)}) async-start(), calls=%async_computation.4 | async-start | bytes 1310720 | tf_op jit(solution)/shard_map/all_gather | solution.py:805
  9.6 24.2 %collective-permute-start = (bf16[256,1024]{1,0:T(8,128)(2,1)}, bf16[256,1024]{1,0:T(8,128)(2,1)}, u32[]{:S(2)}, u32[]{:S(2)}) collective-permute-start(bf16[256,1024]{1,0:T(8,128)(2,1)} %get-tuple-element.210), channel_id=1, source_target_pairs={{0,0},{1,1},{2,4},{3,5},{4,2},{5,3},{6,6},{7,7},{8,8},{9,9},{10,12... | collective-permute-start | bytes 1572872 | tf_op jit(solution)/shard_map/ppermute | solution.py:701
  15.7 16.8 %collective-permute-start.1 = (bf16[2048]{0:T(1024)(128)(2,1)S(1)}, bf16[2048]{0:T(1024)(128)(2,1)}, u32[]{:S(2)}, u32[]{:S(2)}) collective-permute-start(bf16[2048]{0:T(1024)(128)(2,1)S(1)} %fusion.4), channel_id=1, source_target_pairs={{0,4},{4,0},{8,12},{12,8},{16,20},{20,16},{24,28},{28,24},{1,5},{5... | collective-permute-start | bytes 12296 | tf_op jit(solution)/shard_map/ppermute | solution.py:672
  16.4 20.3 %collective-permute-start.2 = (bf16[256,1024]{1,0:T(8,128)(2,1)}, bf16[256,1024]{1,0:T(8,128)(2,1)}, u32[]{:S(2)}, u32[]{:S(2)}) collective-permute-start(bf16[256,1024]{1,0:T(8,128)(2,1)} %get-tuple-element.209), channel_id=1, source_target_pairs={{0,0},{1,1},{2,4},{3,5},{4,2},{5,3},{6,6},{7,7},{8,8},{9,9},{10,12... | collective-permute-start | bytes 1572872 | tf_op jit(solution)/shard_map/ppermute | solution.py:701
  33.8 7.6 %collective-permute-start.3 = (bf16[4,256,256]{2,1,0:T(8,128)(2,1)S(1)}, bf16[4,256,256]{2,1,0:T(8,128)(2,1)S(1)}, u32[]{:S(2)}, u32[]{:S(2)}) collective-permute-start(bf16[4,256,256]{2,1,0:T(8,128)(2,1)S(1)} %pad_maximum_fusion.1), channel_id=1, source_target_pairs={{4,6},{5,7},{6,4},{7,5},{12,14},{13,15},{14,12},{15,13},{20,22},{2... | collective-permute-start | bytes 1572872 | tf_op jit(solution)/shard_map/ppermute | solution.py:763
  39.0 107.9 %all-gather.11.cloned.1.call-start = ((), (), s32[]{:S(2)}) async-start(), calls=%async_computation.5 | async-start | bytes 1310720 | tf_op jit(solution)/shard_map/all_gather | solution.py:805
  39.1 22.7 %collective-permute-start.8 = (bf16[256,1024]{1,0:T(8,128)(2,1)S(1)}, bf16[256,1024]{1,0:T(8,128)(2,1)S(1)}, u32[]{:S(2)}, u32[]{:S(2)}) collective-permute-start(bf16[256,1024]{1,0:T(8,128)(2,1)S(1)} %copy-done.25), channel_id=1, source_target_pairs={{1,0},{0,1},{3,2},{2,3},{5,4},{4,5},{7,6},{6,7},{9,8},{8,9},{11,10... | collective-permute-start | bytes 1572872 | tf_op jit(solution)/shard_map/ppermute | solution.py:691
  41.5 36.7 %copy-start.29 = (bf16[4,256,256]{2,1,0:T(8,128)(2,1)}, bf16[4,256,256]{2,1,0:T(8,128)(2,1)S(1)}, u32[]{:S(2)}) copy-start(bf16[4,256,256]{2,1,0:T(8,128)(2,1)S(1)} %collective-permute-done.3.refs_0_) | copy-start | bytes 1572868
  41.5 36.2 %collective-permute-start.4 = (bf16[4,256,256]{2,1,0:T(8,128)(2,1)S(1)}, bf16[4,256,256]{2,1,0:T(8,128)(2,1)S(1)}, u32[]{:S(2)}, u32[]{:S(2)}) collective-permute-start(bf16[4,256,256]{2,1,0:T(8,128)(2,1)S(1)} %collective-permute-done.3.refs_0_), channel_id=1, source_target_pairs={{4,12},{12,4},{20,28},{28,20},{5,13},{13,5},{21,29},{29,21},{6,14}... | collective-permute-start | bytes 1572872 | tf_op jit(solution)/shard_map/ppermute | solution.py:765
  42.2 35.6 %collective-permute-start.5 = (bf16[4,256,256]{2,1,0:T(8,128)(2,1)S(1)}, bf16[4,256,256]{2,1,0:T(8,128)(2,1)S(1)}, u32[]{:S(2)}, u32[]{:S(2)}) collective-permute-start(bf16[4,256,256]{2,1,0:T(8,128)(2,1)S(1)} %collective-permute-done.3.refs_0_), channel_id=1, source_target_pairs={{4,20},{12,28},{20,4},{28,12},{5,21},{13,29},{21,5},{29,13},{6,22}... | collective-permute-start | bytes 1572872 | tf_op jit(solution)/shard_map/ppermute | solution.py:765
  42.9 35.3 %collective-permute-start.6 = (bf16[4,256,256]{2,1,0:T(8,128)(2,1)S(1)}, bf16[4,256,256]{2,1,0:T(8,128)(2,1)S(1)}, u32[]{:S(2)}, u32[]{:S(2)}) collective-permute-start(bf16[4,256,256]{2,1,0:T(8,128)(2,1)S(1)} %collective-permute-done.3.refs_0_), channel_id=1, source_target_pairs={{4,28},{12,20},{20,12},{28,4},{5,29},{13,21},{21,13},{29,5},{6,30}... | collective-permute-start | bytes 1572872 | tf_op jit(solution)/shard_map/ppermute | solution.py:765
  43.6 40.4 %collective-permute-start.11 = (bf16[256,1024]{1,0:T(8,128)(2,1)}, bf16[256,1024]{1,0:T(8,128)(2,1)S(1)}, u32[]{:S(2)}, u32[]{:S(2)}) collective-permute-start(bf16[256,1024]{1,0:T(8,128)(2,1)} %norm_tokens.3.refs_4_.refs_16_), channel_id=1, source_target_pairs={{1,0},{0,1},{3,2},{2,3},{5,4},{4,5},{7,6},{6,7},{9,8},{8,9},{11,10... | collective-permute-start | bytes 1572872 | tf_op jit(solution)/shard_map/ppermute | solution.py:691
  61.7 26.9 %collective-permute-start.10 = (bf16[256,1024]{1,0:T(8,128)(2,1)}, bf16[256,1024]{1,0:T(8,128)(2,1)S(1)}, u32[]{:S(2)}, u32[]{:S(2)}) collective-permute-start(bf16[256,1024]{1,0:T(8,128)(2,1)} %norm_tokens.3.refs_4_.refs_16_), channel_id=1, source_target_pairs={{0,4},{4,0},{8,12},{12,8},{16,20},{20,16},{24,28},{28,24},{1,5},{5... | collective-permute-start | bytes 1572872 | tf_op jit(solution)/shard_map/ppermute | solution.py:672
  77.6 11.0 %collective-permute-start.7 = (bf16[256,1024]{1,0:T(8,128)(2,1)S(1)}, bf16[256,1024]{1,0:T(8,128)(2,1)}, u32[]{:S(2)}, u32[]{:S(2)}) collective-permute-start(bf16[256,1024]{1,0:T(8,128)(2,1)S(1)} %copy-done.25), channel_id=1, source_target_pairs={{0,4},{4,0},{8,12},{12,8},{16,20},{20,16},{24,28},{28,24},{1,5},{5... | collective-permute-start | bytes 1572872 | tf_op jit(solution)/shard_map/ppermute | solution.py:672
  77.7 10.9 %collective-permute-start.9 = (bf16[256,1024]{1,0:T(8,128)(2,1)S(1)}, bf16[256,1024]{1,0:T(8,128)(2,1)}, u32[]{:S(2)}, u32[]{:S(2)}) collective-permute-start(bf16[256,1024]{1,0:T(8,128)(2,1)S(1)} %collective-permute-done.8.refs_2_.refs_14_), channel_id=1, source_target_pairs={{0,4},{4,0},{8,12},{12,8},{16,20},{20,16},{24,28},{28,24},{1,5},{5... | collective-permute-start | bytes 1572872 | tf_op jit(solution)/shard_map/ppermute | solution.py:672
  83.9 4.7 collective-permute-start.12
  86.7 39.4 %collective-permute-start.13 = (bf16[512,1024]{1,0:T(8,128)(2,1)}, bf16[512,1024]{1,0:T(8,128)(2,1)S(1)}, u32[]{:S(2)}, u32[]{:S(2)}) collective-permute-start(bf16[512,1024]{1,0:T(8,128)(2,1)} %bitcast.25), channel_id=1, source_target_pairs={{0,0},{1,1},{2,4},{3,5},{4,2},{5,3},{6,6},{7,7},{8,8},{9,9},{10,12... | collective-permute-start | bytes 3145736 | tf_op jit(solution)/shard_map/ppermute | solution.py:701
  88.6 92.0 %all-gather.13.cloned.1.call-start = ((), (), s32[]{:S(2)}) async-start(), calls=%async_computation.6 | async-start | bytes 1310720 | tf_op jit(solution)/shard_map/all_gather | solution.py:805
  126.0 63.8 %copy-start.2 = (bf16[512,1024]{1,0:T(8,128)(2,1)}, bf16[512,1024]{1,0:T(8,128)(2,1)S(1)}, u32[]{:S(2)}) copy-start(bf16[512,1024]{1,0:T(8,128)(2,1)S(1)} %collective-permute-done.13.refs_2_.refs_4_.base_ref) | copy-start | bytes 3145732
  130.3 9.4 %collective-permute-start.15 = (bf16[512,1024]{1,0:T(8,128)(2,1)}, bf16[512,1024]{1,0:T(8,128)(2,1)S(1)}, u32[]{:S(2)}, u32[]{:S(2)}) collective-permute-start(bf16[512,1024]{1,0:T(8,128)(2,1)} %get-tuple-element.123), channel_id=1, source_target_pairs={{0,4},{4,0},{8,12},{12,8},{16,20},{20,16},{24,28},{28,24},{1,5},{5... | collective-permute-start | bytes 3145736 | tf_op jit(solution)/shard_map/ppermute | solution.py:672
  137.2 271.7 %reduce-scatter.5.cloned.1.call-start = ((), (), s32[]{:S(2)}) async-start(), calls=%async_computation.3 | async-start | bytes 1310720 | tf_op jit(solution)/shard_map/reduce_scatter | solution.py:863
  137.2 43.3 %collective-permute-start.14 = (bf16[512,1024]{1,0:T(8,128)(2,1)}, bf16[512,1024]{1,0:T(8,128)(2,1)}, u32[]{:S(2)}, u32[]{:S(2)}) collective-permute-start(bf16[512,1024]{1,0:T(8,128)(2,1)} %get-tuple-element.121), channel_id=1, source_target_pairs={{0,4},{4,0},{8,12},{12,8},{16,20},{20,16},{24,28},{28,24},{1,5},{5... | collective-permute-start | bytes 3145736 | tf_op jit(solution)/shard_map/ppermute | solution.py:672
  142.3 42.6 %collective-permute-start.16 = (bf16[512,1024]{1,0:T(8,128)(2,1)}, bf16[512,1024]{1,0:T(8,128)(2,1)}, u32[]{:S(2)}, u32[]{:S(2)}) collective-permute-start(bf16[512,1024]{1,0:T(8,128)(2,1)} %add_convert_fusion.5), channel_id=1, source_target_pairs={{1,0},{0,1},{3,2},{2,3},{5,4},{4,5},{7,6},{6,7},{9,8},{8,9},{11,10... | collective-permute-start | bytes 3145736 | tf_op jit(solution)/shard_map/ppermute | solution.py:691
  143.2 46.7 %collective-permute-start.18 = (bf16[512,1024]{1,0:T(8,128)(2,1)S(1)}, bf16[512,1024]{1,0:T(8,128)(2,1)S(1)}, u32[]{:S(2)}, u32[]{:S(2)}) collective-permute-start(bf16[512,1024]{1,0:T(8,128)(2,1)S(1)} %collective-permute-done.13.refs_2_.refs_4_.base_ref), channel_id=1, source_target_pairs={{0,4},{4,0},{8,12},{12,8},{16,20},{20,16},{24,28},{28,24},{1,5},{5... | collective-permute-start | bytes 3145736 | tf_op jit(solution)/shard_map/ppermute | solution.py:672
  143.2 48.2 %collective-permute-start.19 = (bf16[4,128,1024]{2,1,0:T(8,128)(2,1)}, bf16[4,128,1024]{2,1,0:T(8,128)(2,1)}, u32[]{:S(2)}, u32[]{:S(2)}) collective-permute-start(bf16[4,128,1024]{2,1,0:T(8,128)(2,1)} %bitcast.78), channel_id=1, source_target_pairs={{0,8},{4,12},{8,0},{12,4},{16,24},{20,28},{24,16},{28,20},{1,9},{5... | collective-permute-start | bytes 3145736 | tf_op jit(solution)/shard_map/ppermute | solution.py:672
  146.9 38.0 %copy-start.10 = (bf16[512,1024]{1,0:T(8,128)(2,1)}, bf16[512,1024]{1,0:T(8,128)(2,1)S(1)}, u32[]{:S(2)}) copy-start(bf16[512,1024]{1,0:T(8,128)(2,1)S(1)} %constant_dynamic-update-slice_fusion.x_ref) | copy-start | bytes 3145732
  146.9 45.0 %collective-permute-start.20 = (bf16[4,128,1024]{2,1,0:T(8,128)(2,1)}, bf16[4,128,1024]{2,1,0:T(8,128)(2,1)}, u32[]{:S(2)}, u32[]{:S(2)}) collective-permute-start(bf16[4,128,1024]{2,1,0:T(8,128)(2,1)} %bitcast.81), channel_id=1, source_target_pairs={{0,8},{4,12},{8,0},{12,4},{16,24},{20,28},{24,16},{28,20},{1,9},{5... | collective-permute-start | bytes 3145736 | tf_op jit(solution)/shard_map/ppermute | solution.py:672
  180.6 33.3 %collective-permute-start.21 = (bf16[4,128,1024]{2,1,0:T(8,128)(2,1)}, bf16[4,128,1024]{2,1,0:T(8,128)(2,1)S(1)}, u32[]{:S(2)}, u32[]{:S(2)}) collective-permute-start(bf16[4,128,1024]{2,1,0:T(8,128)(2,1)} %bitcast.84), channel_id=1, source_target_pairs={{0,8},{4,12},{8,0},{12,4},{16,24},{20,28},{24,16},{28,20},{1,9},{5... | collective-permute-start | bytes 3145736 | tf_op jit(solution)/shard_map/ppermute | solution.py:672
  189.8 24.1 %collective-permute-start.17 = (bf16[512,1024]{1,0:T(8,128)(2,1)}, bf16[512,1024]{1,0:T(8,128)(2,1)S(1)}, u32[]{:S(2)}, u32[]{:S(2)}) collective-permute-start(bf16[512,1024]{1,0:T(8,128)(2,1)} %get-tuple-element.148.refs_0_), channel_id=1, source_target_pairs={{0,4},{4,0},{8,12},{12,8},{16,20},{20,16},{24,28},{28,24},{1,5},{5... | collective-permute-start | bytes 3145736 | tf_op jit(solution)/shard_map/ppermute | solution.py:672
  189.9 47.3 %collective-permute-start.25 = (bf16[512,1024]{1,0:T(8,128)(2,1)S(1)}, bf16[512,1024]{1,0:T(8,128)(2,1)S(1)}, u32[]{:S(2)}, u32[]{:S(2)}) collective-permute-start(bf16[512,1024]{1,0:T(8,128)(2,1)S(1)} %collective-permute-done.13.refs_2_.refs_4_.base_ref), channel_id=1, source_target_pairs={{0,16},{4,20},{8,24},{12,28},{16,0},{20,4},{24,8},{28,12},{1,17},{... | collective-permute-start | bytes 3145736 | tf_op jit(solution)/shard_map/ppermute | solution.py:672
  191.4 46.5 %collective-permute-start.22 = (bf16[512,1024]{1,0:T(8,128)(2,1)}, bf16[512,1024]{1,0:T(8,128)(2,1)S(1)}, u32[]{:S(2)}, u32[]{:S(2)}) collective-permute-start(bf16[512,1024]{1,0:T(8,128)(2,1)} %get-tuple-element.148.refs_0_), channel_id=1, source_target_pairs={{0,16},{4,20},{8,24},{12,28},{16,0},{20,4},{24,8},{28,12},{1,17},{... | collective-permute-start | bytes 3145736 | tf_op jit(solution)/shard_map/ppermute | solution.py:672
  237.1 3.4 collective-permute-start.23
  237.2 4.1 collective-permute-start.26
  238.0 4.9 collective-permute-start.24
  264.9 2.9 collective-permute-start.27
  269.5 25.3 %collective-permute-start.28 = (bf16[512,1024]{1,0:T(8,128)(2,1)S(1)}, bf16[512,1024]{1,0:T(8,128)(2,1)S(1)}, u32[]{:S(2)}, u32[]{:S(2)}) collective-permute-start(bf16[512,1024]{1,0:T(8,128)(2,1)S(1)} %add_convert_fusion.4), channel_id=1, source_target_pairs={{0,16},{4,20},{8,24},{12,28},{16,0},{20,4},{24,8},{28,12},{1,17},{... | collective-permute-start | bytes 3145736 | tf_op jit(solution)/shard_map/ppermute | solution.py:672
  301.7 2.9 collective-permute-start.29
  301.8 25.6 %collective-permute-start.31 = (bf16[4,1024,128]{2,1,0:T(8,128)(2,1)S(1)}, bf16[4,1024,128]{2,1,0:T(8,128)(2,1)S(1)}, u32[]{:S(2)}, u32[]{:S(2)}) collective-permute-start(bf16[4,1024,128]{2,1,0:T(8,128)(2,1)S(1)} %copy-done.41), channel_id=1, source_target_pairs={{0,8},{4,12},{8,0},{12,4},{16,24},{20,28},{24,16},{28,20},{1,9},{5... | collective-permute-start | bytes 3145736 | tf_op jit(solution)/shard_map/ppermute | solution.py:672
  303.3 26.5 %collective-permute-start.30 = (bf16[512,1024]{1,0:T(8,128)(2,1)}, bf16[512,1024]{1,0:T(8,128)(2,1)S(1)}, u32[]{:S(2)}, u32[]{:S(2)}) collective-permute-start(bf16[512,1024]{1,0:T(8,128)(2,1)} %get-tuple-element.147.refs_2_), channel_id=1, source_target_pairs={{1,0},{0,1},{3,2},{2,3},{5,4},{4,5},{7,6},{6,7},{9,8},{8,9},{11,10... | collective-permute-start | bytes 3145736 | tf_op jit(solution)/shard_map/ppermute | solution.py:691
  304.5 27.0 %collective-permute-start.34 = (bf16[512,1024]{1,0:T(8,128)(2,1)}, bf16[512,1024]{1,0:T(8,128)(2,1)}, u32[]{:S(2)}, u32[]{:S(2)}) collective-permute-start(bf16[512,1024]{1,0:T(8,128)(2,1)} %get-tuple-element.159), channel_id=1, source_target_pairs={{0,4},{4,0},{8,12},{12,8},{16,20},{20,16},{24,28},{28,24},{1,5},{5... | collective-permute-start | bytes 3145736 | tf_op jit(solution)/shard_map/ppermute | solution.py:672
  329.8 4.9 collective-permute-start.32
  329.8 48.4 %collective-permute-start.37 = (bf16[4,2,1024,128]{3,2,1,0:T(8,128)(2,1)}, bf16[4,2,1024,128]{3,2,1,0:T(8,128)(2,1)}, u32[]{:S(2)}, u32[]{:S(2)}) collective-permute-start(bf16[4,2,1024,128]{3,2,1,0:T(8,128)(2,1)} %get-tuple-element.163), channel_id=1, source_target_pairs={{0,8},{4,12},{8,0},{12,4},{16,24},{20,28},{24,16},{28,20},{1,9},{5... | collective-permute-start | bytes 6291464 | tf_op jit(solution)/shard_map/ppermute | solution.py:672
  331.4 106.4 %reduce-scatter.3.cloned.1.call-start = ((), (), s32[]{:S(2)}) async-start(), calls=%async_computation.2 | async-start | bytes 2621440 | tf_op jit(solution)/shard_map/reduce_scatter | solution.py:863
  333.1 25.3 %collective-permute-start.35 = (bf16[512,1024]{1,0:T(8,128)(2,1)S(1)}, bf16[512,1024]{1,0:T(8,128)(2,1)S(1)}, u32[]{:S(2)}, u32[]{:S(2)}) collective-permute-start(bf16[512,1024]{1,0:T(8,128)(2,1)S(1)} %add_convert_fusion.2), channel_id=1, source_target_pairs={{0,16},{4,20},{8,24},{12,28},{16,0},{20,4},{24,8},{28,12},{1,17},{... | collective-permute-start | bytes 3145736 | tf_op jit(solution)/shard_map/ppermute | solution.py:672
  341.8 16.6 %collective-permute-start.33 = (bf16[512,1024]{1,0:T(8,128)(2,1)S(1)}, bf16[512,1024]{1,0:T(8,128)(2,1)S(1)}, u32[]{:S(2)}, u32[]{:S(2)}) collective-permute-start(bf16[512,1024]{1,0:T(8,128)(2,1)S(1)} %copy-done.39), channel_id=1, source_target_pairs={{0,4},{4,0},{8,12},{12,8},{16,20},{20,16},{24,28},{28,24},{1,5},{5... | collective-permute-start | bytes 3145736 | tf_op jit(solution)/shard_map/ppermute | solution.py:672
  381.7 164.6 %all-gather.15.cloned.1.call-start = ((), (), s32[]{:S(2)}) async-start(), calls=%async_computation.7 | async-start | bytes 7077888 | tf_op jit(solution)/shard_map/all_gather | solution.py:892
  439.9 4.8 collective-permute-start.39
  441.3 19.7 %collective-permute-start.42 = (bf16[4,256,256]{2,1,0:T(8,128)(2,1)}, bf16[4,256,256]{2,1,0:T(8,128)(2,1)}, u32[]{:S(2)}, u32[]{:S(2)}) collective-permute-start(bf16[4,256,256]{2,1,0:T(8,128)(2,1)} %get-tuple-element.206), channel_id=1, source_target_pairs={{0,8},{4,12},{8,0},{12,4},{16,24},{20,28},{24,16},{28,20},{1,9},{5... | collective-permute-start | bytes 1572872 | tf_op jit(solution)/shard_map/ppermute | solution.py:672
  442.7 23.4 %collective-permute-start.43 = (bf16[4,256,256]{2,1,0:T(8,128)(2,1)}, bf16[4,256,256]{2,1,0:T(8,128)(2,1)}, u32[]{:S(2)}, u32[]{:S(2)}) collective-permute-start(bf16[4,256,256]{2,1,0:T(8,128)(2,1)} %get-tuple-element.208), channel_id=1, source_target_pairs={{0,16},{4,20},{8,24},{12,28},{16,0},{20,4},{24,8},{28,12},{1,17},{... | collective-permute-start | bytes 1572872 | tf_op jit(solution)/shard_map/ppermute | solution.py:672
  444.3 32.3 %collective-permute-start.44 = (bf16[4,256,256]{2,1,0:T(8,128)(2,1)}, bf16[4,256,256]{2,1,0:T(8,128)(2,1)}, u32[]{:S(2)}, u32[]{:S(2)}) collective-permute-start(bf16[4,256,256]{2,1,0:T(8,128)(2,1)} %get-tuple-element.207), channel_id=1, source_target_pairs={{0,24},{4,28},{8,16},{12,20},{16,8},{20,12},{24,0},{28,4},{1,25},{... | collective-permute-start | bytes 1572872 | tf_op jit(solution)/shard_map/ppermute | solution.py:672
  444.7 66.7 %collective-permute-start.38 = (bf16[512,1024]{1,0:T(8,128)(2,1)}, bf16[512,1024]{1,0:T(8,128)(2,1)S(1)}, u32[]{:S(2)}, u32[]{:S(2)}) collective-permute-start(bf16[512,1024]{1,0:T(8,128)(2,1)} %get-tuple-element.189), channel_id=1, source_target_pairs={{0,4},{4,0},{8,12},{12,8},{16,20},{20,16},{24,28},{28,24},{1,5},{5... | collective-permute-start | bytes 3145736 | tf_op jit(solution)/shard_map/ppermute | solution.py:672
  446.4 65.1 %collective-permute-start.40 = (bf16[512,1024]{1,0:T(8,128)(2,1)S(1)}, bf16[512,1024]{1,0:T(8,128)(2,1)S(1)}, u32[]{:S(2)}, u32[]{:S(2)}) collective-permute-start(bf16[512,1024]{1,0:T(8,128)(2,1)S(1)} %add_convert_fusion.1), channel_id=1, source_target_pairs={{1,0},{0,1},{3,2},{2,3},{5,4},{4,5},{7,6},{6,7},{9,8},{8,9},{11,10... | collective-permute-start | bytes 3145736 | tf_op jit(solution)/shard_map/ppermute | solution.py:691
  478.2 33.1 %collective-permute-start.45 = (bf16[4,256,256]{2,1,0:T(8,128)(2,1)S(1)}, bf16[4,256,256]{2,1,0:T(8,128)(2,1)S(1)}, u32[]{:S(2)}, u32[]{:S(2)}) collective-permute-start(bf16[4,256,256]{2,1,0:T(8,128)(2,1)S(1)} %fusion.2), channel_id=1, source_target_pairs={{4,2},{5,3},{6,0},{7,1},{12,10},{13,11},{14,8},{15,9},{20,18},{21,... | collective-permute-start | bytes 1572872 | tf_op jit(solution)/shard_map/ppermute | solution.py:906
  479.5 61.5 %collective-permute-start.36 = (bf16[512,1024]{1,0:T(8,128)(2,1)}, bf16[512,1024]{1,0:T(8,128)(2,1)S(1)}, u32[]{:S(2)}, u32[]{:S(2)}) collective-permute-start(bf16[512,1024]{1,0:T(8,128)(2,1)} %output_sum.1), channel_id=1, source_target_pairs={{0,0},{1,1},{2,4},{3,5},{4,2},{5,3},{6,6},{7,7},{8,8},{9,9},{10,12... | collective-permute-start | bytes 3145736 | tf_op jit(solution)/shard_map/ppermute | solution.py:701
  511.4 8.4 %collective-permute-start.46 = (bf16[4,256,256]{2,1,0:T(8,128)(2,1)S(1)}, bf16[4,256,256]{2,1,0:T(8,128)(2,1)}, u32[]{:S(2)}, u32[]{:S(2)}) collective-permute-start(bf16[4,256,256]{2,1,0:T(8,128)(2,1)S(1)} %add_convert_fusion.6), channel_id=1, source_target_pairs={{0,4},{4,0},{8,12},{12,8},{16,20},{20,16},{24,28},{28,24},{1,5},{5... | collective-permute-start | bytes 1572872 | tf_op jit(solution)/shard_map/ppermute | solution.py:672
  517.9 28.3 %collective-permute-start.41 = (bf16[512,1024]{1,0:T(8,128)(2,1)}, bf16[512,1024]{1,0:T(8,128)(2,1)S(1)}, u32[]{:S(2)}, u32[]{:S(2)}) collective-permute-start(bf16[512,1024]{1,0:T(8,128)(2,1)} %get-tuple-element.192), channel_id=1, source_target_pairs={{0,0},{1,1},{2,4},{3,5},{4,2},{5,3},{6,6},{7,7},{8,8},{9,9},{10,12... | collective-permute-start | bytes 3145736 | tf_op jit(solution)/shard_map/ppermute | solution.py:701
  520.6 2.5 collective-permute-start.47
  523.1 3.7 collective-permute-start.48
  526.8 3.7 collective-permute-start.49
  530.5 8.9 %collective-permute-start.50 = (f32[2,1024]{1,0:T(2,128)S(1)}, f32[2,1024]{1,0:T(2,128)S(1)}, u32[]{:S(2)}, u32[]{:S(2)}) collective-permute-start(f32[2,1024]{1,0:T(2,128)S(1)} %add.186), channel_id=1, source_target_pairs={{0,1},{1,0},{2,3},{3,2},{4,5},{5,4},{6,7},{7,6},{8,9},{9,8},{10,11... | collective-permute-start | bytes 24584 | tf_op jit(solution)/shard_map/ppermute | solution.py:732
  530.5 24.0 %collective-permute-start.52 = (bf16[4,256,256]{2,1,0:T(8,128)(2,1)S(1)}, bf16[4,256,256]{2,1,0:T(8,128)(2,1)}, u32[]{:S(2)}, u32[]{:S(2)}) collective-permute-start(bf16[4,256,256]{2,1,0:T(8,128)(2,1)S(1)} %broadcast_select_fusion.refs_0_), channel_id=1, source_target_pairs={{0,8},{4,12},{8,0},{12,4},{16,24},{20,28},{24,16},{28,20},{1,9},{5... | collective-permute-start | bytes 1572872 | tf_op jit(solution)/shard_map/ppermute | solution.py:672
  531.9 22.9 %collective-permute-start.53 = (bf16[4,256,256]{2,1,0:T(8,128)(2,1)S(1)}, bf16[4,256,256]{2,1,0:T(8,128)(2,1)}, u32[]{:S(2)}, u32[]{:S(2)}) collective-permute-start(bf16[4,256,256]{2,1,0:T(8,128)(2,1)S(1)} %broadcast_select_fusion.refs_0_), channel_id=1, source_target_pairs={{0,16},{4,20},{8,24},{12,28},{16,0},{20,4},{24,8},{28,12},{1,17},{... | collective-permute-start | bytes 1572872 | tf_op jit(solution)/shard_map/ppermute | solution.py:672
  539.4 15.5 %collective-permute-start.54 = (bf16[4,256,256]{2,1,0:T(8,128)(2,1)S(1)}, bf16[4,256,256]{2,1,0:T(8,128)(2,1)}, u32[]{:S(2)}, u32[]{:S(2)}) collective-permute-start(bf16[4,256,256]{2,1,0:T(8,128)(2,1)S(1)} %broadcast_select_fusion.refs_0_), channel_id=1, source_target_pairs={{0,24},{4,28},{8,16},{12,20},{16,8},{20,12},{24,0},{28,4},{1,25},{... | collective-permute-start | bytes 1572872 | tf_op jit(solution)/shard_map/ppermute | solution.py:672
  541.0 4.6 collective-permute-start.51
  (39 other events, 272.8 us)
Sparse Core Ops, SparseCore 0:
  39.1 44.4 all-gather.8
  88.7 39.7 all-gather.10
  137.3 43.2 all-gather.12
  331.5 27.3 reduce-scatter.4
  381.8 45.0 reduce-scatter.2
  440.1 63.0 all-gather.14

commit v3 on v2

--- a/solution.py
+++ b/solution.py
@@ -103,29 +103,22 @@
     total = base_ref[...].astype(F32) + inverse * (through - first - scaled * second)
     if keep:
         outs[0][...] = total
-    outs[-2][...] = total.astype(BF16)
-
-    @pl.when(pl.program_id(0) == 0)
-    def _():
-        outs[-1][...] = jnp.zeros_like(outs[-1])
-
-    outs[-1][...] += jnp.sum(e * scaled, axis=0, keepdims=True)
+    outs[-1][...] = total.astype(BF16)
 
 
 def back_call(name, base, x, gain, parts, keep):
     n, d = x.shape
-    b = min(128, n)
+    b = min(256, n)
     row = pl.BlockSpec((b, d), lambda i: (i, 0))
     one = pl.BlockSpec((1, d), lambda i: (0, 0))
-    out = [shape((n, d), F32)] * keep + [shape((n, d), BF16), shape((1, d), F32)]
     return call(
         functools.partial(back_kernel, len(parts), keep),
         name,
-        tuple(out),
+        [shape((n, d), F32)] * keep + [shape((n, d), BF16)],
+        us=5,
         grid=(n // b,),
         in_specs=[row, row, one] + [row] * len(parts),
-        out_specs=tuple([row] * (keep + 1) + [one]),
-        us=5.5,
+        out_specs=[row] * (keep + 1),
     )(base, x, gain, *parts)
 
 
@@ -500,28 +493,38 @@
     )(index, wq, wo, *parts)
 
 
-def unpack_kernel(n_parts, index_ref, *refs):
-    parts, (q_ref, o_ref) = refs[:n_parts], refs[n_parts:]
+def column_sums(x):
+    return jnp.sum(x.T, axis=0, keepdims=True)
+
+
+def unpack_kernel(n_parts, index_ref, w_ref, *refs):
+    parts, (q_ref, o_ref, gain_ref) = refs[:n_parts], refs[n_parts:]
     a, b = parts[0].shape[1:]
     for i, p in enumerate(parts):
         j = index_ref[i]
+        rows = pl.ds(pl.multiple_of(j * a, a), a)
+        gain = None
         for which in range(3):
-            q_ref[which, pl.ds(pl.multiple_of(j * a, a), a), :] = p[which].astype(F32)
+            g = p[which].astype(F32)
+            q_ref[which, rows, :] = g
+            term = g * w_ref[which, rows, :].astype(F32)
+            gain = term if gain is None else gain + term
         o_ref[:, pl.ds(pl.multiple_of(j * b, b), b)] = p[3].astype(F32)
-
-
-def unpack_call(index, parts):
+        gain_ref[:, rows] = column_sums(gain)
+
+
+def unpack_call(index, wq, parts):
     _, a, b = parts[0].shape
     J = len(parts)
     vmem = pl.BlockSpec(memory_space=pltpu.VMEM)
     return call(
         functools.partial(unpack_kernel, J),
         "unpack_heads",
-        (shape((3, J * a, b), F32), shape((a, J * b), F32)),
-        in_specs=[pl.BlockSpec(memory_space=pltpu.SMEM)] + [vmem] * J,
-        out_specs=(vmem, vmem),
+        (shape((3, J * a, b), F32), shape((a, J * b), F32), shape((1, J * a), F32)),
+        in_specs=[pl.BlockSpec(memory_space=pltpu.SMEM)] + [vmem] * (J + 1),
+        out_specs=(vmem, vmem, vmem),
         us=3.8,
-    )(index, *parts)
+    )(index, wq, *parts)
 
 
 def ffn_kernel(groups, steps, *refs):
@@ -603,11 +606,12 @@
 
     dw = product(c, lambda i, rows: h[i // 2][rows])
     for t in range(T):
-        outs[1][t, 1] = dw[:, t * us : (t + 1) * us]
+        outs[0][t, 2] = dw[:, t * us : (t + 1) * us]
     dw = product(x, lambda i, rows: jnp.concatenate([gl[i // 2][rows], ul[i // 2][rows]], axis=1))
-    for t in range(T):
-        outs[0][t] = dw[:, t * us : (t + 1) * us]
-        outs[1][t, 0] = dw[:, (T + t) * us : (T + t + 1) * us]
+    for j in range(2):
+        for t in range(T):
+            at = (j * T + t) * us
+            outs[0][t, j] = dw[:, at : at + us]
 
 
 def ffn_weight_call(x, c, h, gl, ul, m, T, us):
@@ -618,41 +622,46 @@
     return call(
         functools.partial(ffn_weight_kernel, T, us),
         "feed_forward_weights",
-        (shape((T, d, us), BF16), shape((T, 2, d, us), BF16)),
+        shape((T, 3, d, us), BF16),
         grid=(d // db,),
         in_specs=spec,
-        out_specs=(
-            pl.BlockSpec((T, db, us), lambda i: (0, i, 0)),
-            pl.BlockSpec((T, 2, db, us), lambda i: (0, 0, i, 0)),
-        ),
+        out_specs=pl.BlockSpec((T, 3, db, us), lambda i: (0, 0, i, 0)),
         us=12.4,
     )(*x, *c, *h, *gl, *ul)
 
 
-def assemble_kernel(w_ref, gu_ref, dn_ref):
+def assemble_kernel(w_ref, old_ref, gu_ref, dn_ref, gain_ref):
     DP, _, _, us = w_ref.shape
+    gain = None
     for j in range(2):
-        rows = jnp.concatenate([w_ref[p, j] for p in range(DP)], axis=1)
-        gu_ref[:, j, :] = rows.astype(F32)
+        rows = jnp.concatenate([w_ref[p, j] for p in range(DP)], axis=1).astype(F32)
+        gu_ref[:, j, :] = rows
+        term = rows * old_ref[:, j, :].astype(F32)
+        gain = term if gain is None else gain + term
+    gain_ref[...] = column_sums(gain)
     rows = jnp.concatenate([w_ref[p, 2] for p in range(DP)], axis=1)
     dn_ref[...] = rows.T.astype(F32)
 
 
-def assemble_call(w):
+def assemble_call(w, old):
     DP, _, d, us = w.shape
     b = min(256, d)
     return call(
         assemble_kernel,
         "feed_forward_gradients",
-        (shape((d, 2, DP * us), F32), shape((DP * us, d), F32)),
+        (shape((d, 2, DP * us), F32), shape((DP * us, d), F32), shape((1, d), F32)),
+        us=9,
         grid=(d // b,),
-        in_specs=[pl.BlockSpec((DP, 3, b, us), lambda i: (0, 0, i, 0))],
+        in_specs=[
+            pl.BlockSpec((DP, 3, b, us), lambda i: (0, 0, i, 0)),
+            pl.BlockSpec((b, 2, DP * us), lambda i: (i, 0, 0)),
+        ],
         out_specs=(
             pl.BlockSpec((b, 2, DP * us), lambda i: (i, 0, 0)),
             pl.BlockSpec((DP * us, b), lambda i: (0, i)),
+            pl.BlockSpec((1, b), lambda i: (0, i)),
         ),
-        us=8,
-    )(w)
+    )(w, old)
 
 
 def after(x, *deps):
@@ -709,6 +718,13 @@
             y = after(y, hold)
             out += [y, core_flip(y)]
         return out
+
+    def sum_heads(pieces):
+        flips = [core_flip(z) for z in pieces[1::2]]
+        sums = [
+            (pieces[2 * k].astype(F32) + flips[k].astype(F32)).astype(BF16) for k in range(1, R)
+        ]
+        return sums, [pieces[0], flips[0]]
 
     def scatter_heads(pieces):
         out = []
@@ -725,9 +741,7 @@
         z = top_flip(y)
         return [y, core_flip(y), z, core_flip(z)]
 
-    def sum_all(x):
-        for bit in range(DP.bit_length() - 1):
-            x = x + over_dp(x, lambda i, bit=bit: i ^ (1 << bit))
+    def sum_rows(x):
         for bit in range(T.bit_length() - 1):
             x = x + lax.ppermute(x, "tensor", [(t, t ^ (1 << bit)) for t in range(T)])
         return x
@@ -828,74 +842,68 @@
         far_x, near_dx = tie(xs[2], near_dx)
         far = ffn_call([far_x, xs[3]], cots[2:], weights)
 
-        def cross(mine, theirs):
-            both = mine.astype(F32) + core_flip(theirs).astype(F32)
-            return top_flip(both.astype(BF16))
-
-        crossed = cross(far[5], far[6])
+        def core_sum(mine, theirs):
+            return (mine.astype(F32) + core_flip(theirs).astype(F32)).astype(BF16)
+
+        dx_both = core_sum(far[5], far[6])
+        crossed = top_flip(dx_both)
 
         def weight_grads(m, hold):
             return ffn_weight_call(
                 [after(xs[0], hold), *xs[1:]], cots, *[[near[i], far[i]] for i in range(3)], m, T, us
             )
 
-        sent, hold = [], far[0]
+        sent, hold = [], dx_both
         for m in range(M - 1, 0, -1):
-            got = weight_grads(m, hold)
-            hold = got[0]
-            sent.append([mid_from(g, M - m) for g in got])
-        crossed, _ = tie(crossed, hold)
-        middle_grad, middle_low, gain_two_part = back_call(
+            hold = weight_grads(m, hold)
+            sent.append(mid_from(hold, M - m))
+        out_both = core_sum(after(far[3], hold), far[4])
+        near_out = core_flip(after(near[4], hold))
+        crossed, out_both, near_out = tie(crossed, out_both, near_out)
+        middle_grad, middle_low = back_call(
             "middle_grad", cot, middle, gain_two, [near[5], near_dx, crossed], 1
         )
         low_rows = send_rows(middle_low)
+        out_crossed = top_flip(out_both)
         flipped = core_flip(middle_low)
         own_grads = weight_grads(0, flipped)
-        out_crossed = cross(after(far[3], flipped), far[4])
-
-        def total(i, hold):
-            t = after(own_grads[i], hold).astype(F32)
-            for z in sent:
-                t = t + z[i].astype(F32)
-            return t.astype(BF16)
-
-        def reduce_rows(g):
-            return lax.psum_scatter(g, "tensor", scatter_dimension=0)
-
-        first_sum = total(0, own_grads[0])
-        first_part = reduce_rows(first_sum)
-        lows = gather_heads(middle_low, flipped, low_rows, first_sum)
+        output = output_call(after(middle, own_grads), [near[3], near_out, out_crossed])
+        lows = gather_heads(middle_low, flipped, low_rows, output)
+        moved_output = reshard(output)
         g, wo_grad = heads_grad_call(o, pack, lows)
 
         back = []
         for i in range(heads):
             if i == 1:
-                near_out = core_flip(after(near[4], g))
-                output = output_call(after(middle, back[0][0]), [near[3], near_out, out_crossed])
-                moved_output = reshard(output)
-                second_sum = total(1, output)
-                g, second_sum = tie(g, second_sum)
-                second_part = reduce_rows(second_sum)
+                total = after(own_grads, back[0][0]).astype(F32)
+                for z in sent:
+                    total = total + z.astype(F32)
+                total = total.astype(BF16)
+                g, total, moved_output = tie(g, total, moved_output)
+                slices = lax.psum_scatter(total, "tensor", scatter_dimension=0)
             elif i:
                 g = after(g, back[-1][0])
-            if i == heads - 1:
-                g, first_part = tie(g, first_part)
             j = i // count
             back.append(
                 attend_back_call(q, k, v, bias, o[j], lse[j], g, cos, sin, i, i - j * count)
             )
-        wo_grad, _ = tie(wo_grad, back[-1][0])
+        pieces = qkv_back_call(after(pack, back[-1][0]), back, T, d)
+        sums, mine = sum_heads(pieces)
+        rows = [row_from(z, R - k) for k, z in enumerate(sums, 1)]
+        wo_grad, *sums = tie(wo_grad, *sums)
         dw = qkv_weight_call(wo_grad, back, normed_one, pack.shape)
-        pieces = qkv_back_call(after(pack, dw), back, T, d)
-        second_part, *pieces = tie(second_part, *pieces)
-        slices = jnp.concatenate([first_part[None], second_part])
-        slices = lax.all_gather(slices, "dp", axis=0)
 
         def share_of(k):
             return lax.dynamic_index_in_dim(dw, pair ^ k, 0, keepdims=False)
 
         travelled = [pair_from(share_of(k), k) for k in range(1, J)]
-        arrived = scatter_heads(pieces)
+        slices, dw = tie(slices, dw)
+        slices = lax.all_gather(slices, "dp", axis=0)
+        tokens_low = back_call(
+            "tokens_grad", middle_grad, after(x, dw), gain_one, mine + rows, 0
+        )[0]
+        tokens_grad = reshard(tokens_low)[:, None]
+        tokens_low, *travelled = tie(tokens_low, *travelled)
         part = share_of(0).astype(F32)
         for p in travelled:
             part = part + p.astype(F32)
@@ -908,15 +916,13 @@
         part = jnp.where(core == 0, part, core_flip(part))
         shares = [part] + [pair_from(part, k) for k in range(1, J)]
 
-        tokens_low, gain_one_part = back_call(
-            "tokens_grad", middle_grad, x, gain_one, arrived, 0
+        gate_up_grad, down_grad, gain_two_part = assemble_call(
+            after(slices, part), gate_up_weight
         )
-        tokens_grad = reshard(tokens_low)[:, None]
-        gains = jnp.concatenate([gain_one_part, gain_two_part], axis=0)
-        gains = sum_all(after(gains, part))
-        gate_up_grad, down_grad = assemble_call(after(slices, gains))
-        qkv_grad, out_grad = unpack_call(after(index, down_grad), shares)
+        qkv_grad, out_grad, gain_one_part = unpack_call(after(index, down_grad), wq_own, shares)
         qkv_grad = qkv_grad.transpose(1, 0, 2)
+        gains = sum_rows(jnp.concatenate([gain_one_part, gain_two_part], axis=0))
+        gains = gains / jnp.concatenate([gain_one, gain_two], axis=0)
         return (
             moved_output[:, None], tokens_grad, qkv_grad, out_grad, gate_up_grad, down_grad, gains[0], gains[1]
         )

time: 576 us -> 541 us (0.939)
  waiting for transfers between devices: 204 us -> 162 us
  starting transfers between devices: 77.1 us -> 86.5 us
    ppermute x38 -> x34, waiting for transfers between devices: 107 us -> 75.1 us  [over_dp(): return lax.ppermute(x, 'dp', [(i, f(i)) for i in range(DP)])]
    ppermute x38 -> x34, starting transfers between devices: 50.6 us -> 67.8 us  [over_dp(): return lax.ppermute(x, 'dp', [(i, f(i)) for i in range(DP)])]
    ppermute x1, waiting for transfers between devices: 29.9 us -> 15.7 us  [on_device(): moved = lax.ppermute(part, ('dp', 'tensor'), home_pairs)]
    ppermute x5, starting transfers between devices: 16.3 us -> 7.86 us  [reshard(): return lax.ppermute(x, ('dp', 'tensor'), pairs)]
    ppermute x5, waiting for transfers between devices: 22.1 us -> 30.4 us  [row_from(): lax.ppermute(x, 'tensor', [(t // R * R + (t % R + k) % R, t) for t in ran...]
    unnamed x90 -> x92, local copies, waits for them, and re-layouts: 12.8 us -> 13.2 us
  transfers between devices with their start and end apart: 61 -> 56, of which waited for: 26 -> 23; matrix products, arithmetic and copies ran while one was open for 5% -> 6% of each run, Pallas kernels for 34% -> 38%
where the time goes in v3:
time: 541 us; the launch traced here: 534 us
  Pallas kernels  225 us (42%)
  waiting for transfers between devices  162 us (30%)
  starting transfers between devices  86.5 us (16%)
  local copies, waits for them, and re-layouts  27.2 us (5%)
  other arithmetic  17.8 us (3%)
  between operations  15.3 us (3%)
    ppermute x34, waiting for transfers between devices, over_dp(): return lax.ppermute(x, 'dp', [(i, f(i)) for i in range(DP)])  75.1 us
    ppermute x34, starting transfers between devices, over_dp(): return lax.ppermute(x, 'dp', [(i, f(i)) for i in range(DP)])  67.8 us
    pallas_call x4, Pallas kernels, attend_back_call(): call(functools.partial(attend_back_kernel, sub=min(256, S)), 'attend_back...  54.6 us
    pallas_call x2, Pallas kernels, ffn_call(): call(functools.partial(ffn_kernel, groups, steps), 'feed_forward', (shape...  42.4 us
    all_gather x3, waiting for transfers between devices, on_device(): lax.all_gather(z, 'tensor', axis=0)  33.9 us
    ppermute x5, waiting for transfers between devices, row_from(): lax.ppermute(x, 'tensor', [(t // R * R + (t % R + k) % R, t) for t in ran...  30.4 us
    pallas_call x2, Pallas kernels, attend_call(): call(functools.partial(attend_kernel, sub=sub), 'attend', (shape((count *...  29.3 us
    pallas_call x2, Pallas kernels, ffn_weight_call(): call(functools.partial(ffn_weight_kernel, T, us), 'feed_forward_weights',...  24.6 us
  transfers between devices with their start and end apart: 56, of which 23 were waited for; matrix products, arithmetic and copies ran while one was open for 6% of the time, Pallas kernels for 38%

profile of v3, /device:TPU:0, one launch (start us, length us, event | category | flops | bytes accessed | tf_op | source)
XLA Modules:
  0.0 534.0 jit_solution(1458938123149252840)
XLA Ops:
  9.3 2.2 slice_bitcast_fusion
  11.5 1.7 collective-permute-start.8
  13.2 1.7 collective-permute-start
  16.2 1.6 dynamic-slice_bitcast_fusion.4
  19.5 1.4 constant_dynamic-slice_fusion.1
  22.3 1.8 multiply_sine_fusion
  27.0 2.2 norm_tokens.2.refs_0_.refs_12_
  30.0 2.2 norm_tokens.3.refs_4_.refs_16_
  32.2 2.7 collective-permute-start.7
  37.1 10.0 %collective-permute-done.7.refs_2_.refs_14_ = bf16[256,1024]{1,0:T(8,128)(2,1)S(1)} collective-permute-done((bf16[256,1024]{1,0:T(8,128)(2,1)S(1)}, bf16[256,1024]{1,0:T(8,128)(2,1)S(1)}, u32[]{:S(2)}, u32[]{:S(2)}) %collective-permute-start.7) | collective-permute-done | bytes 524320 | tf_op jit(solution)/shard_map/ppermute | solution.py:700
  47.1 28.0 %collective-permute-start.10 = (bf16[256,1024]{1,0:T(8,128)(2,1)}, bf16[256,1024]{1,0:T(8,128)(2,1)S(1)}, u32[]{:S(2)}, u32[]{:S(2)}) collective-permute-start(bf16[256,1024]{1,0:T(8,128)(2,1)} %norm_tokens.3.refs_4_.refs_16_), channel_id=1, source_target_pairs={{0,4},{4,0},{8,12},{12,8},{16,20},{20,16},{24,28},{28,24},{1,5},{5... | collective-permute-start | bytes 1572872 | tf_op jit(solution)/shard_map/ppermute | solution.py:681
  76.4 3.6 pack_heads.1.w_ref
  80.1 6.3 %collective-permute-start.12 = (bf16[256,1024]{1,0:T(8,128)(2,1)S(1)}, bf16[256,1024]{1,0:T(8,128)(2,1)}, u32[]{:S(2)}, u32[]{:S(2)}) collective-permute-start(bf16[256,1024]{1,0:T(8,128)(2,1)S(1)} %collective-permute-done.11.refs_6_.refs_18_), channel_id=1, source_target_pairs={{0,4},{4,0},{8,12},{12,8},{16,20},{20,16},{24,28},{28,24},{1,5},{5... | collective-permute-start | bytes 1572872 | tf_op jit(solution)/shard_map/ppermute | solution.py:681
  86.3 1.9 collective-permute-start.13
  89.1 7.5 %project_heads.1 = (bf16[256,2048]{1,0:T(8,128)(2,1)}, bf16[256,2048]{1,0:T(8,128)(2,1)}, bf16[256,2048]{1,0:T(8,128)(2,1)}) custom-call(f32[32,2048]{1,0:T(8,128)} %get-tuple-element.206.c_ref.ck_ref, f32[32,2048]{1,0:T(8,128)} %get-tuple-element.205.s_ref.sk_ref, bf16[4,4,256,256]{3,2,1,0:T(8,128)(2,1)} %pack_heads.1.w_ref, ...), custom_call_target="tpu_custom_call" | custom-call | flops 2184999936 | tf_op jit(solution)/shard_map/project_heads/pallas_call | solution.py:186
  96.6 14.9 %attend.2 = (bf16[128,2048]{1,0:T(8,128)(2,1)}, f32[2,8,2048]{2,1,0:T(8,128)}) custom-call(bf16[256,2048]{1,0:T(8,128)(2,1)} %get-tuple-element.112.q_ref, bf16[256,2048]{1,0:T(8,128)(2,1)} %get-tuple-element.108.k_ref, bf16[256,2048]{1,0:T(8,128)(2,1)} %get-tuple-element.109.v_ref, bf16[16,2048]{1,0:T(8,128)(2,1)} %concatenate.41.b_ref), custom_call_target="tpu_custom_call" | custom-call | flops 4255000064 | tf_op jit(solution)/shard_map/attend/pallas_call | solution.py:242
  111.6 14.4 %attend.3 = (bf16[128,2048]{1,0:T(8,128)(2,1)}, f32[2,8,2048]{2,1,0:T(8,128)}) custom-call(bf16[256,2048]{1,0:T(8,128)(2,1)} %get-tuple-element.112.q_ref, bf16[256,2048]{1,0:T(8,128)(2,1)} %get-tuple-element.108.k_ref, bf16[256,2048]{1,0:T(8,128)(2,1)} %get-tuple-element.109.v_ref, bf16[16,2048]{1,0:T(8,128)(2,1)} %concatenate.41.b_ref), custom_call_target="tpu_custom_call" | custom-call | flops 4255000064 | tf_op jit(solution)/shard_map/attend/pallas_call | solution.py:242
  126.0 4.2 output_projection.1
  130.2 9.9 %collective-permute-start.15 = (bf16[512,1024]{1,0:T(8,128)(2,1)}, bf16[512,1024]{1,0:T(8,128)(2,1)S(1)}, u32[]{:S(2)}, u32[]{:S(2)}) collective-permute-start(bf16[512,1024]{1,0:T(8,128)(2,1)} %get-tuple-element.120), channel_id=1, source_target_pairs={{0,4},{4,0},{8,12},{12,8},{16,20},{20,16},{24,28},{28,24},{1,5},{5... | collective-permute-start | bytes 3145736 | tf_op jit(solution)/shard_map/ppermute | solution.py:681
  140.3 2.4 collective-permute-done.15
  142.6 1.6 add_convert_fusion.4
  149.4 33.9 %all-gather.9.cloned.1.call-done = bf16[512,1024]{1,0:T(8,128)(2,1)} async-done(((bf16[128,1024]{1,0:T(8,128)(2,1)}), bf16[512,1024]{1,0:T(8,128)(2,1)}) %all-gather.9.cloned.1.call-update) | async-done | bytes 1048592 | tf_op jit(solution)/shard_map/all_gather | solution.py:819
  183.3 1.7 collective-permute-start.19
  185.0 1.7 collective-permute-done.16.refs_2_
  186.7 4.7 middle_norm.1
  195.3 20.1 %collective-permute-done.19.refs_7_ = bf16[4,128,1024]{2,1,0:T(8,128)(2,1)S(1)} collective-permute-done((bf16[4,128,1024]{2,1,0:T(8,128)(2,1)}, bf16[4,128,1024]{2,1,0:T(8,128)(2,1)S(1)}, u32[]{:S(2)}, u32[]{:S(2)}) %collective-permute-start.19) | collective-permute-done | bytes 1048608 | tf_op jit(solution)/shard_map/ppermute | solution.py:681
  217.7 21.3 %feed_forward.2 = (bf16[1024,1024]{1,0:T(8,128)(2,1)}, bf16[1024,1024]{1,0:T(8,128)(2,1)}, bf16[1024,1024]{1,0:T(8,128)(2,1)}, bf16[512,1024]{1,0:T(8,128)(2,1)}...) custom-call(bf16[512,1024]{1,0:T(8,128)(2,1)} %get-tuple-element.147.refs_0_, ...), custom_call_target="tpu_custom_call" | custom-call | flops 6037499904 | tf_op jit(solution)/shard_map/feed_forward/pallas_call | solution.py:582
  239.7 2.8 collective-permute-done.23.refs_1_
  243.3 1.5 collective-permute-done.24.refs_1_.refs_3_
  245.7 21.1 %feed_forward.3 = (bf16[1024,1024]{1,0:T(8,128)(2,1)}, bf16[1024,1024]{1,0:T(8,128)(2,1)}, bf16[1024,1024]{1,0:T(8,128)(2,1)}, bf16[512,1024]{1,0:T(8,128)(2,1)}...) custom-call(bf16[512,1024]{1,0:T(8,128)(2,1)} %copy-done.7, ...), custom_call_target="tpu_custom_call" | custom-call | flops 6037499904 | tf_op jit(solution)/shard_map/feed_forward/pallas_call | solution.py:582
  267.5 2.4 collective-permute-done.27
  269.8 1.6 add_convert_fusion.3
  272.9 12.2 %feed_forward_weights.2 = bf16[4,3,1024,128]{3,2,1,0:T(8,128)(2,1)} custom-call(bf16[512,1024]{1,0:T(8,128)(2,1)} %get-tuple-element.147.refs_0_, bf16[512,1024]{1,0:T(8,128)(2,1)} %copy-done.5, bf16[512,1024]{1,0:T(8,128)(2,1)} %copy-done.7, bf16[512,1024]{1,0:T(8,128)(2,1)} %copy-done.9, bf16[512,1024]{1,0:T(8,128)(2,1)} %copy-done.3, ...), custom_call_target="tpu_custom_call" | custom-call | flops 3564999936 | tf_op jit(solution)/shard_map/feed_forward_weights/pallas_call | solution.py:622
  285.2 1.6 collective-permute-start.35
  287.1 9.6 %collective-permute-done.28.refs_2_ = bf16[512,1024]{1,0:T(8,128)(2,1)S(1)} collective-permute-done((bf16[512,1024]{1,0:T(8,128)(2,1)S(1)}, bf16[512,1024]{1,0:T(8,128)(2,1)S(1)}, u32[]{:S(2)}, u32[]{:S(2)}) %collective-permute-start.28) | collective-permute-done | bytes 1048608 | tf_op jit(solution)/shard_map/ppermute | solution.py:681
  297.7 5.1 middle_grad.1
  305.8 12.4 %feed_forward_weights.3 = bf16[4,3,1024,128]{3,2,1,0:T(8,128)(2,1)} custom-call(bf16[512,1024]{1,0:T(8,128)(2,1)} %get-tuple-element.147.refs_0_, bf16[512,1024]{1,0:T(8,128)(2,1)} %copy-done.5, bf16[512,1024]{1,0:T(8,128)(2,1)} %copy-done.7, bf16[512,1024]{1,0:T(8,128)(2,1)} %copy-done.9, bf16[512,1024]{1,0:T(8,128)(2,1)} %copy-done.3, ...), custom_call_target="tpu_custom_call" | custom-call | flops 3564999936 | tf_op jit(solution)/shard_map/feed_forward_weights/pallas_call | solution.py:622
  318.2 10.3 %collective-permute-done.33.refs_2_ = bf16[512,1024]{1,0:T(8,128)(2,1)S(1)} collective-permute-done((bf16[512,1024]{1,0:T(8,128)(2,1)S(1)}, bf16[512,1024]{1,0:T(8,128)(2,1)S(1)}, u32[]{:S(2)}, u32[]{:S(2)}) %collective-permute-start.33) | collective-permute-done | bytes 1048608 | tf_op jit(solution)/shard_map/ppermute | solution.py:681
  329.4 3.6 output_sum.1
  333.1 1.9 collective-permute-start.36
  336.7 5.9 %heads_grad.1 = (bf16[256,2048]{1,0:T(8,128)(2,1)}, bf16[4,256,256]{2,1,0:T(8,128)(2,1)}) custom-call(bf16[4,4,256,256]{3,2,1,0:T(8,128)(2,1)} %pack_heads.1.w_ref, bf16[128,2048]{1,0:T(8,128)(2,1)} %get-tuple-element.111.refs_0_.o_ref, bf16[128,2048]{1,0:T(8,128)(2,1)} %get-tuple-element.115.refs_1_.o_ref, bf16[512,1024]{1,0:T(8,128)(2,1)} %get-tuple-element.146.refs_2_, ...), custom_call_target="tpu_custom_call" | custom-call | flops 1724999936 | tf_op jit(solution)/shard_map/heads_grad/pallas_call | solution.py:401
  342.6 13.5 %attend_back.4 = (bf16[64,2048]{1,0:T(8,128)(2,1)}, bf16[64,2048]{1,0:T(8,128)(2,1)}, bf16[64,2048]{1,0:T(8,128)(2,1)}) custom-call(bf16[256,2048]{1,0:T(8,128)(2,1)} %get-tuple-element.112.q_ref, bf16[256,2048]{1,0:T(8,128)(2,1)} %get-tuple-element.108.k_ref, bf16[256,2048]{1,0:T(8,128)(2,1)} %get-tuple-element.109.v_ref, ...), custom_call_target="tpu_custom_call" | custom-call | flops 3536250112 | tf_op jit(solution)/shard_map/attend_back/pallas_call | solution.py:315
  356.2 4.4 add_convert_fusion
  360.7 13.9 %attend_back.5 = (bf16[64,2048]{1,0:T(8,128)(2,1)}, bf16[64,2048]{1,0:T(8,128)(2,1)}, bf16[64,2048]{1,0:T(8,128)(2,1)}) custom-call(bf16[256,2048]{1,0:T(8,128)(2,1)} %get-tuple-element.112.q_ref, bf16[256,2048]{1,0:T(8,128)(2,1)} %get-tuple-element.108.k_ref, bf16[256,2048]{1,0:T(8,128)(2,1)} %get-tuple-element.109.v_ref, ...), custom_call_target="tpu_custom_call" | custom-call | flops 3536250112 | tf_op jit(solution)/shard_map/attend_back/pallas_call | solution.py:315
  374.6 13.5 %attend_back.6 = (bf16[64,2048]{1,0:T(8,128)(2,1)}, bf16[64,2048]{1,0:T(8,128)(2,1)}, bf16[64,2048]{1,0:T(8,128)(2,1)}) custom-call(bf16[256,2048]{1,0:T(8,128)(2,1)} %get-tuple-element.112.q_ref, bf16[256,2048]{1,0:T(8,128)(2,1)} %get-tuple-element.108.k_ref, bf16[256,2048]{1,0:T(8,128)(2,1)} %get-tuple-element.109.v_ref, ...), custom_call_target="tpu_custom_call" | custom-call | flops 3536250112 | tf_op jit(solution)/shard_map/attend_back/pallas_call | solution.py:315
  388.2 13.6 %attend_back.7 = (bf16[64,2048]{1,0:T(8,128)(2,1)}, bf16[64,2048]{1,0:T(8,128)(2,1)}, bf16[64,2048]{1,0:T(8,128)(2,1)}) custom-call(bf16[256,2048]{1,0:T(8,128)(2,1)} %get-tuple-element.112.q_ref, bf16[256,2048]{1,0:T(8,128)(2,1)} %get-tuple-element.108.k_ref, bf16[256,2048]{1,0:T(8,128)(2,1)} %get-tuple-element.109.v_ref, ...), custom_call_target="tpu_custom_call" | custom-call | flops 3536250112 | tf_op jit(solution)/shard_map/attend_back/pallas_call | solution.py:315
  401.8 7.0 %qkv_back.1 = (bf16[512,1024]{1,0:T(8,128)(2,1)}, bf16[512,1024]{1,0:T(8,128)(2,1)}, bf16[512,1024]{1,0:T(8,128)(2,1)}, bf16[512,1024]{1,0:T(8,128)(2,1)}) custom-call(bf16[4,4,256,256]{3,2,1,0:T(8,128)(2,1)} %pack_heads.1.w_ref, bf16[64,2048]{1,0:T(8,128)(2,1)} %get-tuple-element.155.refs_0_, bf16[64,2048]{1,0:T(8,128)(2,1)} %get-tuple-element.169.refs_1_, ...), custom_call_target="tpu_custom_call" | custom-call | flops 2012499968 | tf_op jit(solution)/shard_map/qkv_back/pallas_call | solution.py:430
  408.7 2.6 collective-permute-start.37
  411.4 2.5 collective-permute-done.37
  413.9 1.6 add_convert_fusion.1
  415.5 8.1 %qkv_weights.1 = bf16[4,4,256,256]{3,2,1,0:T(8,128)(2,1)} custom-call(bf16[4,256,256]{2,1,0:T(8,128)(2,1)} %get-tuple-element.179.wo_ref, bf16[64,2048]{1,0:T(8,128)(2,1)} %get-tuple-element.155.refs_0_, bf16[64,2048]{1,0:T(8,128)(2,1)} %get-tuple-element.169.refs_1_, bf16[64,2048]{1,0:T(8,128)(2,1)} %get-tuple-element.170.refs_2_, ...), custom_call_target="tpu_custom_call" | custom-call | flops 2300000000 | tf_op jit(solution)/shard_map/qkv_weights/pallas_call | solution.py:457
  424.5 2.6 dynamic-slice_bitcast_fusion
  427.1 2.3 collective-permute-start.43
  430.6 18.7 %collective-permute-done.39.refs_2_ = bf16[512,1024]{1,0:T(8,128)(2,1)S(1)} collective-permute-done((bf16[512,1024]{1,0:T(8,128)(2,1)S(1)}, bf16[512,1024]{1,0:T(8,128)(2,1)S(1)}, u32[]{:S(2)}, u32[]{:S(2)}) %collective-permute-start.39) | collective-permute-done | bytes 1048608 | tf_op jit(solution)/shard_map/ppermute | solution.py:700
  450.2 4.4 tokens_grad.1
  454.7 6.9 %collective-permute-done.42 = bf16[4,256,256]{2,1,0:T(8,128)(2,1)} collective-permute-done((bf16[4,256,256]{2,1,0:T(8,128)(2,1)}, bf16[4,256,256]{2,1,0:T(8,128)(2,1)}, u32[]{:S(2)}, u32[]{:S(2)}) %collective-permute-start.42) | collective-permute-done | bytes 524320 | tf_op jit(solution)/shard_map/ppermute | solution.py:681
  461.6 1.8 fusion.2
  464.7 15.7 %collective-permute-done.44 = bf16[4,256,256]{2,1,0:T(8,128)(2,1)S(1)} collective-permute-done((bf16[4,256,256]{2,1,0:T(8,128)(2,1)S(1)}, bf16[4,256,256]{2,1,0:T(8,128)(2,1)S(1)}, u32[]{:S(2)}, u32[]{:S(2)}) %collective-permute-start.44) | collective-permute-done | bytes 524320 | tf_op jit(solution)/shard_map/ppermute | solution.py:914
  482.7 1.8 collective-permute-start.48
  486.3 11.0 %feed_forward_gradients.1 = (f32[1024,2,1024]{2,1,0:T(2,128)}, f32[1024,1024]{1,0:T(8,128)}, f32[1,1024]{1,0:T(1,128)}) custom-call(bf16[8,3,1024,128]{3,2,1,0:T(8,128)(2,1)} %bitcast.61, bf16[1024,2,1024]{2,1,0:T(2,128)(2,1)} %old_ref.1), custom_call_target="tpu_custom_call" | custom-call | flops 2587500032 | tf_op jit(solution)/shard_map/feed_forward_gradients/pallas_call | solution.py:649
  498.3 11.5 %collective-permute-done.47.refs_2_ = bf16[4,256,256]{2,1,0:T(8,128)(2,1)} collective-permute-done((bf16[4,256,256]{2,1,0:T(8,128)(2,1)S(1)}, bf16[4,256,256]{2,1,0:T(8,128)(2,1)}, u32[]{:S(2)}, u32[]{:S(2)}) %collective-permute-start.47) | collective-permute-done | bytes 524320 | tf_op jit(solution)/shard_map/ppermute | solution.py:681
  509.8 4.4 unpack_heads.1
  515.0 3.6 collective-permute-done.49
  520.6 3.3 collective-permute-done.50
  (205 shorter events, 52.1 us)
Async XLA Ops:
  7.2 138.0 %all-gather.13.cloned.1.call-start = ((), (), s32[]{:S(2)}) async-start(), calls=%async_computation.4 | async-start | bytes 1310720 | tf_op jit(solution)/shard_map/all_gather | solution.py:819
  8.8 16.1 %collective-permute-start.5 = (bf16[2048]{0:T(1024)(128)(2,1)S(1)}, bf16[2048]{0:T(1024)(128)(2,1)}, u32[]{:S(2)}, u32[]{:S(2)}) collective-permute-start(bf16[2048]{0:T(1024)(128)(2,1)S(1)} %fusion.4), channel_id=1, source_target_pairs={{0,4},{4,0},{8,12},{12,8},{16,20},{20,16},{24,28},{28,24},{1,5},{5... | collective-permute-start | bytes 12296 | tf_op jit(solution)/shard_map/ppermute | solution.py:681
  11.5 17.7 %collective-permute-start.8 = (bf16[256,1024]{1,0:T(8,128)(2,1)}, bf16[256,1024]{1,0:T(8,128)(2,1)S(1)}, u32[]{:S(2)}, u32[]{:S(2)}) collective-permute-start(bf16[256,1024]{1,0:T(8,128)(2,1)} %get-tuple-element.201), channel_id=1, source_target_pairs={{0,0},{1,1},{2,4},{3,5},{4,2},{5,3},{6,6},{7,7},{8,8},{9,9},{10,12... | collective-permute-start | bytes 1572872 | tf_op jit(solution)/shard_map/ppermute | solution.py:710
  13.2 13.0 %collective-permute-start = (bf16[256,1024]{1,0:T(8,128)(2,1)}, bf16[256,1024]{1,0:T(8,128)(2,1)S(1)}, u32[]{:S(2)}, u32[]{:S(2)}) collective-permute-start(bf16[256,1024]{1,0:T(8,128)(2,1)} %get-tuple-element.202), channel_id=1, source_target_pairs={{0,0},{1,1},{2,4},{3,5},{4,2},{5,3},{6,6},{7,7},{8,8},{9,9},{10,12... | collective-permute-start | bytes 1572872 | tf_op jit(solution)/shard_map/ppermute | solution.py:710
  26.2 8.7 %collective-permute-start.1 = (bf16[4,256,256]{2,1,0:T(8,128)(2,1)S(1)}, bf16[4,256,256]{2,1,0:T(8,128)(2,1)S(1)}, u32[]{:S(2)}, u32[]{:S(2)}) collective-permute-start(bf16[4,256,256]{2,1,0:T(8,128)(2,1)S(1)} %pad_maximum_fusion), channel_id=1, source_target_pairs={{4,6},{5,7},{6,4},{7,5},{12,14},{13,15},{14,12},{15,13},{20,22},{2... | collective-permute-start | bytes 1572872 | tf_op jit(solution)/shard_map/ppermute | solution.py:777
  32.2 114.3 %all-gather.11.cloned.1.call-start = ((), (), s32[]{:S(2)}) async-start(), calls=%async_computation.3 | async-start | bytes 1310720 | tf_op jit(solution)/shard_map/all_gather | solution.py:819
  32.2 14.9 %collective-permute-start.7 = (bf16[256,1024]{1,0:T(8,128)(2,1)S(1)}, bf16[256,1024]{1,0:T(8,128)(2,1)S(1)}, u32[]{:S(2)}, u32[]{:S(2)}) collective-permute-start(bf16[256,1024]{1,0:T(8,128)(2,1)S(1)} %copy-done.24), channel_id=1, source_target_pairs={{1,0},{0,1},{3,2},{2,3},{5,4},{4,5},{7,6},{6,7},{9,8},{8,9},{11,10... | collective-permute-start | bytes 1572872 | tf_op jit(solution)/shard_map/ppermute | solution.py:700
  34.9 40.8 %copy-start.28 = (bf16[4,256,256]{2,1,0:T(8,128)(2,1)}, bf16[4,256,256]{2,1,0:T(8,128)(2,1)S(1)}, u32[]{:S(2)}) copy-start(bf16[4,256,256]{2,1,0:T(8,128)(2,1)S(1)} %collective-permute-done.1.refs_0_) | copy-start | bytes 1572868
  34.9 40.2 %collective-permute-start.4 = (bf16[4,256,256]{2,1,0:T(8,128)(2,1)S(1)}, bf16[4,256,256]{2,1,0:T(8,128)(2,1)S(1)}, u32[]{:S(2)}, u32[]{:S(2)}) collective-permute-start(bf16[4,256,256]{2,1,0:T(8,128)(2,1)S(1)} %collective-permute-done.1.refs_0_), channel_id=1, source_target_pairs={{4,28},{12,20},{20,12},{28,4},{5,29},{13,21},{21,13},{29,5},{6,30}... | collective-permute-start | bytes 1572872 | tf_op jit(solution)/shard_map/ppermute | solution.py:779
  35.6 39.6 %collective-permute-start.3 = (bf16[4,256,256]{2,1,0:T(8,128)(2,1)S(1)}, bf16[4,256,256]{2,1,0:T(8,128)(2,1)S(1)}, u32[]{:S(2)}, u32[]{:S(2)}) collective-permute-start(bf16[4,256,256]{2,1,0:T(8,128)(2,1)S(1)} %collective-permute-done.1.refs_0_), channel_id=1, source_target_pairs={{4,20},{12,28},{20,4},{28,12},{5,21},{13,29},{21,5},{29,13},{6,22}... | collective-permute-start | bytes 1572872 | tf_op jit(solution)/shard_map/ppermute | solution.py:779
  36.3 39.4 %collective-permute-start.2 = (bf16[4,256,256]{2,1,0:T(8,128)(2,1)S(1)}, bf16[4,256,256]{2,1,0:T(8,128)(2,1)S(1)}, u32[]{:S(2)}, u32[]{:S(2)}) collective-permute-start(bf16[4,256,256]{2,1,0:T(8,128)(2,1)S(1)} %collective-permute-done.1.refs_0_), channel_id=1, source_target_pairs={{4,12},{12,4},{20,28},{28,20},{5,13},{13,5},{21,29},{29,21},{6,14}... | collective-permute-start | bytes 1572872 | tf_op jit(solution)/shard_map/ppermute | solution.py:779
  37.0 43.1 %collective-permute-start.11 = (bf16[256,1024]{1,0:T(8,128)(2,1)}, bf16[256,1024]{1,0:T(8,128)(2,1)S(1)}, u32[]{:S(2)}, u32[]{:S(2)}) collective-permute-start(bf16[256,1024]{1,0:T(8,128)(2,1)} %norm_tokens.3.refs_4_.refs_16_), channel_id=1, source_target_pairs={{1,0},{0,1},{3,2},{2,3},{5,4},{4,5},{7,6},{6,7},{9,8},{8,9},{11,10... | collective-permute-start | bytes 1572872 | tf_op jit(solution)/shard_map/ppermute | solution.py:700
  47.1 33.0 %copy-start.25 = (bf16[256,1024]{1,0:T(8,128)(2,1)}, bf16[256,1024]{1,0:T(8,128)(2,1)S(1)}, u32[]{:S(2)}) copy-start(bf16[256,1024]{1,0:T(8,128)(2,1)S(1)} %collective-permute-done.7.refs_2_.refs_14_) | copy-start | bytes 1572868
  47.1 41.2 %collective-permute-start.10 = (bf16[256,1024]{1,0:T(8,128)(2,1)}, bf16[256,1024]{1,0:T(8,128)(2,1)S(1)}, u32[]{:S(2)}, u32[]{:S(2)}) collective-permute-start(bf16[256,1024]{1,0:T(8,128)(2,1)} %norm_tokens.3.refs_4_.refs_16_), channel_id=1, source_target_pairs={{0,4},{4,0},{8,12},{12,8},{16,20},{20,16},{24,28},{28,24},{1,5},{5... | collective-permute-start | bytes 1572872 | tf_op jit(solution)/shard_map/ppermute | solution.py:681
  75.1 13.2 %collective-permute-start.6 = (bf16[256,1024]{1,0:T(8,128)(2,1)S(1)}, bf16[256,1024]{1,0:T(8,128)(2,1)}, u32[]{:S(2)}, u32[]{:S(2)}) collective-permute-start(bf16[256,1024]{1,0:T(8,128)(2,1)S(1)} %copy-done.24), channel_id=1, source_target_pairs={{0,4},{4,0},{8,12},{12,8},{16,20},{20,16},{24,28},{28,24},{1,5},{5... | collective-permute-start | bytes 1572872 | tf_op jit(solution)/shard_map/ppermute | solution.py:681
  75.2 13.1 %collective-permute-start.9 = (bf16[256,1024]{1,0:T(8,128)(2,1)S(1)}, bf16[256,1024]{1,0:T(8,128)(2,1)}, u32[]{:S(2)}, u32[]{:S(2)}) collective-permute-start(bf16[256,1024]{1,0:T(8,128)(2,1)S(1)} %collective-permute-done.7.refs_2_.refs_14_), channel_id=1, source_target_pairs={{0,4},{4,0},{8,12},{12,8},{16,20},{20,16},{24,28},{28,24},{1,5},{5... | collective-permute-start | bytes 1572872 | tf_op jit(solution)/shard_map/ppermute | solution.py:681
  80.1 8.3 %collective-permute-start.12 = (bf16[256,1024]{1,0:T(8,128)(2,1)S(1)}, bf16[256,1024]{1,0:T(8,128)(2,1)}, u32[]{:S(2)}, u32[]{:S(2)}) collective-permute-start(bf16[256,1024]{1,0:T(8,128)(2,1)S(1)} %collective-permute-done.11.refs_6_.refs_18_), channel_id=1, source_target_pairs={{0,4},{4,0},{8,12},{12,8},{16,20},{20,16},{24,28},{28,24},{1,5},{5... | collective-permute-start | bytes 1572872 | tf_op jit(solution)/shard_map/ppermute | solution.py:681
  86.3 39.6 %collective-permute-start.13 = (bf16[512,1024]{1,0:T(8,128)(2,1)}, bf16[512,1024]{1,0:T(8,128)(2,1)S(1)}, u32[]{:S(2)}, u32[]{:S(2)}) collective-permute-start(bf16[512,1024]{1,0:T(8,128)(2,1)} %bitcast.24), channel_id=1, source_target_pairs={{0,0},{1,1},{2,4},{3,5},{4,2},{5,3},{6,6},{7,7},{8,8},{9,9},{10,12... | collective-permute-start | bytes 3145736 | tf_op jit(solution)/shard_map/ppermute | solution.py:710
  88.2 95.1 %all-gather.9.cloned.1.call-start = ((), (), s32[]{:S(2)}) async-start(), calls=%async_computation.2 | async-start | bytes 1310720 | tf_op jit(solution)/shard_map/all_gather | solution.py:819
  125.9 65.5 %copy-start.3 = (bf16[512,1024]{1,0:T(8,128)(2,1)}, bf16[512,1024]{1,0:T(8,128)(2,1)S(1)}, u32[]{:S(2)}) copy-start(bf16[512,1024]{1,0:T(8,128)(2,1)S(1)} %collective-permute-done.13.refs_2_.refs_4_.base_ref) | copy-start | bytes 3145732
  130.2 12.5 %collective-permute-start.15 = (bf16[512,1024]{1,0:T(8,128)(2,1)}, bf16[512,1024]{1,0:T(8,128)(2,1)S(1)}, u32[]{:S(2)}, u32[]{:S(2)}) collective-permute-start(bf16[512,1024]{1,0:T(8,128)(2,1)} %get-tuple-element.120), channel_id=1, source_target_pairs={{0,4},{4,0},{8,12},{12,8},{16,20},{20,16},{24,28},{28,24},{1,5},{5... | collective-permute-start | bytes 3145736 | tf_op jit(solution)/shard_map/ppermute | solution.py:681
  140.1 283.5 %reduce-scatter.2.cloned.1.call-start = ((), (), s32[]{:S(2)}) async-start(), calls=%async_computation.1 | async-start | bytes 3932160 | tf_op jit(solution)/shard_map/reduce_scatter | solution.py:883
  140.2 44.8 %collective-permute-start.14 = (bf16[512,1024]{1,0:T(8,128)(2,1)}, bf16[512,1024]{1,0:T(8,128)(2,1)}, u32[]{:S(2)}, u32[]{:S(2)}) collective-permute-start(bf16[512,1024]{1,0:T(8,128)(2,1)} %get-tuple-element.118), channel_id=1, source_target_pairs={{0,4},{4,0},{8,12},{12,8},{16,20},{20,16},{24,28},{28,24},{1,5},{5... | collective-permute-start | bytes 3145736 | tf_op jit(solution)/shard_map/ppermute | solution.py:681
  144.3 42.5 %collective-permute-start.16 = (bf16[512,1024]{1,0:T(8,128)(2,1)S(1)}, bf16[512,1024]{1,0:T(8,128)(2,1)}, u32[]{:S(2)}, u32[]{:S(2)}) collective-permute-start(bf16[512,1024]{1,0:T(8,128)(2,1)S(1)} %add_convert_fusion.4), channel_id=1, source_target_pairs={{1,0},{0,1},{3,2},{2,3},{5,4},{4,5},{7,6},{6,7},{9,8},{8,9},{11,10... | collective-permute-start | bytes 3145736 | tf_op jit(solution)/shard_map/ppermute | solution.py:700
  145.2 46.3 %collective-permute-start.21 = (bf16[4,128,1024]{2,1,0:T(8,128)(2,1)}, bf16[4,128,1024]{2,1,0:T(8,128)(2,1)}, u32[]{:S(2)}, u32[]{:S(2)}) collective-permute-start(bf16[4,128,1024]{2,1,0:T(8,128)(2,1)} %bitcast.79), channel_id=1, source_target_pairs={{0,8},{4,12},{8,0},{12,4},{16,24},{20,28},{24,16},{28,20},{1,9},{5... | collective-permute-start | bytes 3145736 | tf_op jit(solution)/shard_map/ppermute | solution.py:681
  146.5 47.5 %collective-permute-start.20 = (bf16[4,128,1024]{2,1,0:T(8,128)(2,1)}, bf16[4,128,1024]{2,1,0:T(8,128)(2,1)}, u32[]{:S(2)}, u32[]{:S(2)}) collective-permute-start(bf16[4,128,1024]{2,1,0:T(8,128)(2,1)} %bitcast.82), channel_id=1, source_target_pairs={{0,8},{4,12},{8,0},{12,4},{16,24},{20,28},{24,16},{28,20},{1,9},{5... | collective-permute-start | bytes 3145736 | tf_op jit(solution)/shard_map/ppermute | solution.py:681
  149.4 37.3 %copy-start.10 = (bf16[512,1024]{1,0:T(8,128)(2,1)}, bf16[512,1024]{1,0:T(8,128)(2,1)S(1)}, u32[]{:S(2)}) copy-start(bf16[512,1024]{1,0:T(8,128)(2,1)S(1)} %constant_dynamic-update-slice_fusion.x_ref) | copy-start | bytes 3145732
  183.3 32.1 %collective-permute-start.19 = (bf16[4,128,1024]{2,1,0:T(8,128)(2,1)}, bf16[4,128,1024]{2,1,0:T(8,128)(2,1)S(1)}, u32[]{:S(2)}, u32[]{:S(2)}) collective-permute-start(bf16[4,128,1024]{2,1,0:T(8,128)(2,1)} %bitcast.85), channel_id=1, source_target_pairs={{0,8},{4,12},{8,0},{12,4},{16,24},{20,28},{24,16},{28,20},{1,9},{5... | collective-permute-start | bytes 3145736 | tf_op jit(solution)/shard_map/ppermute | solution.py:681
  185.0 30.4 %collective-permute-start.18 = (bf16[512,1024]{1,0:T(8,128)(2,1)S(1)}, bf16[512,1024]{1,0:T(8,128)(2,1)S(1)}, u32[]{:S(2)}, u32[]{:S(2)}) collective-permute-start(bf16[512,1024]{1,0:T(8,128)(2,1)S(1)} %collective-permute-done.13.refs_2_.refs_4_.base_ref), channel_id=1, source_target_pairs={{0,4},{4,0},{8,12},{12,8},{16,20},{20,16},{24,28},{28,24},{1,5},{5... | collective-permute-start | bytes 3145736 | tf_op jit(solution)/shard_map/ppermute | solution.py:681
  191.5 24.0 %collective-permute-start.17 = (bf16[512,1024]{1,0:T(8,128)(2,1)}, bf16[512,1024]{1,0:T(8,128)(2,1)S(1)}, u32[]{:S(2)}, u32[]{:S(2)}) collective-permute-start(bf16[512,1024]{1,0:T(8,128)(2,1)} %get-tuple-element.147.refs_0_), channel_id=1, source_target_pairs={{0,4},{4,0},{8,12},{12,8},{16,20},{20,16},{24,28},{28,24},{1,5},{5... | collective-permute-start | bytes 3145736 | tf_op jit(solution)/shard_map/ppermute | solution.py:681
  191.5 47.6 %collective-permute-start.25 = (bf16[512,1024]{1,0:T(8,128)(2,1)S(1)}, bf16[512,1024]{1,0:T(8,128)(2,1)S(1)}, u32[]{:S(2)}, u32[]{:S(2)}) collective-permute-start(bf16[512,1024]{1,0:T(8,128)(2,1)S(1)} %collective-permute-done.13.refs_2_.refs_4_.base_ref), channel_id=1, source_target_pairs={{0,16},{4,20},{8,24},{12,28},{16,0},{20,4},{24,8},{28,12},{1,17},{... | collective-permute-start | bytes 3145736 | tf_op jit(solution)/shard_map/ppermute | solution.py:681
  194.0 45.6 %collective-permute-start.22 = (bf16[512,1024]{1,0:T(8,128)(2,1)}, bf16[512,1024]{1,0:T(8,128)(2,1)S(1)}, u32[]{:S(2)}, u32[]{:S(2)}) collective-permute-start(bf16[512,1024]{1,0:T(8,128)(2,1)} %get-tuple-element.147.refs_0_), channel_id=1, source_target_pairs={{0,16},{4,20},{8,24},{12,28},{16,0},{20,4},{24,8},{28,12},{1,17},{... | collective-permute-start | bytes 3145736 | tf_op jit(solution)/shard_map/ppermute | solution.py:681
  239.0 3.4 collective-permute-start.23
  239.1 4.1 collective-permute-start.26
  239.6 5.1 collective-permute-start.24
  266.9 2.9 collective-permute-start.27
  267.1 19.6 %collective-permute-start.29 = (bf16[512,1024]{1,0:T(8,128)(2,1)}, bf16[512,1024]{1,0:T(8,128)(2,1)S(1)}, u32[]{:S(2)}, u32[]{:S(2)}) collective-permute-start(bf16[512,1024]{1,0:T(8,128)(2,1)} %get-tuple-element.142), channel_id=1, source_target_pairs={{0,4},{4,0},{8,12},{12,8},{16,20},{20,16},{24,28},{28,24},{1,5},{5... | collective-permute-start | bytes 3145736 | tf_op jit(solution)/shard_map/ppermute | solution.py:681
  271.5 25.3 %collective-permute-start.28 = (bf16[512,1024]{1,0:T(8,128)(2,1)S(1)}, bf16[512,1024]{1,0:T(8,128)(2,1)S(1)}, u32[]{:S(2)}, u32[]{:S(2)}) collective-permute-start(bf16[512,1024]{1,0:T(8,128)(2,1)S(1)} %add_convert_fusion.3), channel_id=1, source_target_pairs={{0,16},{4,20},{8,24},{12,28},{16,0},{20,4},{24,8},{28,12},{1,17},{... | collective-permute-start | bytes 3145736 | tf_op jit(solution)/shard_map/ppermute | solution.py:681
  285.1 11.6 %collective-permute-start.30 = (bf16[512,1024]{1,0:T(8,128)(2,1)S(1)}, bf16[512,1024]{1,0:T(8,128)(2,1)S(1)}, u32[]{:S(2)}, u32[]{:S(2)}) collective-permute-start(bf16[512,1024]{1,0:T(8,128)(2,1)S(1)} %copy-done.42), channel_id=1, source_target_pairs={{0,4},{4,0},{8,12},{12,8},{16,20},{20,16},{24,28},{28,24},{1,5},{5... | collective-permute-start | bytes 3145736 | tf_op jit(solution)/shard_map/ppermute | solution.py:681
  285.2 71.0 %collective-permute-start.35 = (bf16[4,3,1024,128]{3,2,1,0:T(8,128)(2,1)}, bf16[4,3,1024,128]{3,2,1,0:T(8,128)(2,1)}, u32[]{:S(2)}, u32[]{:S(2)}) collective-permute-start(bf16[4,3,1024,128]{3,2,1,0:T(8,128)(2,1)} %feed_forward_weights.2), channel_id=1, source_target_pairs={{0,8},{4,12},{8,0},{12,4},{16,24},{20,28},{24,16},{28,20},{1,9},{5... | collective-permute-start | bytes 9437192 | tf_op jit(solution)/shard_map/ppermute | solution.py:681
  302.8 2.9 collective-permute-start.31
  302.9 25.6 %collective-permute-start.33 = (bf16[512,1024]{1,0:T(8,128)(2,1)S(1)}, bf16[512,1024]{1,0:T(8,128)(2,1)S(1)}, u32[]{:S(2)}, u32[]{:S(2)}) collective-permute-start(bf16[512,1024]{1,0:T(8,128)(2,1)S(1)} %add_convert_fusion.2), channel_id=1, source_target_pairs={{0,16},{4,20},{8,24},{12,28},{16,0},{20,4},{24,8},{28,12},{1,17},{... | collective-permute-start | bytes 3145736 | tf_op jit(solution)/shard_map/ppermute | solution.py:681
  304.3 28.7 %collective-permute-start.32 = (bf16[512,1024]{1,0:T(8,128)(2,1)}, bf16[512,1024]{1,0:T(8,128)(2,1)S(1)}, u32[]{:S(2)}, u32[]{:S(2)}) collective-permute-start(bf16[512,1024]{1,0:T(8,128)(2,1)} %get-tuple-element.146.refs_2_), channel_id=1, source_target_pairs={{1,0},{0,1},{3,2},{2,3},{5,4},{4,5},{7,6},{6,7},{9,8},{8,9},{11,10... | collective-permute-start | bytes 3145736 | tf_op jit(solution)/shard_map/ppermute | solution.py:700
  333.0 2.7 collective-permute-start.34
  333.1 27.6 %collective-permute-start.36 = (bf16[512,1024]{1,0:T(8,128)(2,1)}, bf16[512,1024]{1,0:T(8,128)(2,1)S(1)}, u32[]{:S(2)}, u32[]{:S(2)}) collective-permute-start(bf16[512,1024]{1,0:T(8,128)(2,1)} %output_sum.1), channel_id=1, source_target_pairs={{0,0},{1,1},{2,4},{3,5},{4,2},{5,3},{6,6},{7,7},{8,8},{9,9},{10,12... | collective-permute-start | bytes 3145736 | tf_op jit(solution)/shard_map/ppermute | solution.py:710
  360.7 125.6 %all-gather.15.cloned.1.call-start = ((), (), s32[]{:S(2)}) async-start(), calls=%async_computation.5 | async-start | bytes 7077888 | tf_op jit(solution)/shard_map/all_gather | solution.py:901
  408.7 5.1 collective-permute-start.37
  423.6 7.0 %collective-permute-start.38 = (bf16[512,1024]{1,0:T(8,128)(2,1)}, bf16[512,1024]{1,0:T(8,128)(2,1)S(1)}, u32[]{:S(2)}, u32[]{:S(2)}) collective-permute-start(bf16[512,1024]{1,0:T(8,128)(2,1)} %get-tuple-element.183), channel_id=1, source_target_pairs={{0,4},{4,0},{8,12},{12,8},{16,20},{20,16},{24,28},{28,24},{1,5},{5... | collective-permute-start | bytes 3145736 | tf_op jit(solution)/shard_map/ppermute | solution.py:681
  424.1 25.2 %collective-permute-start.39 = (bf16[512,1024]{1,0:T(8,128)(2,1)S(1)}, bf16[512,1024]{1,0:T(8,128)(2,1)S(1)}, u32[]{:S(2)}, u32[]{:S(2)}) collective-permute-start(bf16[512,1024]{1,0:T(8,128)(2,1)S(1)} %add_convert_fusion.1), channel_id=1, source_target_pairs={{1,0},{0,1},{3,2},{2,3},{5,4},{4,5},{7,6},{6,7},{9,8},{8,9},{11,10... | collective-permute-start | bytes 3145736 | tf_op jit(solution)/shard_map/ppermute | solution.py:700
  427.1 27.6 %collective-permute-start.43 = (bf16[4,256,256]{2,1,0:T(8,128)(2,1)}, bf16[4,256,256]{2,1,0:T(8,128)(2,1)}, u32[]{:S(2)}, u32[]{:S(2)}) collective-permute-start(bf16[4,256,256]{2,1,0:T(8,128)(2,1)} %get-tuple-element.198), channel_id=1, source_target_pairs={{0,24},{4,28},{8,16},{12,20},{16,8},{20,12},{24,0},{28,4},{1,25},{... | collective-permute-start | bytes 1572872 | tf_op jit(solution)/shard_map/ppermute | solution.py:681
  429.4 32.2 %collective-permute-start.42 = (bf16[4,256,256]{2,1,0:T(8,128)(2,1)}, bf16[4,256,256]{2,1,0:T(8,128)(2,1)}, u32[]{:S(2)}, u32[]{:S(2)}) collective-permute-start(bf16[4,256,256]{2,1,0:T(8,128)(2,1)} %get-tuple-element.199), channel_id=1, source_target_pairs={{0,16},{4,20},{8,24},{12,28},{16,0},{20,4},{24,8},{28,12},{1,17},{... | collective-permute-start | bytes 1572872 | tf_op jit(solution)/shard_map/ppermute | solution.py:681
  429.9 31.7 %collective-permute-start.41 = (bf16[4,256,256]{2,1,0:T(8,128)(2,1)}, bf16[4,256,256]{2,1,0:T(8,128)(2,1)}, u32[]{:S(2)}, u32[]{:S(2)}) collective-permute-start(bf16[4,256,256]{2,1,0:T(8,128)(2,1)} %get-tuple-element.200), channel_id=1, source_target_pairs={{0,8},{4,12},{8,0},{12,4},{16,24},{20,28},{24,16},{28,20},{1,9},{5... | collective-permute-start | bytes 1572872 | tf_op jit(solution)/shard_map/ppermute | solution.py:681
  454.7 26.0 %copy-start.11 = (bf16[512,1024]{1,0:T(8,128)(2,1)S(1)}, bf16[512,1024]{1,0:T(8,128)(2,1)}, u32[]{:S(2)}) copy-start(bf16[512,1024]{1,0:T(8,128)(2,1)} %tokens_grad.1) | copy-start | bytes 3145732
  463.4 17.0 %collective-permute-start.44 = (bf16[4,256,256]{2,1,0:T(8,128)(2,1)S(1)}, bf16[4,256,256]{2,1,0:T(8,128)(2,1)S(1)}, u32[]{:S(2)}, u32[]{:S(2)}) collective-permute-start(bf16[4,256,256]{2,1,0:T(8,128)(2,1)S(1)} %fusion.2), channel_id=1, source_target_pairs={{4,2},{5,3},{6,0},{7,1},{12,10},{13,11},{14,8},{15,9},{20,18},{21,... | collective-permute-start | bytes 1572872 | tf_op jit(solution)/shard_map/ppermute | solution.py:914
  480.5 2.1 collective-permute-start.45
  480.6 40.0 %collective-permute-start.40 = (bf16[512,1024]{1,0:T(8,128)(2,1)S(1)}, bf16[512,1024]{1,0:T(8,128)(2,1)S(1)}, u32[]{:S(2)}, u32[]{:S(2)}) collective-permute-start(bf16[512,1024]{1,0:T(8,128)(2,1)S(1)} %copy-done.11), channel_id=1, source_target_pairs={{0,0},{1,1},{2,4},{3,5},{4,2},{5,3},{6,6},{7,7},{8,8},{9,9},{10,12... | collective-permute-start | bytes 3145736 | tf_op jit(solution)/shard_map/ppermute | solution.py:710
  482.7 15.6 %collective-permute-start.48 = (bf16[4,256,256]{2,1,0:T(8,128)(2,1)S(1)}, bf16[4,256,256]{2,1,0:T(8,128)(2,1)}, u32[]{:S(2)}, u32[]{:S(2)}) collective-permute-start(bf16[4,256,256]{2,1,0:T(8,128)(2,1)S(1)} %broadcast_select_fusion.refs_0_), channel_id=1, source_target_pairs={{0,24},{4,28},{8,16},{12,20},{16,8},{20,12},{24,0},{28,4},{1,25},{... | collective-permute-start | bytes 1572872 | tf_op jit(solution)/shard_map/ppermute | solution.py:681
  484.5 25.3 %collective-permute-start.47 = (bf16[4,256,256]{2,1,0:T(8,128)(2,1)S(1)}, bf16[4,256,256]{2,1,0:T(8,128)(2,1)}, u32[]{:S(2)}, u32[]{:S(2)}) collective-permute-start(bf16[4,256,256]{2,1,0:T(8,128)(2,1)S(1)} %broadcast_select_fusion.refs_0_), channel_id=1, source_target_pairs={{0,16},{4,20},{8,24},{12,28},{16,0},{20,4},{24,8},{28,12},{1,17},{... | collective-permute-start | bytes 1572872 | tf_op jit(solution)/shard_map/ppermute | solution.py:681
  485.7 24.1 %collective-permute-start.46 = (bf16[4,256,256]{2,1,0:T(8,128)(2,1)S(1)}, bf16[4,256,256]{2,1,0:T(8,128)(2,1)}, u32[]{:S(2)}, u32[]{:S(2)}) collective-permute-start(bf16[4,256,256]{2,1,0:T(8,128)(2,1)S(1)} %broadcast_select_fusion.refs_0_), channel_id=1, source_target_pairs={{0,8},{4,12},{8,0},{12,4},{16,24},{20,28},{24,16},{28,20},{1,9},{5... | collective-permute-start | bytes 1572872 | tf_op jit(solution)/shard_map/ppermute | solution.py:681
  497.3 26.6 %copy-start.37 = (f32[1024]{0:T(1024)S(1)}, f32[1024]{0:T(1024)}, u32[]{:S(2)}) copy-start(f32[1024]{0:T(1024)} %param.15) | copy-start | bytes 12292
  497.3 26.6 %copy-start.38 = (f32[1024]{0:T(1024)S(1)}, f32[1024]{0:T(1024)}, u32[]{:S(2)}) copy-start(f32[1024]{0:T(1024)} %param.16) | copy-start | bytes 12292
  497.3 27.9 %copy-start.19 = (bf16[512,1024]{1,0:T(8,128)(2,1)S(1)}, bf16[512,1024]{1,0:T(8,128)(2,1)}, u32[]{:S(2)}) copy-start(bf16[512,1024]{1,0:T(8,128)(2,1)} %copy-done.18) | copy-start | bytes 3145732
  514.9 3.7 collective-permute-start.49
  519.3 4.6 collective-permute-start.50
  (35 other events, 209.6 us)
Sparse Core Ops, SparseCore 0:
  32.3 54.1 all-gather.12
  88.4 42.9 all-gather.10
  140.3 43.0 all-gather.8
  360.8 61.7 reduce-scatter.1
  424.3 60.9 all-gather.14

commit v4 on v3

--- a/solution.py
+++ b/solution.py
@@ -54,7 +54,7 @@
 
 def norm_call(x, gain):
     n, d = x.shape
-    b = min(128, n)
+    b = min(256, n)
     return call(
         norm_kernel,
         "norm_tokens",
@@ -77,7 +77,7 @@
 
 def middle_call(x, gain, parts):
     n, d = x.shape
-    b = min(128, n)
+    b = min(256, n)
     row = pl.BlockSpec((b, d), lambda i: (i, 0))
     return call(
         middle_kernel,
@@ -435,31 +435,37 @@
     )(pack, *flat)
 
 
-def qkv_weight_kernel(n_parts, n_groups, wo_ref, *refs):
-    grads, parts, dw_ref = refs[: 3 * n_groups], refs[3 * n_groups : -1], refs[-1]
+def qkv_weight_kernel(n_parts, n_groups, J, index_ref, wo_ref, *refs):
+    grads, parts = refs[: 3 * n_groups], refs[3 * n_groups : 3 * n_groups + n_parts]
+    outs, held = refs[3 * n_groups + n_parts : -1], refs[-1]
     n = parts[0].shape[0]
-    J, _, a, b = dw_ref.shape
+    a = outs[0].shape[1]
     for j in range(3):
         total = None
         for i, p in enumerate(parts):
             g = stack_rows(grads[j::3], part_cols(i, n_parts, n))
             term = dot(p[...], g, 0, 1)
             total = term if total is None else total + term
-        dw_ref[:, j] = total.astype(BF16).reshape(J, a, b)
-    dw_ref[:, 3] = wo_ref[...]
-
-
-def qkv_weight_call(wo_grad, grads, parts, pack_shape):
-    n, d = parts[0].shape
-    f = pack_shape[-1]
-    S = n * len(parts)
+        held[...] = total.astype(BF16).reshape(held.shape)
+        for k in range(J):
+            outs[k][j] = held[index_ref[k]]
+    for k in range(J):
+        outs[k][3] = wo_ref[index_ref[k]]
+
+
+def qkv_weight_call(index, wo_grad, grads, parts, pack_shape):
+    J, four, a, b = pack_shape
     flat = [g for group in grads for g in group]
-    return call(
-        functools.partial(qkv_weight_kernel, len(parts), len(grads)),
+    vmem = pl.BlockSpec(memory_space=pltpu.VMEM)
+    return call(
+        functools.partial(qkv_weight_kernel, len(parts), len(grads), J),
         "qkv_weights",
-        shape(pack_shape, BF16),
+        (shape((four, a, b), BF16),) * J,
         us=8,
-    )(wo_grad, *flat, *parts)
+        in_specs=[pl.BlockSpec(memory_space=pltpu.SMEM)] + [vmem] * (1 + len(flat) + len(parts)),
+        out_specs=(vmem,) * J,
+        scratch_shapes=[pltpu.VMEM((J, a, b), BF16)],
+    )(index, wo_grad, *flat, *parts)
 
 
 def pack_kernel(n_parts, index_ref, q_ref, o_ref, *refs):
@@ -822,7 +828,7 @@
         weights = [own_units] + [[mid_from(z, k) for z in own_units] for k in range(1, M)]
         q, k, v = qkv_call(normed_one, pack, cos, sin)
         heads = f // HEAD_DIM
-        count = max(1, heads // 2)
+        count = heads
         o, lse = [], []
         for first in range(0, heads, count):
             if first:
@@ -839,8 +845,7 @@
         xs = gather_units(normed)
         near = ffn_call(xs[:2], cots[:2], weights)
         near_dx = core_flip(near[6])
-        far_x, near_dx = tie(xs[2], near_dx)
-        far = ffn_call([far_x, xs[3]], cots[2:], weights)
+        far = ffn_call([after(xs[2], near[0]), xs[3]], cots[2:], weights)
 
         def core_sum(mine, theirs):
             return (mine.astype(F32) + core_flip(theirs).astype(F32)).astype(BF16)
@@ -891,20 +896,17 @@
         sums, mine = sum_heads(pieces)
         rows = [row_from(z, R - k) for k, z in enumerate(sums, 1)]
         wo_grad, *sums = tie(wo_grad, *sums)
-        dw = qkv_weight_call(wo_grad, back, normed_one, pack.shape)
-
-        def share_of(k):
-            return lax.dynamic_index_in_dim(dw, pair ^ k, 0, keepdims=False)
-
-        travelled = [pair_from(share_of(k), k) for k in range(1, J)]
-        slices, dw = tie(slices, dw)
+        dw = qkv_weight_call(index, wo_grad, back, normed_one, pack.shape)
+
+        travelled = [pair_from(dw[k], k) for k in range(1, J)]
+        slices, share = tie(slices, dw[0])
         slices = lax.all_gather(slices, "dp", axis=0)
         tokens_low = back_call(
-            "tokens_grad", middle_grad, after(x, dw), gain_one, mine + rows, 0
+            "tokens_grad", middle_grad, after(x, share), gain_one, mine + rows, 0
         )[0]
         tokens_grad = reshard(tokens_low)[:, None]
         tokens_low, *travelled = tie(tokens_low, *travelled)
-        part = share_of(0).astype(F32)
+        part = share.astype(F32)
         for p in travelled:
             part = part + p.astype(F32)
         part = part.astype(BF16)

time: 541 us -> 535 us (0.989)
    ppermute x5, waiting for transfers between devices: 30.4 us -> 66 us  [row_from(): lax.ppermute(x, 'tensor', [(t // R * R + (t % R + k) % R, t) for t in ran...]
    all_gather x3, waiting for transfers between devices: 33.9 us -> 0.02 us  [on_device(): lax.all_gather(z, 'tensor', axis=0)]
    pallas_call x2 -> x1, Pallas kernels: 29.3 us -> 27 us  [attend_call(): call(functools.partial(attend_kernel, sub=sub), 'attend', (shape((count *...]
    unnamed x92 -> x82, local copies, waits for them, and re-layouts: 13.2 us -> 15.5 us
  transfers between devices with their start and end apart: 56 -> 56, of which waited for: 23 -> 20; matrix products, arithmetic and copies ran while one was open for 6% -> 5% of each run, Pallas kernels for 38% -> 38%
where the time goes in v4:
time: 535 us; the launch traced here: 530 us
  Pallas kernels  222 us (41%)
  waiting for transfers between devices  161 us (30%)
  starting transfers between devices  88.4 us (17%)
  local copies, waits for them, and re-layouts  26.8 us (5%)
  other arithmetic  16.3 us (3%)
  between operations  15.3 us (3%)
    ppermute x34, waiting for transfers between devices, over_dp(): return lax.ppermute(x, 'dp', [(i, f(i)) for i in range(DP)])  72.1 us
    ppermute x34, starting transfers between devices, over_dp(): return lax.ppermute(x, 'dp', [(i, f(i)) for i in range(DP)])  67.3 us
    ppermute x5, waiting for transfers between devices, row_from(): lax.ppermute(x, 'tensor', [(t // R * R + (t % R + k) % R, t) for t in ran...  66 us
    pallas_call x4, Pallas kernels, attend_back_call(): call(functools.partial(attend_back_kernel, sub=min(256, S)), 'attend_back...  54.3 us
    pallas_call x2, Pallas kernels, ffn_call(): call(functools.partial(ffn_kernel, groups, steps), 'feed_forward', (shape...  42.4 us
    pallas_call x1, Pallas kernels, attend_call(): call(functools.partial(attend_kernel, sub=sub), 'attend', (shape((count *...  27 us
    pallas_call x2, Pallas kernels, ffn_weight_call(): call(functools.partial(ffn_weight_kernel, T, us), 'feed_forward_weights',...  24.7 us
    ppermute x1, waiting for transfers between devices, on_device(): moved = lax.ppermute(part, ('dp', 'tensor'), home_pairs)  15.5 us
  transfers between devices with their start and end apart: 56, of which 20 were waited for; matrix products, arithmetic and copies ran while one was open for 5% of the time, Pallas kernels for 38%

profile of v4, /device:TPU:0, one launch (start us, length us, event | category | flops | bytes accessed | tf_op | source)
XLA Modules:
  0.0 529.7 jit_solution(10290507187650162209)
XLA Ops:
  9.3 2.2 slice_bitcast_fusion
  11.5 1.7 collective-permute-start.8
  13.2 1.7 collective-permute-start
  16.2 1.6 dynamic-slice_bitcast_fusion.1
  19.5 1.4 constant_dynamic-slice_fusion.1
  22.3 1.8 multiply_sine_fusion
  27.0 2.2 norm_tokens.2.refs_0_.refs_12_
  30.0 2.2 norm_tokens.3.refs_4_.refs_16_
  32.3 2.7 collective-permute-start.7
  37.1 10.1 %collective-permute-done.7.refs_2_.refs_14_ = bf16[256,1024]{1,0:T(8,128)(2,1)} collective-permute-done((bf16[256,1024]{1,0:T(8,128)(2,1)}, bf16[256,1024]{1,0:T(8,128)(2,1)}, u32[]{:S(2)}, u32[]{:S(2)}) %collective-permute-start.7) | collective-permute-done | bytes 524320 | tf_op jit(solution)/shard_map/ppermute | solution.py:706
  47.2 27.6 %collective-permute-start.10 = (bf16[256,1024]{1,0:T(8,128)(2,1)}, bf16[256,1024]{1,0:T(8,128)(2,1)}, u32[]{:S(2)}, u32[]{:S(2)}) collective-permute-start(bf16[256,1024]{1,0:T(8,128)(2,1)} %norm_tokens.3.refs_4_.refs_16_), channel_id=1, source_target_pairs={{0,4},{4,0},{8,12},{12,8},{16,20},{20,16},{24,28},{28,24},{1,5},{5... | collective-permute-start | bytes 1572872 | tf_op jit(solution)/shard_map/ppermute | solution.py:687
  76.1 3.7 pack_heads.1.w_ref
  79.8 6.2 %collective-permute-start.12 = (bf16[256,1024]{1,0:T(8,128)(2,1)}, bf16[256,1024]{1,0:T(8,128)(2,1)S(1)}, u32[]{:S(2)}, u32[]{:S(2)}) collective-permute-start(bf16[256,1024]{1,0:T(8,128)(2,1)} %collective-permute-done.11.refs_6_.refs_18_), channel_id=1, source_target_pairs={{0,4},{4,0},{8,12},{12,8},{16,20},{20,16},{24,28},{28,24},{1,5},{5... | collective-permute-start | bytes 1572872 | tf_op jit(solution)/shard_map/ppermute | solution.py:687
  88.6 7.5 %project_heads.1 = (bf16[256,2048]{1,0:T(8,128)(2,1)}, bf16[256,2048]{1,0:T(8,128)(2,1)}, bf16[256,2048]{1,0:T(8,128)(2,1)}) custom-call(f32[32,2048]{1,0:T(8,128)} %get-tuple-element.201.c_ref.ck_ref, f32[32,2048]{1,0:T(8,128)} %get-tuple-element.200.s_ref.sk_ref, bf16[4,4,256,256]{3,2,1,0:T(8,128)(2,1)} %pack_heads.1.w_ref, ...), custom_call_target="tpu_custom_call" | custom-call | flops 2184999936 | tf_op jit(solution)/shard_map/project_heads/pallas_call | solution.py:186
  96.1 27.0 %attend.1 = (bf16[256,2048]{1,0:T(8,128)(2,1)}, f32[4,8,2048]{2,1,0:T(8,128)}) custom-call(bf16[256,2048]{1,0:T(8,128)(2,1)} %get-tuple-element.106.q_ref, bf16[256,2048]{1,0:T(8,128)(2,1)} %get-tuple-element.107.k_ref, bf16[256,2048]{1,0:T(8,128)(2,1)} %get-tuple-element.108.v_ref, bf16[16,2048]{1,0:T(8,128)(2,1)} %concatenate.41.b_ref), custom_call_target="tpu_custom_call" | custom-call | flops 8510000128 | tf_op jit(solution)/shard_map/attend/pallas_call | solution.py:242
  123.1 4.2 output_projection.1
  127.3 12.7 %collective-permute-start.15 = (bf16[512,1024]{1,0:T(8,128)(2,1)}, bf16[512,1024]{1,0:T(8,128)(2,1)S(1)}, u32[]{:S(2)}, u32[]{:S(2)}) collective-permute-start(bf16[512,1024]{1,0:T(8,128)(2,1)} %get-tuple-element.116), channel_id=1, source_target_pairs={{0,4},{4,0},{8,12},{12,8},{16,20},{20,16},{24,28},{28,24},{1,5},{5... | collective-permute-start | bytes 3145736 | tf_op jit(solution)/shard_map/ppermute | solution.py:687
  140.1 4.0 collective-permute-done.15
  144.0 1.6 add_convert_fusion.4
  150.8 1.3 collective-permute-start.25
  152.2 35.9 %collective-permute-done.16.refs_2_ = bf16[512,1024]{1,0:T(8,128)(2,1)} collective-permute-done((bf16[512,1024]{1,0:T(8,128)(2,1)S(1)}, bf16[512,1024]{1,0:T(8,128)(2,1)}, u32[]{:S(2)}, u32[]{:S(2)}) %collective-permute-start.16) | collective-permute-done | bytes 1048608 | tf_op jit(solution)/shard_map/ppermute | solution.py:706
  188.1 3.9 middle_norm.1
  193.3 1.6 collective-permute-start.19
  195.4 21.4 %collective-permute-done.23.refs_0_.refs_2_ = bf16[512,1024]{1,0:T(8,128)(2,1)S(1)} collective-permute-done((bf16[512,1024]{1,0:T(8,128)(2,1)}, bf16[512,1024]{1,0:T(8,128)(2,1)S(1)}, u32[]{:S(2)}, u32[]{:S(2)}) %collective-permute-start.23) | collective-permute-done | bytes 1048608 | tf_op jit(solution)/shard_map/ppermute | solution.py:687
  216.8 2.3 collective-permute-done.19.refs_7_
  221.0 21.2 %feed_forward.2 = (bf16[1024,1024]{1,0:T(8,128)(2,1)}, bf16[1024,1024]{1,0:T(8,128)(2,1)}, bf16[1024,1024]{1,0:T(8,128)(2,1)}, bf16[512,1024]{1,0:T(8,128)(2,1)}...) custom-call(bf16[512,1024]{1,0:T(8,128)(2,1)} %get-tuple-element.142.refs_0_, ...), custom_call_target="tpu_custom_call" | custom-call | flops 6037499904 | tf_op jit(solution)/shard_map/feed_forward/pallas_call | solution.py:588
  244.2 21.2 %feed_forward.3 = (bf16[1024,1024]{1,0:T(8,128)(2,1)}, bf16[1024,1024]{1,0:T(8,128)(2,1)}, bf16[1024,1024]{1,0:T(8,128)(2,1)}, bf16[512,1024]{1,0:T(8,128)(2,1)}...) custom-call(bf16[512,1024]{1,0:T(8,128)(2,1)} %copy-done.5, ...), custom_call_target="tpu_custom_call" | custom-call | flops 6037499904 | tf_op jit(solution)/shard_map/feed_forward/pallas_call | solution.py:588
  265.9 2.4 collective-permute-done.27
  268.3 1.6 add_convert_fusion.3
  270.7 12.1 %feed_forward_weights.2 = bf16[4,3,1024,128]{3,2,1,0:T(8,128)(2,1)} custom-call(bf16[512,1024]{1,0:T(8,128)(2,1)} %get-tuple-element.142.refs_0_, bf16[512,1024]{1,0:T(8,128)(2,1)} %copy-done.6, bf16[512,1024]{1,0:T(8,128)(2,1)} %copy-done.5, bf16[512,1024]{1,0:T(8,128)(2,1)} %copy-done.8, bf16[512,1024]{1,0:T(8,128)(2,1)} %copy-done.3, ...), custom_call_target="tpu_custom_call" | custom-call | flops 3564999936 | tf_op jit(solution)/shard_map/feed_forward_weights/pallas_call | solution.py:628
  285.1 10.1 %collective-permute-done.28.refs_2_ = bf16[512,1024]{1,0:T(8,128)(2,1)S(1)} collective-permute-done((bf16[512,1024]{1,0:T(8,128)(2,1)S(1)}, bf16[512,1024]{1,0:T(8,128)(2,1)S(1)}, u32[]{:S(2)}, u32[]{:S(2)}) %collective-permute-start.28) | collective-permute-done | bytes 1048608 | tf_op jit(solution)/shard_map/ppermute | solution.py:687
  296.5 5.1 middle_grad.1
  302.4 2.1 collective-permute-done.31.refs_2_
  304.5 12.5 %feed_forward_weights.3 = bf16[4,3,1024,128]{3,2,1,0:T(8,128)(2,1)} custom-call(bf16[512,1024]{1,0:T(8,128)(2,1)} %get-tuple-element.142.refs_0_, bf16[512,1024]{1,0:T(8,128)(2,1)} %copy-done.6, bf16[512,1024]{1,0:T(8,128)(2,1)} %copy-done.5, bf16[512,1024]{1,0:T(8,128)(2,1)} %copy-done.8, bf16[512,1024]{1,0:T(8,128)(2,1)} %copy-done.3, ...), custom_call_target="tpu_custom_call" | custom-call | flops 3564999936 | tf_op jit(solution)/shard_map/feed_forward_weights/pallas_call | solution.py:628
  317.1 10.2 %collective-permute-done.33.refs_2_ = bf16[512,1024]{1,0:T(8,128)(2,1)S(1)} collective-permute-done((bf16[512,1024]{1,0:T(8,128)(2,1)S(1)}, bf16[512,1024]{1,0:T(8,128)(2,1)S(1)}, u32[]{:S(2)}, u32[]{:S(2)}) %collective-permute-start.33) | collective-permute-done | bytes 1048608 | tf_op jit(solution)/shard_map/ppermute | solution.py:687
  328.2 3.5 output_sum.1
  331.7 1.9 collective-permute-start.36
  335.4 5.9 %heads_grad.1 = (bf16[256,2048]{1,0:T(8,128)(2,1)}, bf16[4,256,256]{2,1,0:T(8,128)(2,1)}) custom-call(bf16[4,4,256,256]{3,2,1,0:T(8,128)(2,1)} %pack_heads.1.w_ref, bf16[256,2048]{1,0:T(8,128)(2,1)} %get-tuple-element.111.refs_0_.o_ref, bf16[512,1024]{1,0:T(8,128)(2,1)} %get-tuple-element.141.refs_1_, bf16[512,1024]{1,0:T(8,128)(2,1)} %copy-done.11, ...), custom_call_target="tpu_custom_call" | custom-call | flops 1724999936 | tf_op jit(solution)/shard_map/heads_grad/pallas_call | solution.py:401
  341.4 13.6 %attend_back.4 = (bf16[64,2048]{1,0:T(8,128)(2,1)}, bf16[64,2048]{1,0:T(8,128)(2,1)}, bf16[64,2048]{1,0:T(8,128)(2,1)}) custom-call(bf16[256,2048]{1,0:T(8,128)(2,1)} %get-tuple-element.106.q_ref, bf16[256,2048]{1,0:T(8,128)(2,1)} %get-tuple-element.107.k_ref, bf16[256,2048]{1,0:T(8,128)(2,1)} %get-tuple-element.108.v_ref, ...), custom_call_target="tpu_custom_call" | custom-call | flops 3536250112 | tf_op jit(solution)/shard_map/attend_back/pallas_call | solution.py:315
  354.9 4.4 add_convert_fusion
  359.4 13.6 %attend_back.5 = (bf16[64,2048]{1,0:T(8,128)(2,1)}, bf16[64,2048]{1,0:T(8,128)(2,1)}, bf16[64,2048]{1,0:T(8,128)(2,1)}) custom-call(bf16[256,2048]{1,0:T(8,128)(2,1)} %get-tuple-element.106.q_ref, bf16[256,2048]{1,0:T(8,128)(2,1)} %get-tuple-element.107.k_ref, bf16[256,2048]{1,0:T(8,128)(2,1)} %get-tuple-element.108.v_ref, ...), custom_call_target="tpu_custom_call" | custom-call | flops 3536250112 | tf_op jit(solution)/shard_map/attend_back/pallas_call | solution.py:315
  373.1 13.5 %attend_back.6 = (bf16[64,2048]{1,0:T(8,128)(2,1)}, bf16[64,2048]{1,0:T(8,128)(2,1)}, bf16[64,2048]{1,0:T(8,128)(2,1)}) custom-call(bf16[256,2048]{1,0:T(8,128)(2,1)} %get-tuple-element.106.q_ref, bf16[256,2048]{1,0:T(8,128)(2,1)} %get-tuple-element.107.k_ref, bf16[256,2048]{1,0:T(8,128)(2,1)} %get-tuple-element.108.v_ref, ...), custom_call_target="tpu_custom_call" | custom-call | flops 3536250112 | tf_op jit(solution)/shard_map/attend_back/pallas_call | solution.py:315
  386.5 13.6 %attend_back.7 = (bf16[64,2048]{1,0:T(8,128)(2,1)}, bf16[64,2048]{1,0:T(8,128)(2,1)}, bf16[64,2048]{1,0:T(8,128)(2,1)}) custom-call(bf16[256,2048]{1,0:T(8,128)(2,1)} %get-tuple-element.106.q_ref, bf16[256,2048]{1,0:T(8,128)(2,1)} %get-tuple-element.107.k_ref, bf16[256,2048]{1,0:T(8,128)(2,1)} %get-tuple-element.108.v_ref, ...), custom_call_target="tpu_custom_call" | custom-call | flops 3536250112 | tf_op jit(solution)/shard_map/attend_back/pallas_call | solution.py:315
  400.2 6.9 %qkv_back.1 = (bf16[512,1024]{1,0:T(8,128)(2,1)}, bf16[512,1024]{1,0:T(8,128)(2,1)}, bf16[512,1024]{1,0:T(8,128)(2,1)}, bf16[512,1024]{1,0:T(8,128)(2,1)}) custom-call(bf16[4,4,256,256]{3,2,1,0:T(8,128)(2,1)} %pack_heads.1.w_ref, bf16[64,2048]{1,0:T(8,128)(2,1)} %get-tuple-element.150.refs_0_, bf16[64,2048]{1,0:T(8,128)(2,1)} %get-tuple-element.163.refs_1_, ...), custom_call_target="tpu_custom_call" | custom-call | flops 2012499968 | tf_op jit(solution)/shard_map/qkv_back/pallas_call | solution.py:430
  408.4 2.5 collective-permute-done.37
  410.9 1.7 add_convert_fusion.1
  412.5 8.2 %qkv_weights.1 = (bf16[4,256,256]{2,1,0:T(8,128)(2,1)}, bf16[4,256,256]{2,1,0:T(8,128)(2,1)}, bf16[4,256,256]{2,1,0:T(8,128)(2,1)}, bf16[4,256,256]{2,1,0:T(8,128)(2,1)}) custom-call(s32[5]{0:T(128)} %stack.48.index_ref, bf16[4,256,256]{2,1,0:T(8,128)(2,1)} %get-tuple-element.173.wo_ref, bf16[64,2048]{1,0:T(8,128)(2,1)} %get-tuple-element.150.refs_0_, ...), custom_call_target="tpu_custom_call" | custom-call | flops 2300000000 | tf_op jit(solution)/shard_map/qkv_weights/pallas_call | solution.py:460
  421.2 2.2 collective-permute-start.39
  423.4 1.5 collective-permute-start.41
  425.4 1.5 collective-permute-start.43
  426.9 20.0 %collective-permute-done.39.refs_2_ = bf16[512,1024]{1,0:T(8,128)(2,1)S(1)} collective-permute-done((bf16[512,1024]{1,0:T(8,128)(2,1)S(1)}, bf16[512,1024]{1,0:T(8,128)(2,1)S(1)}, u32[]{:S(2)}, u32[]{:S(2)}) %collective-permute-start.39) | collective-permute-done | bytes 1048608 | tf_op jit(solution)/shard_map/ppermute | solution.py:706
  447.8 4.5 tokens_grad.1
  452.3 4.8 collective-permute-done.43
  458.7 15.5 %collective-permute-done.44 = bf16[4,256,256]{2,1,0:T(8,128)(2,1)S(1)} collective-permute-done((bf16[4,256,256]{2,1,0:T(8,128)(2,1)S(1)}, bf16[4,256,256]{2,1,0:T(8,128)(2,1)S(1)}, u32[]{:S(2)}, u32[]{:S(2)}) %collective-permute-start.44) | collective-permute-done | bytes 524320 | tf_op jit(solution)/shard_map/ppermute | solution.py:916
  474.4 1.7 collective-permute-start.40
  476.5 2.2 collective-permute-start.48
  480.1 2.3 all-gather.15.cloned.1.call-done
  482.4 11.0 %feed_forward_gradients.1 = (f32[1024,2,1024]{2,1,0:T(2,128)}, f32[1024,1024]{1,0:T(8,128)}, f32[1,1024]{1,0:T(1,128)}) custom-call(bf16[8,3,1024,128]{3,2,1,0:T(8,128)(2,1)} %bitcast.52, bf16[1024,2,1024]{2,1,0:T(2,128)(2,1)} %old_ref.1), custom_call_target="tpu_custom_call" | custom-call | flops 2587500032 | tf_op jit(solution)/shard_map/feed_forward_gradients/pallas_call | solution.py:655
  493.5 10.5 %collective-permute-done.47.refs_2_ = bf16[4,256,256]{2,1,0:T(8,128)(2,1)} collective-permute-done((bf16[4,256,256]{2,1,0:T(8,128)(2,1)S(1)}, bf16[4,256,256]{2,1,0:T(8,128)(2,1)}, u32[]{:S(2)}, u32[]{:S(2)}) %collective-permute-start.47) | collective-permute-done | bytes 524320 | tf_op jit(solution)/shard_map/ppermute | solution.py:687
  504.0 4.4 unpack_heads.1
  509.2 3.6 collective-permute-done.49
  513.5 3.2 collective-permute-start.50
  516.7 1.6 collective-permute-done.50
  520.6 2.3 copy.30
  (193 shorter events, 45.3 us)
Async XLA Ops:
  7.2 139.4 %all-gather.13.cloned.1.call-start = ((), (), s32[]{:S(2)}) async-start(), calls=%async_computation.4 | async-start | bytes 1310720 | tf_op jit(solution)/shard_map/all_gather | solution.py:825
  8.8 16.1 %collective-permute-start.5 = (bf16[2048]{0:T(1024)(128)(2,1)S(1)}, bf16[2048]{0:T(1024)(128)(2,1)}, u32[]{:S(2)}, u32[]{:S(2)}) collective-permute-start(bf16[2048]{0:T(1024)(128)(2,1)S(1)} %fusion.1), channel_id=1, source_target_pairs={{0,4},{4,0},{8,12},{12,8},{16,20},{20,16},{24,28},{28,24},{1,5},{5... | collective-permute-start | bytes 12296 | tf_op jit(solution)/shard_map/ppermute | solution.py:687
  11.5 17.7 %collective-permute-start.8 = (bf16[256,1024]{1,0:T(8,128)(2,1)}, bf16[256,1024]{1,0:T(8,128)(2,1)S(1)}, u32[]{:S(2)}, u32[]{:S(2)}) collective-permute-start(bf16[256,1024]{1,0:T(8,128)(2,1)} %get-tuple-element.196), channel_id=1, source_target_pairs={{0,0},{1,1},{2,4},{3,5},{4,2},{5,3},{6,6},{7,7},{8,8},{9,9},{10,12... | collective-permute-start | bytes 1572872 | tf_op jit(solution)/shard_map/ppermute | solution.py:716
  13.2 13.0 %collective-permute-start = (bf16[256,1024]{1,0:T(8,128)(2,1)}, bf16[256,1024]{1,0:T(8,128)(2,1)S(1)}, u32[]{:S(2)}, u32[]{:S(2)}) collective-permute-start(bf16[256,1024]{1,0:T(8,128)(2,1)} %get-tuple-element.197), channel_id=1, source_target_pairs={{0,0},{1,1},{2,4},{3,5},{4,2},{5,3},{6,6},{7,7},{8,8},{9,9},{10,12... | collective-permute-start | bytes 1572872 | tf_op jit(solution)/shard_map/ppermute | solution.py:716
  26.2 8.7 %collective-permute-start.1 = (bf16[4,256,256]{2,1,0:T(8,128)(2,1)S(1)}, bf16[4,256,256]{2,1,0:T(8,128)(2,1)S(1)}, u32[]{:S(2)}, u32[]{:S(2)}) collective-permute-start(bf16[4,256,256]{2,1,0:T(8,128)(2,1)S(1)} %pad_maximum_fusion), channel_id=1, source_target_pairs={{4,6},{5,7},{6,4},{7,5},{12,14},{13,15},{14,12},{15,13},{20,22},{2... | collective-permute-start | bytes 1572872 | tf_op jit(solution)/shard_map/ppermute | solution.py:783
  32.2 115.7 %all-gather.11.cloned.1.call-start = ((), (), s32[]{:S(2)}) async-start(), calls=%async_computation.3 | async-start | bytes 1310720 | tf_op jit(solution)/shard_map/all_gather | solution.py:825
  32.3 14.9 %collective-permute-start.7 = (bf16[256,1024]{1,0:T(8,128)(2,1)}, bf16[256,1024]{1,0:T(8,128)(2,1)}, u32[]{:S(2)}, u32[]{:S(2)}) collective-permute-start(bf16[256,1024]{1,0:T(8,128)(2,1)} %norm_tokens.2.refs_0_.refs_12_), channel_id=1, source_target_pairs={{1,0},{0,1},{3,2},{2,3},{5,4},{4,5},{7,6},{6,7},{9,8},{8,9},{11,10... | collective-permute-start | bytes 1572872 | tf_op jit(solution)/shard_map/ppermute | solution.py:706
  34.9 40.4 %copy-start.22 = (bf16[4,256,256]{2,1,0:T(8,128)(2,1)}, bf16[4,256,256]{2,1,0:T(8,128)(2,1)S(1)}, u32[]{:S(2)}) copy-start(bf16[4,256,256]{2,1,0:T(8,128)(2,1)S(1)} %collective-permute-done.1.refs_0_) | copy-start | bytes 1572868
  34.9 39.9 %collective-permute-start.4 = (bf16[4,256,256]{2,1,0:T(8,128)(2,1)S(1)}, bf16[4,256,256]{2,1,0:T(8,128)(2,1)S(1)}, u32[]{:S(2)}, u32[]{:S(2)}) collective-permute-start(bf16[4,256,256]{2,1,0:T(8,128)(2,1)S(1)} %collective-permute-done.1.refs_0_), channel_id=1, source_target_pairs={{4,28},{12,20},{20,12},{28,4},{5,29},{13,21},{21,13},{29,5},{6,30}... | collective-permute-start | bytes 1572872 | tf_op jit(solution)/shard_map/ppermute | solution.py:785
  35.6 39.3 %collective-permute-start.3 = (bf16[4,256,256]{2,1,0:T(8,128)(2,1)S(1)}, bf16[4,256,256]{2,1,0:T(8,128)(2,1)S(1)}, u32[]{:S(2)}, u32[]{:S(2)}) collective-permute-start(bf16[4,256,256]{2,1,0:T(8,128)(2,1)S(1)} %collective-permute-done.1.refs_0_), channel_id=1, source_target_pairs={{4,20},{12,28},{20,4},{28,12},{5,21},{13,29},{21,5},{29,13},{6,22}... | collective-permute-start | bytes 1572872 | tf_op jit(solution)/shard_map/ppermute | solution.py:785
  36.3 39.0 %collective-permute-start.2 = (bf16[4,256,256]{2,1,0:T(8,128)(2,1)S(1)}, bf16[4,256,256]{2,1,0:T(8,128)(2,1)S(1)}, u32[]{:S(2)}, u32[]{:S(2)}) collective-permute-start(bf16[4,256,256]{2,1,0:T(8,128)(2,1)S(1)} %collective-permute-done.1.refs_0_), channel_id=1, source_target_pairs={{4,12},{12,4},{20,28},{28,20},{5,13},{13,5},{21,29},{29,21},{6,14}... | collective-permute-start | bytes 1572872 | tf_op jit(solution)/shard_map/ppermute | solution.py:785
  37.0 42.8 %collective-permute-start.11 = (bf16[256,1024]{1,0:T(8,128)(2,1)}, bf16[256,1024]{1,0:T(8,128)(2,1)}, u32[]{:S(2)}, u32[]{:S(2)}) collective-permute-start(bf16[256,1024]{1,0:T(8,128)(2,1)} %norm_tokens.3.refs_4_.refs_16_), channel_id=1, source_target_pairs={{1,0},{0,1},{3,2},{2,3},{5,4},{4,5},{7,6},{6,7},{9,8},{8,9},{11,10... | collective-permute-start | bytes 1572872 | tf_op jit(solution)/shard_map/ppermute | solution.py:706
  47.2 39.8 %collective-permute-start.10 = (bf16[256,1024]{1,0:T(8,128)(2,1)}, bf16[256,1024]{1,0:T(8,128)(2,1)}, u32[]{:S(2)}, u32[]{:S(2)}) collective-permute-start(bf16[256,1024]{1,0:T(8,128)(2,1)} %norm_tokens.3.refs_4_.refs_16_), channel_id=1, source_target_pairs={{0,4},{4,0},{8,12},{12,8},{16,20},{20,16},{24,28},{28,24},{1,5},{5... | collective-permute-start | bytes 1572872 | tf_op jit(solution)/shard_map/ppermute | solution.py:687
  74.8 12.2 %collective-permute-start.6 = (bf16[256,1024]{1,0:T(8,128)(2,1)}, bf16[256,1024]{1,0:T(8,128)(2,1)}, u32[]{:S(2)}, u32[]{:S(2)}) collective-permute-start(bf16[256,1024]{1,0:T(8,128)(2,1)} %norm_tokens.2.refs_0_.refs_12_), channel_id=1, source_target_pairs={{0,4},{4,0},{8,12},{12,8},{16,20},{20,16},{24,28},{28,24},{1,5},{5... | collective-permute-start | bytes 1572872 | tf_op jit(solution)/shard_map/ppermute | solution.py:687
  74.9 12.2 %collective-permute-start.9 = (bf16[256,1024]{1,0:T(8,128)(2,1)}, bf16[256,1024]{1,0:T(8,128)(2,1)}, u32[]{:S(2)}, u32[]{:S(2)}) collective-permute-start(bf16[256,1024]{1,0:T(8,128)(2,1)} %collective-permute-done.7.refs_2_.refs_14_), channel_id=1, source_target_pairs={{0,4},{4,0},{8,12},{12,8},{16,20},{20,16},{24,28},{28,24},{1,5},{5... | collective-permute-start | bytes 1572872 | tf_op jit(solution)/shard_map/ppermute | solution.py:687
  79.8 7.9 %collective-permute-start.12 = (bf16[256,1024]{1,0:T(8,128)(2,1)}, bf16[256,1024]{1,0:T(8,128)(2,1)S(1)}, u32[]{:S(2)}, u32[]{:S(2)}) collective-permute-start(bf16[256,1024]{1,0:T(8,128)(2,1)} %collective-permute-done.11.refs_6_.refs_18_), channel_id=1, source_target_pairs={{0,4},{4,0},{8,12},{12,8},{16,20},{20,16},{24,28},{28,24},{1,5},{5... | collective-permute-start | bytes 1572872 | tf_op jit(solution)/shard_map/ppermute | solution.py:687
  86.0 37.0 %collective-permute-start.13 = (bf16[512,1024]{1,0:T(8,128)(2,1)S(1)}, bf16[512,1024]{1,0:T(8,128)(2,1)S(1)}, u32[]{:S(2)}, u32[]{:S(2)}) collective-permute-start(bf16[512,1024]{1,0:T(8,128)(2,1)S(1)} %bitcast.69), channel_id=1, source_target_pairs={{0,0},{1,1},{2,4},{3,5},{4,2},{5,3},{6,6},{7,7},{8,8},{9,9},{10,12... | collective-permute-start | bytes 3145736 | tf_op jit(solution)/shard_map/ppermute | solution.py:716
  86.8 106.5 %all-gather.9.cloned.1.call-start = ((), (), s32[]{:S(2)}) async-start(), calls=%async_computation.2 | async-start | bytes 1310720 | tf_op jit(solution)/shard_map/all_gather | solution.py:825
  123.1 70.2 %copy-start.3 = (bf16[512,1024]{1,0:T(8,128)(2,1)}, bf16[512,1024]{1,0:T(8,128)(2,1)S(1)}, u32[]{:S(2)}) copy-start(bf16[512,1024]{1,0:T(8,128)(2,1)S(1)} %collective-permute-done.13.refs_2_.refs_4_.base_ref) | copy-start | bytes 3145732
  127.3 16.7 %collective-permute-start.15 = (bf16[512,1024]{1,0:T(8,128)(2,1)}, bf16[512,1024]{1,0:T(8,128)(2,1)S(1)}, u32[]{:S(2)}, u32[]{:S(2)}) collective-permute-start(bf16[512,1024]{1,0:T(8,128)(2,1)} %get-tuple-element.116), channel_id=1, source_target_pairs={{0,4},{4,0},{8,12},{12,8},{16,20},{20,16},{24,28},{28,24},{1,5},{5... | collective-permute-start | bytes 3145736 | tf_op jit(solution)/shard_map/ppermute | solution.py:687
  140.0 12.1 %collective-permute-start.14 = (bf16[512,1024]{1,0:T(8,128)(2,1)}, bf16[512,1024]{1,0:T(8,128)(2,1)}, u32[]{:S(2)}, u32[]{:S(2)}) collective-permute-start(bf16[512,1024]{1,0:T(8,128)(2,1)} %get-tuple-element.114), channel_id=1, source_target_pairs={{0,4},{4,0},{8,12},{12,8},{16,20},{20,16},{24,28},{28,24},{1,5},{5... | collective-permute-start | bytes 3145736 | tf_op jit(solution)/shard_map/ppermute | solution.py:687
  145.6 42.5 %collective-permute-start.16 = (bf16[512,1024]{1,0:T(8,128)(2,1)S(1)}, bf16[512,1024]{1,0:T(8,128)(2,1)}, u32[]{:S(2)}, u32[]{:S(2)}) collective-permute-start(bf16[512,1024]{1,0:T(8,128)(2,1)S(1)} %add_convert_fusion.4), channel_id=1, source_target_pairs={{1,0},{0,1},{3,2},{2,3},{5,4},{4,5},{7,6},{6,7},{9,8},{8,9},{11,10... | collective-permute-start | bytes 3145736 | tf_op jit(solution)/shard_map/ppermute | solution.py:706
  146.5 274.2 %reduce-scatter.2.cloned.1.call-start = ((), (), s32[]{:S(2)}) async-start(), calls=%async_computation.1 | async-start | bytes 3932160 | tf_op jit(solution)/shard_map/reduce_scatter | solution.py:888
  146.6 46.7 %collective-permute-start.21 = (bf16[4,128,1024]{2,1,0:T(8,128)(2,1)}, bf16[4,128,1024]{2,1,0:T(8,128)(2,1)}, u32[]{:S(2)}, u32[]{:S(2)}) collective-permute-start(bf16[4,128,1024]{2,1,0:T(8,128)(2,1)} %bitcast.70), channel_id=1, source_target_pairs={{0,8},{4,12},{8,0},{12,4},{16,24},{20,28},{24,16},{28,20},{1,9},{5... | collective-permute-start | bytes 3145736 | tf_op jit(solution)/shard_map/ppermute | solution.py:687
  147.9 47.0 %collective-permute-start.20 = (bf16[4,128,1024]{2,1,0:T(8,128)(2,1)}, bf16[4,128,1024]{2,1,0:T(8,128)(2,1)}, u32[]{:S(2)}, u32[]{:S(2)}) collective-permute-start(bf16[4,128,1024]{2,1,0:T(8,128)(2,1)} %bitcast.73), channel_id=1, source_target_pairs={{0,8},{4,12},{8,0},{12,4},{16,24},{20,28},{24,16},{28,20},{1,9},{5... | collective-permute-start | bytes 3145736 | tf_op jit(solution)/shard_map/ppermute | solution.py:687
  150.8 37.3 %copy-start.9 = (bf16[512,1024]{1,0:T(8,128)(2,1)}, bf16[512,1024]{1,0:T(8,128)(2,1)S(1)}, u32[]{:S(2)}) copy-start(bf16[512,1024]{1,0:T(8,128)(2,1)S(1)} %constant_dynamic-update-slice_fusion.x_ref) | copy-start | bytes 3145732
  150.8 44.2 %collective-permute-start.25 = (bf16[512,1024]{1,0:T(8,128)(2,1)S(1)}, bf16[512,1024]{1,0:T(8,128)(2,1)S(1)}, u32[]{:S(2)}, u32[]{:S(2)}) collective-permute-start(bf16[512,1024]{1,0:T(8,128)(2,1)S(1)} %collective-permute-done.13.refs_2_.refs_4_.base_ref), channel_id=1, source_target_pairs={{0,16},{4,20},{8,24},{12,28},{16,0},{20,4},{24,8},{28,12},{1,17},{... | collective-permute-start | bytes 3145736 | tf_op jit(solution)/shard_map/ppermute | solution.py:687
  192.0 24.8 %collective-permute-start.23 = (bf16[512,1024]{1,0:T(8,128)(2,1)}, bf16[512,1024]{1,0:T(8,128)(2,1)S(1)}, u32[]{:S(2)}, u32[]{:S(2)}) collective-permute-start(bf16[512,1024]{1,0:T(8,128)(2,1)} %get-tuple-element.142.refs_0_), channel_id=1, source_target_pairs={{0,16},{4,20},{8,24},{12,28},{16,0},{20,4},{24,8},{28,12},{1,17},{... | collective-permute-start | bytes 3145736 | tf_op jit(solution)/shard_map/ppermute | solution.py:687
  193.3 25.8 %collective-permute-start.18 = (bf16[512,1024]{1,0:T(8,128)(2,1)S(1)}, bf16[512,1024]{1,0:T(8,128)(2,1)}, u32[]{:S(2)}, u32[]{:S(2)}) collective-permute-start(bf16[512,1024]{1,0:T(8,128)(2,1)S(1)} %collective-permute-done.13.refs_2_.refs_4_.base_ref), channel_id=1, source_target_pairs={{0,4},{4,0},{8,12},{12,8},{16,20},{20,16},{24,28},{28,24},{1,5},{5... | collective-permute-start | bytes 3145736 | tf_op jit(solution)/shard_map/ppermute | solution.py:687
  193.3 25.8 %collective-permute-start.19 = (bf16[4,128,1024]{2,1,0:T(8,128)(2,1)}, bf16[4,128,1024]{2,1,0:T(8,128)(2,1)S(1)}, u32[]{:S(2)}, u32[]{:S(2)}) collective-permute-start(bf16[4,128,1024]{2,1,0:T(8,128)(2,1)} %bitcast.76), channel_id=1, source_target_pairs={{0,8},{4,12},{8,0},{12,4},{16,24},{20,28},{24,16},{28,20},{1,9},{5... | collective-permute-start | bytes 3145736 | tf_op jit(solution)/shard_map/ppermute | solution.py:687
  194.8 24.2 %collective-permute-start.17 = (bf16[512,1024]{1,0:T(8,128)(2,1)}, bf16[512,1024]{1,0:T(8,128)(2,1)S(1)}, u32[]{:S(2)}, u32[]{:S(2)}) collective-permute-start(bf16[512,1024]{1,0:T(8,128)(2,1)} %get-tuple-element.142.refs_0_), channel_id=1, source_target_pairs={{0,4},{4,0},{8,12},{12,8},{16,20},{20,16},{24,28},{28,24},{1,5},{5... | collective-permute-start | bytes 3145736 | tf_op jit(solution)/shard_map/ppermute | solution.py:687
  195.0 47.2 %copy-start.4 = (bf16[512,1024]{1,0:T(8,128)(2,1)}, bf16[512,1024]{1,0:T(8,128)(2,1)S(1)}, u32[]{:S(2)}) copy-start(bf16[512,1024]{1,0:T(8,128)(2,1)S(1)} %collective-permute-done.25.refs_2_.refs_6_) | copy-start | bytes 3145732
  195.0 47.2 %collective-permute-start.26 = (bf16[512,1024]{1,0:T(8,128)(2,1)S(1)}, bf16[512,1024]{1,0:T(8,128)(2,1)S(1)}, u32[]{:S(2)}, u32[]{:S(2)}) collective-permute-start(bf16[512,1024]{1,0:T(8,128)(2,1)S(1)} %collective-permute-done.25.refs_2_.refs_6_), channel_id=1, source_target_pairs={{0,4},{4,0},{8,12},{12,8},{16,20},{20,16},{24,28},{28,24},{1,5},{5... | collective-permute-start | bytes 3145736 | tf_op jit(solution)/shard_map/ppermute | solution.py:687
  216.8 25.4 %copy-start.5 = (bf16[512,1024]{1,0:T(8,128)(2,1)}, bf16[512,1024]{1,0:T(8,128)(2,1)S(1)}, u32[]{:S(2)}) copy-start(bf16[512,1024]{1,0:T(8,128)(2,1)S(1)} %collective-permute-done.23.refs_0_.refs_2_) | copy-start | bytes 3145732
  216.8 25.4 %collective-permute-start.24 = (bf16[512,1024]{1,0:T(8,128)(2,1)S(1)}, bf16[512,1024]{1,0:T(8,128)(2,1)S(1)}, u32[]{:S(2)}, u32[]{:S(2)}) collective-permute-start(bf16[512,1024]{1,0:T(8,128)(2,1)S(1)} %collective-permute-done.23.refs_0_.refs_2_), channel_id=1, source_target_pairs={{0,4},{4,0},{8,12},{12,8},{16,20},{20,16},{24,28},{28,24},{1,5},{5... | collective-permute-start | bytes 3145736 | tf_op jit(solution)/shard_map/ppermute | solution.py:687
  265.3 2.9 collective-permute-start.27
  265.4 19.3 %collective-permute-start.29 = (bf16[512,1024]{1,0:T(8,128)(2,1)}, bf16[512,1024]{1,0:T(8,128)(2,1)S(1)}, u32[]{:S(2)}, u32[]{:S(2)}) collective-permute-start(bf16[512,1024]{1,0:T(8,128)(2,1)} %get-tuple-element.137), channel_id=1, source_target_pairs={{0,4},{4,0},{8,12},{12,8},{16,20},{20,16},{24,28},{28,24},{1,5},{5... | collective-permute-start | bytes 3145736 | tf_op jit(solution)/shard_map/ppermute | solution.py:687
  269.9 25.3 %collective-permute-start.28 = (bf16[512,1024]{1,0:T(8,128)(2,1)S(1)}, bf16[512,1024]{1,0:T(8,128)(2,1)S(1)}, u32[]{:S(2)}, u32[]{:S(2)}) collective-permute-start(bf16[512,1024]{1,0:T(8,128)(2,1)S(1)} %add_convert_fusion.3), channel_id=1, source_target_pairs={{0,16},{4,20},{8,24},{12,28},{16,0},{20,4},{24,8},{28,12},{1,17},{... | collective-permute-start | bytes 3145736 | tf_op jit(solution)/shard_map/ppermute | solution.py:687
  282.8 12.4 %collective-permute-start.30 = (bf16[512,1024]{1,0:T(8,128)(2,1)}, bf16[512,1024]{1,0:T(8,128)(2,1)S(1)}, u32[]{:S(2)}, u32[]{:S(2)}) collective-permute-start(bf16[512,1024]{1,0:T(8,128)(2,1)} %get-tuple-element.139), channel_id=1, source_target_pairs={{0,4},{4,0},{8,12},{12,8},{16,20},{20,16},{24,28},{28,24},{1,5},{5... | collective-permute-start | bytes 3145736 | tf_op jit(solution)/shard_map/ppermute | solution.py:687
  282.9 12.3 %collective-permute-start.22 = (bf16[512,1024]{1,0:T(8,128)(2,1)}, bf16[512,1024]{1,0:T(8,128)(2,1)S(1)}, u32[]{:S(2)}, u32[]{:S(2)}) collective-permute-start(bf16[512,1024]{1,0:T(8,128)(2,1)} %get-tuple-element.124), channel_id=1, source_target_pairs={{0,4},{4,0},{8,12},{12,8},{16,20},{20,16},{24,28},{28,24},{1,5},{5... | collective-permute-start | bytes 3145736 | tf_op jit(solution)/shard_map/ppermute | solution.py:687
  283.4 71.5 %collective-permute-start.35 = (bf16[4,3,1024,128]{3,2,1,0:T(8,128)(2,1)}, bf16[4,3,1024,128]{3,2,1,0:T(8,128)(2,1)}, u32[]{:S(2)}, u32[]{:S(2)}) collective-permute-start(bf16[4,3,1024,128]{3,2,1,0:T(8,128)(2,1)} %feed_forward_weights.2), channel_id=1, source_target_pairs={{0,8},{4,12},{8,0},{12,4},{16,24},{20,28},{24,16},{28,20},{1,9},{5... | collective-permute-start | bytes 9437192 | tf_op jit(solution)/shard_map/ppermute | solution.py:687
  301.6 2.9 collective-permute-start.31
  301.7 25.6 %collective-permute-start.33 = (bf16[512,1024]{1,0:T(8,128)(2,1)S(1)}, bf16[512,1024]{1,0:T(8,128)(2,1)S(1)}, u32[]{:S(2)}, u32[]{:S(2)}) collective-permute-start(bf16[512,1024]{1,0:T(8,128)(2,1)S(1)} %add_convert_fusion.2), channel_id=1, source_target_pairs={{0,16},{4,20},{8,24},{12,28},{16,0},{20,4},{24,8},{28,12},{1,17},{... | collective-permute-start | bytes 3145736 | tf_op jit(solution)/shard_map/ppermute | solution.py:687
  302.4 29.2 %collective-permute-start.32 = (bf16[512,1024]{1,0:T(8,128)(2,1)}, bf16[512,1024]{1,0:T(8,128)(2,1)S(1)}, u32[]{:S(2)}, u32[]{:S(2)}) collective-permute-start(bf16[512,1024]{1,0:T(8,128)(2,1)} %get-tuple-element.141.refs_1_), channel_id=1, source_target_pairs={{1,0},{0,1},{3,2},{2,3},{5,4},{4,5},{7,6},{6,7},{9,8},{8,9},{11,10... | collective-permute-start | bytes 3145736 | tf_op jit(solution)/shard_map/ppermute | solution.py:706
  331.7 2.7 collective-permute-start.34
  331.7 27.6 %collective-permute-start.36 = (bf16[512,1024]{1,0:T(8,128)(2,1)}, bf16[512,1024]{1,0:T(8,128)(2,1)S(1)}, u32[]{:S(2)}, u32[]{:S(2)}) collective-permute-start(bf16[512,1024]{1,0:T(8,128)(2,1)} %output_sum.1), channel_id=1, source_target_pairs={{0,0},{1,1},{2,4},{3,5},{4,2},{5,3},{6,6},{7,7},{8,8},{9,9},{10,12... | collective-permute-start | bytes 3145736 | tf_op jit(solution)/shard_map/ppermute | solution.py:716
  359.4 123.0 %all-gather.15.cloned.1.call-start = ((), (), s32[]{:S(2)}) async-start(), calls=%async_computation.5 | async-start | bytes 7077888 | tf_op jit(solution)/shard_map/all_gather | solution.py:903
  407.1 3.7 collective-permute-start.37
  420.7 6.1 %collective-permute-start.38 = (bf16[512,1024]{1,0:T(8,128)(2,1)}, bf16[512,1024]{1,0:T(8,128)(2,1)S(1)}, u32[]{:S(2)}, u32[]{:S(2)}) collective-permute-start(bf16[512,1024]{1,0:T(8,128)(2,1)} %get-tuple-element.178), channel_id=1, source_target_pairs={{0,4},{4,0},{8,12},{12,8},{16,20},{20,16},{24,28},{28,24},{1,5},{5... | collective-permute-start | bytes 3145736 | tf_op jit(solution)/shard_map/ppermute | solution.py:687
  421.2 25.6 %collective-permute-start.39 = (bf16[512,1024]{1,0:T(8,128)(2,1)S(1)}, bf16[512,1024]{1,0:T(8,128)(2,1)S(1)}, u32[]{:S(2)}, u32[]{:S(2)}) collective-permute-start(bf16[512,1024]{1,0:T(8,128)(2,1)S(1)} %add_convert_fusion.1), channel_id=1, source_target_pairs={{1,0},{0,1},{3,2},{2,3},{5,4},{4,5},{7,6},{6,7},{9,8},{8,9},{11,10... | collective-permute-start | bytes 3145736 | tf_op jit(solution)/shard_map/ppermute | solution.py:706
  423.4 28.9 %collective-permute-start.41 = (bf16[4,256,256]{2,1,0:T(8,128)(2,1)}, bf16[4,256,256]{2,1,0:T(8,128)(2,1)S(1)}, u32[]{:S(2)}, u32[]{:S(2)}) collective-permute-start(bf16[4,256,256]{2,1,0:T(8,128)(2,1)} %get-tuple-element.180), channel_id=1, source_target_pairs={{0,8},{4,12},{8,0},{12,4},{16,24},{20,28},{24,16},{28,20},{1,9},{5... | collective-permute-start | bytes 1572872 | tf_op jit(solution)/shard_map/ppermute | solution.py:687
  424.9 27.4 %collective-permute-start.42 = (bf16[4,256,256]{2,1,0:T(8,128)(2,1)}, bf16[4,256,256]{2,1,0:T(8,128)(2,1)S(1)}, u32[]{:S(2)}, u32[]{:S(2)}) collective-permute-start(bf16[4,256,256]{2,1,0:T(8,128)(2,1)} %get-tuple-element.181), channel_id=1, source_target_pairs={{0,16},{4,20},{8,24},{12,28},{16,0},{20,4},{24,8},{28,12},{1,17},{... | collective-permute-start | bytes 1572872 | tf_op jit(solution)/shard_map/ppermute | solution.py:687
  425.4 31.8 %collective-permute-start.43 = (bf16[4,256,256]{2,1,0:T(8,128)(2,1)}, bf16[4,256,256]{2,1,0:T(8,128)(2,1)S(1)}, u32[]{:S(2)}, u32[]{:S(2)}) collective-permute-start(bf16[4,256,256]{2,1,0:T(8,128)(2,1)} %get-tuple-element.182), channel_id=1, source_target_pairs={{0,24},{4,28},{8,16},{12,20},{16,8},{20,12},{24,0},{28,4},{1,25},{... | collective-permute-start | bytes 1572872 | tf_op jit(solution)/shard_map/ppermute | solution.py:687
  452.3 22.1 %copy-start.10 = (bf16[512,1024]{1,0:T(8,128)(2,1)S(1)}, bf16[512,1024]{1,0:T(8,128)(2,1)}, u32[]{:S(2)}) copy-start(bf16[512,1024]{1,0:T(8,128)(2,1)} %tokens_grad.1) | copy-start | bytes 3145732
  457.4 16.8 %collective-permute-start.44 = (bf16[4,256,256]{2,1,0:T(8,128)(2,1)S(1)}, bf16[4,256,256]{2,1,0:T(8,128)(2,1)S(1)}, u32[]{:S(2)}, u32[]{:S(2)}) collective-permute-start(bf16[4,256,256]{2,1,0:T(8,128)(2,1)S(1)} %add_convert_fusion.6), channel_id=1, source_target_pairs={{4,2},{5,3},{6,0},{7,1},{12,10},{13,11},{14,8},{15,9},{20,18},{21,... | collective-permute-start | bytes 1572872 | tf_op jit(solution)/shard_map/ppermute | solution.py:916
  474.3 2.1 collective-permute-start.45
  474.4 42.3 %collective-permute-start.40 = (bf16[512,1024]{1,0:T(8,128)(2,1)S(1)}, bf16[512,1024]{1,0:T(8,128)(2,1)}, u32[]{:S(2)}, u32[]{:S(2)}) collective-permute-start(bf16[512,1024]{1,0:T(8,128)(2,1)S(1)} %copy-done.10), channel_id=1, source_target_pairs={{0,0},{1,1},{2,4},{3,5},{4,2},{5,3},{6,6},{7,7},{8,8},{9,9},{10,12... | collective-permute-start | bytes 3145736 | tf_op jit(solution)/shard_map/ppermute | solution.py:716
  476.5 16.9 %collective-permute-start.48 = (bf16[4,256,256]{2,1,0:T(8,128)(2,1)S(1)}, bf16[4,256,256]{2,1,0:T(8,128)(2,1)}, u32[]{:S(2)}, u32[]{:S(2)}) collective-permute-start(bf16[4,256,256]{2,1,0:T(8,128)(2,1)S(1)} %broadcast_select_fusion.refs_0_), channel_id=1, source_target_pairs={{0,24},{4,28},{8,16},{12,20},{16,8},{20,12},{24,0},{28,4},{1,25},{... | collective-permute-start | bytes 1572872 | tf_op jit(solution)/shard_map/ppermute | solution.py:687
  478.7 25.3 %collective-permute-start.47 = (bf16[4,256,256]{2,1,0:T(8,128)(2,1)S(1)}, bf16[4,256,256]{2,1,0:T(8,128)(2,1)}, u32[]{:S(2)}, u32[]{:S(2)}) collective-permute-start(bf16[4,256,256]{2,1,0:T(8,128)(2,1)S(1)} %broadcast_select_fusion.refs_0_), channel_id=1, source_target_pairs={{0,16},{4,20},{8,24},{12,28},{16,0},{20,4},{24,8},{28,12},{1,17},{... | collective-permute-start | bytes 1572872 | tf_op jit(solution)/shard_map/ppermute | solution.py:687
  479.3 24.7 %collective-permute-start.46 = (bf16[4,256,256]{2,1,0:T(8,128)(2,1)S(1)}, bf16[4,256,256]{2,1,0:T(8,128)(2,1)}, u32[]{:S(2)}, u32[]{:S(2)}) collective-permute-start(bf16[4,256,256]{2,1,0:T(8,128)(2,1)S(1)} %broadcast_select_fusion.refs_0_), channel_id=1, source_target_pairs={{0,8},{4,12},{8,0},{12,4},{16,24},{20,28},{24,16},{28,20},{1,9},{5... | collective-permute-start | bytes 1572872 | tf_op jit(solution)/shard_map/ppermute | solution.py:687
  493.4 24.9 %copy-start.31 = (f32[1024]{0:T(1024)S(1)}, f32[1024]{0:T(1024)}, u32[]{:S(2)}) copy-start(f32[1024]{0:T(1024)} %param.15) | copy-start | bytes 12292
  493.4 24.9 %copy-start.32 = (f32[1024]{0:T(1024)S(1)}, f32[1024]{0:T(1024)}, u32[]{:S(2)}) copy-start(f32[1024]{0:T(1024)} %param.16) | copy-start | bytes 12292
  509.1 3.7 collective-permute-start.49
  513.5 4.8 collective-permute-start.50
  (30 other events, 159.5 us)
Sparse Core Ops, SparseCore 0:
  32.3 54.2 all-gather.12
  88.2 43.1 all-gather.10
  146.6 39.7 all-gather.8
  359.5 60.6 reduce-scatter.1
  421.9 60.4 all-gather.14
